TPU v7x, 1024 devices: a whole 4x4x32 slice. The times are simulated.
1024 devices in a mesh: rep: 128 (over x_lo, z, core), tp: 8 (over y, x_hi).
Axes of the slice: x: 4 (x_hi: 2, x_lo: 2; x = x_hi * 2 + x_lo), y: 4, z: 32, core: 2. Of those that a mesh axis runs over, the one named last changes fastest.
Arguments:
- tokens: bfloat16 [65536, 8192], P(('rep', 'tp')), may hold values from -6 to 6
- base_weight: bfloat16 [8192, 1024], P('tp'), may hold values from -0.0625 to 0.0625
- adapter_down: bfloat16 [128, 8192, 16], P('rep', 'tp'), may hold values from -0.0625 to 0.0625
- adapter_up: bfloat16 [128, 16, 1024], P('rep', None, 'tp'), may hold values from -1.5 to 1.5
- upstream: bfloat16 [65536, 1024], P('rep', 'tp'), may hold values from -3 to 3
- block_tenant_index: int32 [128], replicated, may hold values from 0 to 127
- valid_lengths: int32 [128], replicated, may hold values from 1 to 512, 49152 in all
Outputs:
- projected: bfloat16 [65536, 1024], P('rep', 'tp')
- activation_gradient: bfloat16 [65536, 8192], P('rep', 'tp')
- up_grad: float32 [128, 16, 1024], P('rep', None, 'tp')
All inputs are finite; a program needn't handle non-finite values.
Results may differ from a plain program's by a relative error of at most 0.019.
Values may be sent and summed in bfloat16 or wider, within the bound.
No kernel may reach another device: no remote copies, remote signals or barrier semaphores. Data moves between devices by JAX's collectives and lax.ppermute only.
A program may use at most 32 MiB of HBM per device.

v0:
```python
import jax
import jax.numpy as jnp
from jax import lax
from jax.sharding import PartitionSpec as P

adapter_scale = 2.0


def from_behind(value, axis, steps):
    count = lax.axis_size(axis)
    pairs = [(source, (source + steps) % count) for source in range(count)]
    return lax.ppermute(value, axis, pairs)


def pick_entry(table, wanted):
    hits = jnp.arange(table.shape[0], dtype=jnp.int32) == wanted
    return jnp.sum(jnp.where(hits, table, jnp.zeros_like(table)))


def on_device(
    tokens, base_weight, adapter_down, adapter_up, upstream, block_tenant_index, valid_lengths
):
    replicas = lax.axis_size("rep")
    position = lax.axis_index("rep")
    my_tenant = pick_entry(block_tenant_index, position)
    my_length = pick_entry(valid_lengths, position)
    columns = lax.all_to_all(tokens, "tp", split_axis=1, concat_axis=0, tiled=True)
    partial_value = jnp.dot(columns, base_weight, preferred_element_type=jnp.float32)
    base_part = lax.psum_scatter(
        partial_value.astype(jnp.bfloat16), "tp", scatter_dimension=1, tiled=True
    ).astype(jnp.float32)
    rows_total = columns.shape[0]
    base_gradient = lax.dot_general(
        lax.all_gather(upstream, "tp", axis=1, tiled=True),
        base_weight,
        (((1,), (1,)), ((), ())),
        preferred_element_type=jnp.float32,
    )
    own = (adapter_down[0], adapter_up[0])

    def keep(held, moving, carried):
        match = my_tenant == carried
        return jax.tree.map(lambda fresh, older: jnp.where(match, fresh, older), moving, held)

    start_held = keep(jax.tree.map(jnp.zeros_like, own), own, position)

    def visit_one(offset, state_tuple):
        moving, held = state_tuple
        moving = from_behind((moving[0], moving[1]), "rep", 1)
        held = keep(held, moving, (position - offset) % replicas)
        return (moving, held)

    final_state = lax.fori_loop(1, replicas, visit_one, (own, start_held))
    held_down, frozen_up_weight = final_state[1]
    low_part = jnp.dot(columns, held_down, preferred_element_type=jnp.float32)
    back_part = lax.dot_general(
        upstream, frozen_up_weight, (((1,), (1,)), ((), ())), preferred_element_type=jnp.float32
    )
    low_sum, back_sum = (
        lax.psum(low_part.astype(jnp.bfloat16), "tp").astype(jnp.float32),
        lax.psum(back_part.astype(jnp.bfloat16), "tp").astype(jnp.float32),
    )
    low_rank_state = low_sum.astype(jnp.bfloat16)
    backward_term = back_sum.astype(jnp.bfloat16)
    valid_mask = (jnp.arange(rows_total, dtype=jnp.int32) < my_length).astype(jnp.float32)[:, None]
    projected = (
        base_part
        + adapter_scale
        * valid_mask
        * jnp.dot(low_rank_state, frozen_up_weight, preferred_element_type=jnp.float32)
    ).astype(jnp.bfloat16)
    adapter_gradient = lax.dot_general(
        backward_term, held_down, (((1,), (1,)), ((), ())), preferred_element_type=jnp.float32
    )
    activation_gradient = (base_gradient + adapter_scale * valid_mask * adapter_gradient).astype(
        jnp.bfloat16
    )
    masked_tokens = jnp.where(valid_mask > 0.0, low_rank_state, jnp.zeros_like(low_rank_state))
    adapter_contribution = adapter_scale * lax.dot_general(
        masked_tokens, upstream, (((0,), (0,)), ((), ())), preferred_element_type=jnp.float32
    )
    slots = jnp.arange(replicas, dtype=jnp.int32)[:, None, None] == my_tenant
    table = jnp.where(
        slots,
        adapter_contribution[None],
        jnp.zeros((replicas,) + adapter_contribution.shape, jnp.float32),
    )
    up_grad = lax.psum_scatter(table, "rep", scatter_dimension=0, tiled=True)
    return (projected, activation_gradient, up_grad)


def solution(mesh):
    return jax.shard_map(
        on_device,
        mesh=mesh,
        in_specs=(
            P(("rep", "tp"), None),
            P("tp", None),
            P("rep", "tp", None),
            P("rep", None, "tp"),
            P("rep", "tp"),
            P(),
            P(),
        ),
        out_specs=(P("rep", "tp"), P("rep", "tp"), P("rep", None, "tp")),
        check_vma=False,
    )
```

profile of v0, /device:TPU:6, one launch (start us, length us, event | category | flops | bytes accessed | tf_op | source)
XLA Modules:
  0.0 1702.4 jit_solution(16272652097587409609)
XLA Ops:
  11.2 7.4 all-to-all-start
  21.8 11.3 all-to-all-done
  37.7 1192.6 %while.21 = (s32[]{:T(128)}, bf16[1024,16]{0,1:T(8,128)(2,1)S(1)}, bf16[16,128]{1,0:T(8,128)(2,1)S(1)}, bf16[1024,16]{0,1:T(8,128)(2,1)S(1)}, bf16[16,128]{1,0:T...) while((s32[]{:T(128)}, bf16[1024,16]{0,1:T(8,128)(2,1)S(1)}, ...), condition=%wide.region_4.5_spmd, body=%wide.region_3.4_spmd.sunk | while | flops 18447 | bytes 332097 | solution.py:53
  39.7 3.9 collective-permute-start
  44.2 11.9 collective-permute-done.1
  62.9 2.5 collective-permute-done.1
  81.5 2.5 collective-permute-done.1
  90.8 2.5 collective-permute-done.1
  100.1 2.5 collective-permute-done.1
  109.4 2.5 collective-permute-done.1
  118.7 2.5 collective-permute-done.1
  128.0 2.5 collective-permute-done.1
  137.3 2.5 collective-permute-done.1
  174.5 2.5 collective-permute-done.1
  183.8 2.5 collective-permute-done.1
  193.1 2.5 collective-permute-done.1
  202.4 2.5 collective-permute-done.1
  230.3 2.5 collective-permute-done.1
  239.6 2.5 collective-permute-done.1
  258.2 2.5 collective-permute-done.1
  267.5 2.5 collective-permute-done.1
  276.8 2.5 collective-permute-done.1
  286.1 2.5 collective-permute-done.1
  295.4 2.5 collective-permute-done.1
  304.7 2.5 collective-permute-done.1
  314.0 2.5 collective-permute-done.1
  332.6 2.5 collective-permute-done.1
  341.9 2.5 collective-permute-done.1
  351.2 2.5 collective-permute-done.1
  360.5 2.5 collective-permute-done.1
  1230.8 37.8 %all-reduce = (bf16[512,16]{0,1:T(8,128)(2,1)S(1)}, bf16[512,16]{0,1:T(8,128)(2,1)S(1)}) all-reduce(bf16[512,16]{0,1:T(8,128)(2,1)S(1)} %fusion.2, bf16[512,16]{0,1:T(8,128)(2,1)S(1)} %fusion.3), channel_id=1, replica_groups=mesh['rep'=128,'tp'=8] {'tp'}, use_global_device_ids=true, to_apply=%region_5.6 | all-reduce | flops 16384 | bytes 65536 | tf_op jit(solution)/shard_map/psum | solution.py:60
  1276.5 419.3 %reduce-scatter.5.cloned.1.call-done = f32[1,16,128]{2,1,0:T(8,128)} async-done(((f32[128,16,128]{2,1,0:T(8,128)}), f32[1,16,128]{2,1,0:T(8,128)}) %reduce-scatter.5.cloned.1.call-update) | async-done | bytes 8208 | tf_op jit(solution)/shard_map/reduce_scatter | solution.py:88
  (1025 shorter events, 1047.0 us)
Async XLA Ops:
  7.2 1263.5 %all-gather.2.cloned.1.call-start = ((), (), s32[]{:S(2)}) async-start(), calls=%async_computation.3 | async-start | bytes 1179648 | tf_op jit(solution)/shard_map/all_gather | solution.py:34
  11.2 22.0 %all-to-all-start = ((bf16[64,8,1024]{2,0,1:T(8,128)(2,1)}), bf16[64,8,1024]{2,0,1:T(8,128)(2,1)S(1)}, u32[]{:S(2)}, u32[]{:S(2)}) async-start(bf16[64,8,1024]{2,0,1:T(8,128)(2,1)} %bitcast.33), calls=%async_computation | async-start | bytes 2097152 | tf_op jit(solution)/shard_map/all_to_all | solution.py:27
  18.6 1256.0 %reduce-scatter.7.cloned.1.call-start = ((), (), s32[]{:S(2)}) async-start(), calls=%async_computation.5 | async-start | bytes 1179648
  37.7 1658.2 %reduce-scatter.5.cloned.1.call-start = ((), (), s32[]{:S(2)}) async-start(), calls=%async_computation.4 | async-start | bytes 1056768 | tf_op jit(solution)/shard_map/reduce_scatter | solution.py:88
  37.7 18.4 %collective-permute-start.1 = (bf16[16,128]{1,0:T(8,128)(2,1)S(1)}, bf16[16,128]{1,0:T(8,128)(2,1)S(1)}, u32[]{:S(2)}, u32[]{:S(2)}) collective-permute-start(bf16[16,128]{1,0:T(8,128)(2,1)S(1)} %get-tuple-element.255), channel_id=1, source_target_pairs={{0,8},{8,16},{16,24},{24,32},{32,40},{40,48},{48,56},{56,64},{64,7... | collective-permute-start | bytes 12296 | tf_op jit(solution)/shard_map/while/body/eval_jaxpr/ppermute | solution.py:12
  39.7 18.7 %collective-permute-start = (bf16[1024,16]{0,1:T(8,128)(2,1)S(1)}, bf16[1024,16]{0,1:T(8,128)(2,1)S(1)}, u32[]{:S(2)}, u32[]{:S(2)}) collective-permute-start(bf16[1024,16]{0,1:T(8,128)(2,1)S(1)} %get-tuple-element.254), channel_id=1, source_target_pairs={{0,8},{8,16},{16,24},{24,32},{32,40},{40,48},{48,56},{56,64},{64,7... | collective-permute-start | bytes 98312 | tf_op jit(solution)/shard_map/while/body/eval_jaxpr/ppermute | solution.py:12
  60.3 7.3 collective-permute-start
  69.6 7.3 collective-permute-start
  88.2 7.3 collective-permute-start
  97.5 7.3 collective-permute-start
  106.8 7.3 collective-permute-start
  116.1 7.3 collective-permute-start
  125.4 7.3 collective-permute-start
  134.7 7.3 collective-permute-start
  144.0 7.3 collective-permute-start
  153.3 7.3 collective-permute-start
  162.6 7.3 collective-permute-start
  171.9 7.3 collective-permute-start
  190.5 7.3 collective-permute-start
  199.8 7.3 collective-permute-start
  209.1 7.3 collective-permute-start
  218.4 7.3 collective-permute-start
  227.7 7.3 collective-permute-start
  237.0 7.3 collective-permute-start
  246.3 7.3 collective-permute-start
  264.9 7.3 collective-permute-start
  274.2 7.3 collective-permute-start
  283.5 7.3 collective-permute-start
  292.8 7.3 collective-permute-start
  302.1 7.3 collective-permute-start
  311.4 7.3 collective-permute-start
  320.7 7.3 collective-permute-start
  (230 other events, 2863.2 us)
Sparse Core Ops, SparseCore 0:
  12.2 87.1 all-gather.1
  105.0 106.9 reduce-scatter.6
  1270.1 425.6 reduce-scatter.4
where the time goes:
time: 1710 us; the launch traced here: 1700 us
  waiting for transfers between devices  1040 us (61%)
  starting transfers between devices  497 us (29%)
  loops' own time  85.9 us (5%)
  blocking collectives  37.8 us (2%)
    ppermute x254, waiting for transfers between devices, from_behind(): return lax.ppermute(value, axis, pairs)  613 us
    ppermute x254, starting transfers between devices, from_behind(): return lax.ppermute(value, axis, pairs)  490 us
    reduce_scatter x1, waiting for transfers between devices, on_device(): up_grad = lax.psum_scatter(table, 'rep', scatter_dimension=0, tiled=True)  419 us
    another operation x1, loops' own time, on_device(): final_state = lax.fori_loop(1, replicas, visit_one, (own, start_held))  85.9 us
    psum x1, blocking collectives, on_device(): lax.psum(low_part.astype(jnp.bfloat16), 'tp').astype(jnp.float32)  37.8 us
  transfers between devices with their start and end apart: 258, of which 256 were waited for; matrix products, arithmetic and copies ran while one was open for 1% of the time, Pallas kernels for 0%

commit v1 on v0

v1 whole, which is shorter than its diff:
```python
import functools

import jax
import jax.numpy as jnp
from jax import lax
from jax.experimental import pallas as pl
from jax.experimental.pallas import tpu as pltpu
from jax.sharding import Mesh
from jax.sharding import PartitionSpec as P

adapter_scale = 2.0
VMEM = pl.BlockSpec(memory_space=pltpu.VMEM)
SMEM = pl.BlockSpec(memory_space=pltpu.SMEM)
ANY = pl.BlockSpec(memory_space=pl.ANY)
REP = ("xlo", "far", "near", "core")


def params(mib=24):
    return pltpu.CompilerParams(vmem_limit_bytes=mib * 1024 * 1024)


def cost(flops, moved):
    return pl.CostEstimate(flops=flops, bytes_accessed=moved, transcendentals=0)


def struct(shape, dtype):
    return jax.ShapeDtypeStruct(shape, dtype)


def whole(shape):
    return pl.BlockSpec(shape, lambda i: (0,) * len(shape))


def dot(a, b, ca, cb):
    return lax.dot_general(
        a, b, (((ca,), (cb,)), ((), ())), preferred_element_type=jnp.float32
    )


def split_place(index, sizes):
    xlo_n, far_n, near_n, core_n = sizes
    core = lax.rem(index, core_n)
    index = lax.div(index, core_n)
    near = lax.rem(index, near_n)
    index = lax.div(index, near_n)
    return lax.div(index, far_n), lax.rem(index, far_n), near, core


def slab_kernel(parts, tokens_ref, upstream_ref, out_ref, held_ref, sems):
    rows, features = tokens_ref.shape[0], upstream_ref.shape[1]
    width = tokens_ref.shape[1] // parts
    slices = [
        pltpu.make_async_copy(
            tokens_ref.at[:, pl.ds(s * width, width)],
            out_ref.at[s, pl.ds(0, rows), :],
            sems.at[0, s],
        )
        for s in range(parts)
    ]
    folds = [
        pltpu.make_async_copy(
            upstream_ref.at[pl.ds(g * rows, rows), :],
            held_ref.at[:, pl.ds(g * features, features)],
            sems.at[1, g],
        )
        for g in range(parts)
    ]
    for copy in folds + slices:
        copy.start()
    for copy in folds:
        copy.wait()
    sends = [
        pltpu.make_async_copy(held_ref, out_ref.at[s, pl.ds(rows, rows), :], sems.at[2, s])
        for s in range(parts)
    ]
    for copy in sends:
        copy.start()
    for copy in slices + sends:
        copy.wait()


def table_kernel(sizes, place_ref, tenants_ref, held_ref, other_ref, out_ref, sems):
    xlo_n, far_n, near_n, core_n = sizes
    _, far, _, core = split_place(place_ref[0], sizes)
    for xlo in range(xlo_n):
        for near in range(near_n):
            block = ((xlo * far_n + far) * near_n + near) * core_n + core
            _, source_far, _, source_core = split_place(tenants_ref[block], sizes)
            slot = xlo * near_n + near

            @pl.when(source_core == core)
            def _():
                pltpu.make_async_copy(
                    held_ref.at[source_far], out_ref.at[slot], sems.at[slot]
                ).start()

            @pl.when(source_core != core)
            def _():
                pltpu.make_async_copy(
                    other_ref.at[source_far], out_ref.at[slot], sems.at[slot]
                ).start()

    for slot in range(xlo_n * near_n):
        pltpu.make_async_copy(held_ref.at[0], out_ref.at[slot], sems.at[slot]).wait()


def value_kernel(columns_ref, weight_ref, out_ref):
    sources, rows, width = columns_ref.shape
    columns = columns_ref[...].reshape(sources * rows, width)
    part = dot(columns, weight_ref[...], 1, 0).astype(jnp.bfloat16)
    parts, _, features = out_ref.shape
    for s in range(parts):
        out_ref[s] = part[:, s * features : (s + 1) * features]


def low_kernel(
    sizes,
    place_ref,
    tenants_ref,
    offered_ref,
    arrived_ref,
    upstream_ref,
    _,
    out_ref,
    item_ref,
    sem,
):
    xlo, _, near, _ = split_place(tenants_ref[place_ref[0]], sizes)
    copy = pltpu.make_async_copy(offered_ref.at[xlo * sizes[2] + near], item_ref, sem)
    copy.start()
    copy.wait()
    sources, rows, width = arrived_ref.shape[0], arrived_ref.shape[1] // 2, arrived_ref.shape[2]
    columns = arrived_ref[:, :rows, :].reshape(sources * rows, width)
    low = dot(item_ref[:, :width], columns, 1, 1)
    back = dot(item_ref[:, width:], upstream_ref[...], 1, 1)
    both = jnp.concatenate([low, back], axis=0).astype(jnp.bfloat16)
    ranks, lanes = both.shape[0], out_ref.shape[2]
    for s in range(out_ref.shape[0]):
        for g in range(both.shape[1] // lanes):
            out_ref[s, g * ranks : (g + 1) * ranks, :] = both[:, g * lanes : (g + 1) * lanes]


def rank_kernel(place_ref, lengths_ref, parts_ref, upstream_ref, both_ref, out_ref):
    length = lengths_ref[place_ref[0]]
    total = parts_ref[0].astype(jnp.float32)
    for s in range(1, parts_ref.shape[0]):
        total = total + parts_ref[s].astype(jnp.float32)
    ranks = both_ref.shape[0]
    total = jnp.concatenate(
        [total[g * ranks : (g + 1) * ranks] for g in range(total.shape[0] // ranks)], axis=1
    )
    total = total.astype(jnp.bfloat16).astype(jnp.float32)
    live = lax.broadcasted_iota(jnp.int32, total.shape, 1) < length
    both = jnp.where(live, adapter_scale * total, 0.0).astype(jnp.bfloat16)
    both_ref[...] = both
    mine = dot(both[: ranks // 2], upstream_ref[...], 1, 0)
    for member in range(out_ref.shape[0]):
        out_ref[member] = mine


def route_kernel(sizes, place_ref, tenants_ref, parts_ref, out_ref, total_ref):
    xlo_n, far_n, near_n, core_n = sizes
    my_xlo, far, near, my_core = split_place(place_ref[0], sizes)
    total_ref[...] = jnp.zeros_like(total_ref)
    for xlo in range(xlo_n):
        for core in range(core_n):
            block = ((xlo * far_n + far) * near_n + near) * core_n + core
            to_xlo, to_far, to_near, to_core = split_place(tenants_ref[block], sizes)

            @pl.when((to_xlo == my_xlo) & (to_core == my_core))
            def _():
                total_ref[to_far * near_n + to_near] += parts_ref[xlo * core_n + core]

    out_ref[...] = total_ref[...].astype(out_ref.dtype)


def sum_kernel(parts_ref, out_ref):
    total = parts_ref[0].astype(jnp.float32)
    for s in range(1, parts_ref.shape[0]):
        total = total + parts_ref[s].astype(jnp.float32)
    out_ref[0] = total


def projected_kernel(width, parts_ref, both_ref, item_ref, out_ref):
    rank = item_ref.shape[0]
    total = parts_ref[0].astype(jnp.float32)
    for s in range(1, parts_ref.shape[0]):
        total = total + parts_ref[s].astype(jnp.float32)
    term = dot(both_ref[:rank], item_ref[:, width:], 0, 0)
    out_ref[...] = (total + term).astype(jnp.bfloat16)


def gradient_kernel(upstream_ref, weight_ref, both_ref, item_ref, out_ref):
    rank, width = item_ref.shape[0], weight_ref.shape[0]
    sources, _, lanes = upstream_ref.shape
    features = weight_ref.shape[1] // sources
    rows = jnp.concatenate(
        [
            jnp.concatenate(
                [upstream_ref[s, :, at : at + features] for s in range(sources)], axis=1
            )
            for at in range(0, lanes, features)
        ],
        axis=0,
    )
    total = dot(rows, weight_ref[...], 1, 1)
    total = total + dot(both_ref[rank:], item_ref[:, :width], 0, 0)
    out_ref[...] = total.astype(jnp.bfloat16)


def on_device(
    sizes, parts, tokens, base_weight, adapter_down, adapter_up, upstream, tenants, lengths
):
    bf16, f32 = jnp.bfloat16, jnp.float32
    xlo_n, far_n, near_n, core_n = sizes
    place = lax.axis_index(REP).astype(jnp.int32).reshape(1)
    rows, full_width = tokens.shape
    width = full_width // parts
    block, features = upstream.shape
    rank = adapter_up.shape[1]
    values = base_weight.shape[1]
    row_step = 128
    rank_rows = 2 * rank * block // features
    sent_rows = block + rank_rows

    slabs = pl.pallas_call(
        functools.partial(slab_kernel, parts),
        out_shape=struct((parts, 2 * rows, width), bf16),
        in_specs=[ANY, ANY],
        out_specs=ANY,
        scratch_shapes=[
            pltpu.VMEM((rows, width), bf16),
            pltpu.SemaphoreType.DMA((3, parts)),
        ],
        compiler_params=params(),
        name="slab",
    )(tokens, upstream)
    arrived = lax.all_to_all(slabs, "tp", 0, 0, tiled=True)

    own = jnp.concatenate([adapter_down[0].T, adapter_up[0]], axis=1)
    held = lax.all_gather(own, "far", axis=0, tiled=False)
    other = lax.ppermute(held, "core", [(c, (c + 1) % core_n) for c in range(core_n)])

    value_parts = pl.pallas_call(
        value_kernel,
        grid=(block // row_step,),
        out_shape=struct((parts, sent_rows, features), bf16),
        in_specs=[
            pl.BlockSpec((row_step // rows, rows, width), lambda i: (i, 0, 0)),
            pl.BlockSpec((width, values), lambda i: (0, 0)),
        ],
        out_specs=pl.BlockSpec((parts, row_step, features), lambda i: (0, i, 0)),
        compiler_params=params(),
        cost_estimate=cost(2 * block * width * values, 4 << 20),
        name="value",
    )(arrived, base_weight)

    table = pl.pallas_call(
        functools.partial(table_kernel, sizes),
        out_shape=struct((xlo_n * near_n,) + own.shape, bf16),
        in_specs=[SMEM, SMEM, ANY, ANY],
        out_specs=ANY,
        scratch_shapes=[pltpu.SemaphoreType.DMA((xlo_n * near_n,))],
        compiler_params=params(),
        name="table",
    )(place, tenants, held, other)
    offered = lax.all_to_all(table, ("xlo", "near"), 0, 0, tiled=True)

    sent, item = pl.pallas_call(
        functools.partial(low_kernel, sizes),
        grid=(1,),
        out_shape=(struct((parts, sent_rows, features), bf16), struct(own.shape, bf16)),
        in_specs=[SMEM, SMEM, ANY, VMEM, VMEM, ANY],
        out_specs=(
            pl.BlockSpec((parts, rank_rows, features), lambda i: (0, block // rank_rows, 0)),
            whole(own.shape),
        ),
        scratch_shapes=[pltpu.SemaphoreType.DMA],
        input_output_aliases={5: 0},
        compiler_params=params(),
        name="low",
    )(place, tenants, offered, arrived, upstream, value_parts)
    back = lax.all_to_all(sent, "tp", 0, 0, tiled=True)

    rank_spec = pl.BlockSpec(
        (parts, rank_rows, features), lambda i: (0, block // rank_rows, 0)
    )
    both, mine = pl.pallas_call(
        rank_kernel,
        grid=(1,),
        out_shape=(
            struct((2 * rank, block), bf16),
            struct((xlo_n * core_n, rank, features), f32),
        ),
        in_specs=[SMEM, SMEM, rank_spec, VMEM],
        out_specs=(
            whole((2 * rank, block)),
            whole((xlo_n * core_n, rank, features)),
        ),
        compiler_params=params(),
        name="rank",
    )(place, lengths, back, upstream)
    near_parts = lax.all_to_all(mine, ("xlo", "core"), 0, 0, tiled=True)
    routed = pl.pallas_call(
        functools.partial(route_kernel, sizes),
        grid=(1,),
        out_shape=struct((far_n * near_n, rank, features), bf16),
        in_specs=[SMEM, SMEM, whole((xlo_n * core_n, rank, features))],
        out_specs=whole((far_n * near_n, rank, features)),
        scratch_shapes=[pltpu.VMEM((far_n * near_n, rank, features), f32)],
        compiler_params=params(),
        name="route",
    )(place, tenants, near_parts)
    far_parts = lax.all_to_all(routed, ("far", "near"), 0, 0, tiled=True)
    up_grad = pl.pallas_call(
        sum_kernel,
        grid=(1,),
        out_shape=struct((1, rank, features), f32),
        in_specs=[whole((far_n * near_n, rank, features))],
        out_specs=whole((1, rank, features)),
        compiler_params=params(),
        name="total",
    )(far_parts)

    gradient = pl.pallas_call(
        gradient_kernel,
        grid=(block // row_step,),
        out_shape=struct((block, width), bf16),
        in_specs=[
            pl.BlockSpec(
                (parts, rows, row_step // rows * features), lambda i: (0, 1, i)
            ),
            pl.BlockSpec((width, values), lambda i: (0, 0)),
            pl.BlockSpec((2 * rank, row_step), lambda i: (0, i)),
            pl.BlockSpec(own.shape, lambda i: (0, 0)),
        ],
        out_specs=pl.BlockSpec((row_step, width), lambda i: (i, 0)),
        compiler_params=params(),
        cost_estimate=cost(2 * block * width * values, 4 << 20),
        name="gradient",
    )(arrived, base_weight, both, item)
    projected = pl.pallas_call(
        functools.partial(projected_kernel, width),
        grid=(1,),
        out_shape=struct((block, features), bf16),
        in_specs=[
            pl.BlockSpec((parts, block, features), lambda i: (0, 0, 0)),
            whole((2 * rank, block)),
            whole(own.shape),
        ],
        out_specs=whole((block, features)),
        compiler_params=params(),
        name="projected",
    )(back, both, item)
    return projected, gradient, up_grad


def solution(mesh):
    replicas, parts = mesh.devices.shape
    cores, xlo, near = 2, 2, 4
    sizes = (xlo, replicas // (xlo * near * cores), near, cores)
    fine = Mesh(mesh.devices.reshape(sizes + (parts,)), REP + ("tp",))
    return jax.shard_map(
        functools.partial(on_device, sizes, parts),
        mesh=fine,
        in_specs=(
            P(REP + ("tp",), None),
            P("tp", None),
            P(REP, "tp", None),
            P(REP, None, "tp"),
            P(REP, "tp"),
            P(),
            P(),
        ),
        out_specs=(P(REP, "tp"), P(REP, "tp"), P(REP, None, "tp")),
        check_vma=False,
    )
```

time: 1710 us -> 168 us (0.10)
  waiting for transfers between devices: 1040 us -> 28.9 us
  starting transfers between devices: 497 us -> 26.3 us
  loops' own time: 85.9 us -> 0 us
  blocking collectives: 37.8 us -> 82.7 us
    ppermute x254 -> x1, waiting for transfers between devices: 613 us -> 1.54 us  [on_device(): lax.ppermute(held, 'core', [(c, (c + 1) % core_n) for c in range(core_n)])]
    ppermute x254 -> x1, starting transfers between devices: 490 us -> 1.91 us  [on_device(): lax.ppermute(held, 'core', [(c, (c + 1) % core_n) for c in range(core_n)])]
    reduce_scatter x1 -> x0, waiting for transfers between devices: 419 us -> none  [on_device(): up_grad = lax.psum_scatter(table, 'rep', scatter_dimension=0, tiled=True)]
    another operation x1 -> x0, loops' own time: 85.9 us -> none  [on_device(): final_state = lax.fori_loop(1, replicas, visit_one, (own, start_held))]
    all_gather x0 -> x1, blocking collectives: none -> 53.9 us  [on_device(): held = lax.all_gather(own, 'far', axis=0, tiled=False)]
    psum x1 -> x0, blocking collectives: 37.8 us -> none  [on_device(): lax.psum(low_part.astype(jnp.bfloat16), 'tp').astype(jnp.float32)]
    all_to_all x0 -> x2, blocking collectives: none -> 28.8 us  [the longest x1 23 us: on_device(): back = lax.all_to_all(sent, 'tp', 0, 0, tiled=True)]
  transfers between devices with their start and end apart: 258 -> 4, of which waited for: 256 -> 3; matrix products, arithmetic and copies ran while one was open for 1% -> 0% of each run, Pallas kernels for 0% -> 5%
where the time goes in v1:
time: 168 us; the launch traced here: 165 us
  blocking collectives  82.7 us (49%)
  waiting for transfers between devices  28.9 us (17%)
  starting transfers between devices  26.3 us (16%)
  Pallas kernels  15 us (9%)
  local copies, waits for them, and re-layouts  11.4 us (7%)
    all_gather x1, blocking collectives, on_device(): held = lax.all_gather(own, 'far', axis=0, tiled=False)  53.9 us
    all_to_all x1, blocking collectives, on_device(): back = lax.all_to_all(sent, 'tp', 0, 0, tiled=True)  23 us
    all_to_all x1, waiting for transfers between devices, on_device(): far_parts = lax.all_to_all(routed, ('far', 'near'), 0, 0, tiled=True)  21.3 us
    all_to_all x1, starting transfers between devices, on_device(): far_parts = lax.all_to_all(routed, ('far', 'near'), 0, 0, tiled=True)  11.9 us
    unnamed x34, local copies, waits for them, and re-layouts  11.4 us
    all_to_all x1, starting transfers between devices, on_device(): arrived = lax.all_to_all(slabs, 'tp', 0, 0, tiled=True)  7.56 us
    all_to_all x1, waiting for transfers between devices, on_device(): offered = lax.all_to_all(table, ('xlo', 'near'), 0, 0, tiled=True)  6.1 us
    all_to_all x1, blocking collectives, on_device(): near_parts = lax.all_to_all(mine, ('xlo', 'core'), 0, 0, tiled=True)  5.78 us
  transfers between devices with their start and end apart: 4, of which 3 were waited for; matrix products, arithmetic and copies ran while one was open for 0% of the time, Pallas kernels for 5%

profile of v1, /device:TPU:6, one launch (start us, length us, event | category | flops | bytes accessed | tf_op | source)
XLA Modules:
  0.0 165.0 jit_solution(9511607971601948341)
XLA Ops:
  0.6 0.0 copy-start.4
  0.6 0.9 copy-done.4
  1.5 1.2 copy-done.6
  2.8 1.8 %slab.1 = bf16[8,128,1024]{2,1,0:T(8,128)(2,1)S(1)} custom-call(bf16[64,8192]{1,0:T(8,128)(2,1)S(1)} %copy-done.6, bf16[512,128]{1,0:T(8,128)(2,1)S(1)} %copy-done.4), custom_call_target="tpu_custom_call" | custom-call | tf_op jit(solution)/shard_map/slab/pallas_call | solution.py:226
  4.6 1.3 copy-done.3
  5.9 7.6 %all-to-all-start.1 = ((bf16[8,128,1024]{2,1,0:T(8,128)(2,1)}), bf16[8,128,1024]{2,1,0:T(8,128)(2,1)S(1)}, u32[]{:S(2)}, u32[]{:S(2)}) async-start(bf16[8,128,1024]{2,1,0:T(8,128)(2,1)} %copy-done.3), calls=%async_computation.1 | async-start | bytes 4194304 | tf_op jit(solution)/shard_map/all_to_all | solution.py:238
  13.5 53.9 %all-gather = bf16[128,1152]{1,0:T(8,128)(2,1)S(1)} all-gather(bf16[16,1152]{1,0:T(8,128)(2,1)S(1)} %pad_maximum_fusion), channel_id=2, replica_groups=mesh['xlo'=2,'far'=8,'near'=4,'core'=2,'tp'=8] {'far'}, dimensions={0}, use_global_device_ids=true | all-gather | bytes 331776 | tf_op jit(solution)/shard_map/all_gather | solution.py:241
  67.4 1.9 %collective-permute-start = (bf16[8,16,1152]{2,1,0:T(8,128)(2,1)S(1)}, bf16[8,16,1152]{2,1,0:T(8,128)(2,1)S(1)}, u32[]{:S(2)}, u32[]{:S(2)}) collective-permute-start(bf16[8,16,1152]{2,1,0:T(8,128)(2,1)S(1)} %bitcast.6), channel_id=1, source_target_pairs={{0,8},{8,0},{1,9},{9,1},{2,10},{10,2},{3,11},{11,3},{4,12},{12,4},... | collective-permute-start | bytes 884744 | tf_op jit(solution)/shard_map/ppermute | solution.py:242
  69.3 1.5 collective-permute-done.other_ref
  70.9 1.3 table.1
  72.2 4.9 %all-to-all-start = ((bf16[8,16,1152]{2,1,0:T(8,128)(2,1)}), bf16[8,16,1152]{2,1,0:T(8,128)(2,1)}, u32[]{:S(2)}, u32[]{:S(2)}) async-start(bf16[8,16,1152]{2,1,0:T(8,128)(2,1)} %table.1), calls=%async_computation | async-start | bytes 589824 | tf_op jit(solution)/shard_map/all_to_all | solution.py:267
  77.1 1.6 copy-done.1
  78.7 2.0 %value.1._ = bf16[8,640,128]{2,1,0:T(8,128)(2,1)S(1)} custom-call(bf16[8,128,1024]{2,1,0:T(8,128)(2,1)S(1)} %all-to-all-done.1.columns_ref.arrived_ref.upstream_ref, bf16[1024,1024]{1,0:T(8,128)(2,1)S(1)} %copy-done.1), custom_call_target="tpu_custom_call" | custom-call | flops 1073741824 | bytes 4194304 | tf_op jit(solution)/shard_map/value/pallas_call | solution.py:244
  80.7 6.1 %all-to-all-done.offered_ref = bf16[8,16,1152]{2,1,0:T(8,128)(2,1)} async-done(((bf16[8,16,1152]{2,1,0:T(8,128)(2,1)}), bf16[8,16,1152]{2,1,0:T(8,128)(2,1)}, u32[]{:S(2)}, u32[]{:S(2)}) %all-to-all-start) | async-done | bytes 294944 | tf_op jit(solution)/shard_map/all_to_all | solution.py:267
  86.8 1.8 %low.1 = (bf16[8,640,128]{2,1,0:T(8,128)(2,1)S(1)}, bf16[16,1152]{1,0:T(8,128)(2,1)S(1)}) custom-call(s32[1]{0:T(128)} %bitcast.place_ref, s32[128]{0:T(128)S(1)} %copy-done.13, bf16[8,16,1152]{2,1,0:T(8,128)(2,1)} %all-to-all-done.offered_ref, ...), custom_call_target="tpu_custom_call", output_to_operand_aliasing={{0}: (5, {})} | custom-call | tf_op jit(solution)/shard_map/low/pallas_call | solution.py:269
  88.6 1.1 copy-done
  89.7 23.0 %all_to_all.25.parts_ref = bf16[8,640,128]{2,1,0:T(8,128)(2,1)S(1)} all-to-all(bf16[8,640,128]{2,1,0:T(8,128)(2,1)} %copy-done), channel_id=1, replica_groups=mesh['xlo'=2,'far'=8,'near'=4,'core'=2,'tp'=8] {'tp'}, dimensions={0} | all-to-all | bytes 2621440 | tf_op jit(solution)/shard_map/all_to_all | solution.py:283
  112.7 0.7 rank.1
  113.4 0.6 copy-done.10
  114.0 5.8 %all_to_all.26.parts_ref = f32[4,16,128]{2,1,0:T(8,128)S(1)} all-to-all(f32[4,16,128]{2,1,0:T(8,128)S(1)} %get-tuple-element.10), channel_id=1, replica_groups=mesh['xlo'=2,'far'=8,'near'=4,'core'=2,'tp'=8] {'xlo','core'}, dimensions={0} | all-to-all | bytes 65536 | tf_op jit(solution)/shard_map/all_to_all | solution.py:303
  119.8 1.3 route.1
  121.1 11.9 %all-to-all-start.4 = ((bf16[32,16,128]{2,1,0:T(8,128)(2,1)}), bf16[32,16,128]{2,1,0:T(8,128)(2,1)S(1)}, u32[]{:S(2)}, u32[]{:S(2)}) async-start(bf16[32,16,128]{2,1,0:T(8,128)(2,1)} %route.1), calls=%async_computation.4 | async-start | bytes 262144 | tf_op jit(solution)/shard_map/all_to_all | solution.py:314
  133.0 0.0 copy-start.8
  133.0 0.8 copy-done.8
  133.8 0.8 copy-done.11
  134.5 0.9 projected.1
  135.4 1.6 copy-done.2
  137.0 0.8 copy-done.9
  137.8 0.8 copy-done.12
  138.6 4.6 %gradient.1 = bf16[512,1024]{1,0:T(8,128)(2,1)} custom-call(bf16[8,128,1024]{2,1,0:T(8,128)(2,1)S(1)} %all-to-all-done.1.columns_ref.arrived_ref.upstream_ref, bf16[1024,1024]{1,0:T(8,128)(2,1)S(1)} %copy-done.2, bf16[32,512]{1,0:T(8,128)(2,1)S(1)} %copy-done.12, bf16[16,1152]{1,0:T(8,128)(2,1)S(1)} %copy-done.9), custom_call_target="tpu_custom_call" | custom-call | flops 1073741824 | bytes 4194304 | tf_op jit(solution)/shard_map/gradient/pallas_call | solution.py:325
  143.1 21.3 %all-to-all-done.4.parts_ref = bf16[32,16,128]{2,1,0:T(8,128)(2,1)S(1)} async-done(((bf16[32,16,128]{2,1,0:T(8,128)(2,1)}), bf16[32,16,128]{2,1,0:T(8,128)(2,1)S(1)}, u32[]{:S(2)}, u32[]{:S(2)}) %all-to-all-start.4) | async-done | bytes 131104 | tf_op jit(solution)/shard_map/all_to_all | solution.py:314
  164.4 0.6 total.1
  (23 shorter events, 0.0 us)
Async XLA Ops:
  0.6 0.9 copy-start.4
  1.5 1.2 copy-start.6
  4.6 1.3 copy-start.3
  5.9 7.6 %copy-start.15 = (bf16[1,1024,16]{1,2,0:T(8,128)(2,1)S(1)}, bf16[1,1024,16]{1,2,0:T(8,128)(2,1)}, u32[]{:S(2)}) copy-start(bf16[1,1024,16]{1,2,0:T(8,128)(2,1)} %param.9) | copy-start | bytes 98308
  5.9 7.6 %copy-start.16 = (bf16[1,16,128]{2,1,0:T(8,128)(2,1)S(1)}, bf16[1,16,128]{2,1,0:T(8,128)(2,1)}, u32[]{:S(2)}) copy-start(bf16[1,16,128]{2,1,0:T(8,128)(2,1)} %param.10) | copy-start | bytes 12292
  5.9 65.0 %copy-start.13 = (s32[128]{0:T(128)S(1)}, s32[128]{0:T(128)}, u32[]{:S(2)}) copy-start(s32[128]{0:T(128)} %tenants_ref.5) | copy-start | bytes 1540
  5.9 66.3 %all-to-all-start.1 = ((bf16[8,128,1024]{2,1,0:T(8,128)(2,1)}), bf16[8,128,1024]{2,1,0:T(8,128)(2,1)S(1)}, u32[]{:S(2)}, u32[]{:S(2)}) async-start(bf16[8,128,1024]{2,1,0:T(8,128)(2,1)} %copy-done.3), calls=%async_computation.1 | async-start | bytes 4194304 | tf_op jit(solution)/shard_map/all_to_all | solution.py:238
  67.4 3.5 %collective-permute-start = (bf16[8,16,1152]{2,1,0:T(8,128)(2,1)S(1)}, bf16[8,16,1152]{2,1,0:T(8,128)(2,1)S(1)}, u32[]{:S(2)}, u32[]{:S(2)}) collective-permute-start(bf16[8,16,1152]{2,1,0:T(8,128)(2,1)S(1)} %bitcast.6), channel_id=1, source_target_pairs={{0,8},{8,0},{1,9},{9,1},{2,10},{10,2},{3,11},{11,3},{4,12},{12,4},... | collective-permute-start | bytes 884744 | tf_op jit(solution)/shard_map/ppermute | solution.py:242
  72.2 14.6 %all-to-all-start = ((bf16[8,16,1152]{2,1,0:T(8,128)(2,1)}), bf16[8,16,1152]{2,1,0:T(8,128)(2,1)}, u32[]{:S(2)}, u32[]{:S(2)}) async-start(bf16[8,16,1152]{2,1,0:T(8,128)(2,1)} %table.1), calls=%async_computation | async-start | bytes 589824 | tf_op jit(solution)/shard_map/all_to_all | solution.py:267
  77.1 1.6 copy-start.1
  78.7 8.1 %copy-start.5 = (bf16[512,128]{1,0:T(8,128)(2,1)S(1)}, bf16[512,128]{1,0:T(8,128)(2,1)}, u32[]{:S(2)}) copy-start(bf16[512,128]{1,0:T(8,128)(2,1)} %upstream_ref.5) | copy-start | bytes 393220
  88.6 1.1 copy-start
  89.7 23.7 %copy-start.7 = (bf16[16,1152]{1,0:T(8,128)(2,1)}, bf16[16,1152]{1,0:T(8,128)(2,1)S(1)}, u32[]{:S(2)}) copy-start(bf16[16,1152]{1,0:T(8,128)(2,1)S(1)} %get-tuple-element.9.item_ref) | copy-start | bytes 110596
  89.7 23.0 %copy-start.14 = (s32[128]{0:T(128)S(1)}, s32[128]{0:T(128)}, u32[]{:S(2)}) copy-start(s32[128]{0:T(128)} %lengths_ref.1) | copy-start | bytes 1540
  113.4 0.6 copy-start.10
  121.1 43.4 %all-to-all-start.4 = ((bf16[32,16,128]{2,1,0:T(8,128)(2,1)}), bf16[32,16,128]{2,1,0:T(8,128)(2,1)S(1)}, u32[]{:S(2)}, u32[]{:S(2)}) async-start(bf16[32,16,128]{2,1,0:T(8,128)(2,1)} %route.1), calls=%async_computation.4 | async-start | bytes 262144 | tf_op jit(solution)/shard_map/all_to_all | solution.py:314
  133.0 0.8 copy-start.8
  133.8 0.8 copy-start.11
  135.4 1.6 copy-start.2
  137.0 0.8 copy-start.9
  137.8 0.8 copy-start.12

commit v2 on v1

--- a/solution.py
+++ b/solution.py
@@ -12,10 +12,11 @@
 VMEM = pl.BlockSpec(memory_space=pltpu.VMEM)
 SMEM = pl.BlockSpec(memory_space=pltpu.SMEM)
 ANY = pl.BlockSpec(memory_space=pl.ANY)
+HBM = pl.BlockSpec(memory_space=pltpu.HBM)
 REP = ("xlo", "far", "near", "core")
 
 
-def params(mib=24):
+def params(mib=8):
     return pltpu.CompilerParams(vmem_limit_bytes=mib * 1024 * 1024)
 
 
@@ -104,13 +105,15 @@
         pltpu.make_async_copy(held_ref.at[0], out_ref.at[slot], sems.at[slot]).wait()
 
 
-def value_kernel(columns_ref, weight_ref, out_ref):
+def value_kernel(columns_ref, weight_ref, *refs):
+    outs, held_ref = refs[:-1], refs[-1]
     sources, rows, width = columns_ref.shape
     columns = columns_ref[...].reshape(sources * rows, width)
-    part = dot(columns, weight_ref[...], 1, 0).astype(jnp.bfloat16)
-    parts, _, features = out_ref.shape
-    for s in range(parts):
-        out_ref[s] = part[:, s * features : (s + 1) * features]
+    held_ref[...] = dot(columns, weight_ref[...], 1, 0).astype(jnp.bfloat16)
+    me, parts, features = lax.axis_index("tp"), len(outs), outs[0].shape[1]
+    for k, out_ref in enumerate(outs):
+        at = pl.multiple_of(lax.rem(me + k, parts) * features, features)
+        out_ref[...] = held_ref[:, pl.ds(at, features)]
 
 
 def low_kernel(
@@ -120,7 +123,6 @@
     offered_ref,
     arrived_ref,
     upstream_ref,
-    _,
     out_ref,
     item_ref,
     sem,
@@ -134,10 +136,8 @@
     low = dot(item_ref[:, :width], columns, 1, 1)
     back = dot(item_ref[:, width:], upstream_ref[...], 1, 1)
     both = jnp.concatenate([low, back], axis=0).astype(jnp.bfloat16)
-    ranks, lanes = both.shape[0], out_ref.shape[2]
     for s in range(out_ref.shape[0]):
-        for g in range(both.shape[1] // lanes):
-            out_ref[s, g * ranks : (g + 1) * ranks, :] = both[:, g * lanes : (g + 1) * lanes]
+        out_ref[s] = both
 
 
 def rank_kernel(place_ref, lengths_ref, parts_ref, upstream_ref, both_ref, out_ref):
@@ -146,9 +146,6 @@
     for s in range(1, parts_ref.shape[0]):
         total = total + parts_ref[s].astype(jnp.float32)
     ranks = both_ref.shape[0]
-    total = jnp.concatenate(
-        [total[g * ranks : (g + 1) * ranks] for g in range(total.shape[0] // ranks)], axis=1
-    )
     total = total.astype(jnp.bfloat16).astype(jnp.float32)
     live = lax.broadcasted_iota(jnp.int32, total.shape, 1) < length
     both = jnp.where(live, adapter_scale * total, 0.0).astype(jnp.bfloat16)
@@ -158,7 +155,8 @@
         out_ref[member] = mine
 
 
-def route_kernel(sizes, place_ref, tenants_ref, parts_ref, out_ref, total_ref):
+def route_kernel(sizes, place_ref, tenants_ref, parts_ref, *refs):
+    out_ref, total_ref = refs[-2:]
     xlo_n, far_n, near_n, core_n = sizes
     my_xlo, far, near, my_core = split_place(place_ref[0], sizes)
     total_ref[...] = jnp.zeros_like(total_ref)
@@ -181,11 +179,11 @@
     out_ref[0] = total
 
 
-def projected_kernel(width, parts_ref, both_ref, item_ref, out_ref):
-    rank = item_ref.shape[0]
-    total = parts_ref[0].astype(jnp.float32)
-    for s in range(1, parts_ref.shape[0]):
-        total = total + parts_ref[s].astype(jnp.float32)
+def projected_kernel(width, both_ref, item_ref, *refs):
+    rank, out_ref = item_ref.shape[0], refs[-1]
+    total = refs[0][...].astype(jnp.float32)
+    for part_ref in refs[1:-1]:
+        total = total + part_ref[...].astype(jnp.float32)
     term = dot(both_ref[:rank], item_ref[:, width:], 0, 0)
     out_ref[...] = (total + term).astype(jnp.bfloat16)
 
@@ -220,19 +218,16 @@
     rank = adapter_up.shape[1]
     values = base_weight.shape[1]
     row_step = 128
-    rank_rows = 2 * rank * block // features
-    sent_rows = block + rank_rows
-
     slabs = pl.pallas_call(
         functools.partial(slab_kernel, parts),
         out_shape=struct((parts, 2 * rows, width), bf16),
-        in_specs=[ANY, ANY],
-        out_specs=ANY,
+        in_specs=[HBM, HBM],
+        out_specs=HBM,
         scratch_shapes=[
             pltpu.VMEM((rows, width), bf16),
             pltpu.SemaphoreType.DMA((3, parts)),
         ],
-        compiler_params=params(),
+        compiler_params=params(60),
         name="slab",
     )(tokens, upstream)
     arrived = lax.all_to_all(slabs, "tp", 0, 0, tiled=True)
@@ -244,13 +239,14 @@
     value_parts = pl.pallas_call(
         value_kernel,
         grid=(block // row_step,),
-        out_shape=struct((parts, sent_rows, features), bf16),
+        out_shape=[struct((block, features), bf16)] * parts,
         in_specs=[
             pl.BlockSpec((row_step // rows, rows, width), lambda i: (i, 0, 0)),
             pl.BlockSpec((width, values), lambda i: (0, 0)),
         ],
-        out_specs=pl.BlockSpec((parts, row_step, features), lambda i: (0, i, 0)),
-        compiler_params=params(),
+        out_specs=[pl.BlockSpec((row_step, features), lambda i: (i, 0))] * parts,
+        scratch_shapes=[pltpu.VMEM((row_step, values), bf16)],
+        compiler_params=params(12),
         cost_estimate=cost(2 * block * width * values, 4 << 20),
         name="value",
     )(arrived, base_weight)
@@ -269,22 +265,15 @@
     sent, item = pl.pallas_call(
         functools.partial(low_kernel, sizes),
         grid=(1,),
-        out_shape=(struct((parts, sent_rows, features), bf16), struct(own.shape, bf16)),
-        in_specs=[SMEM, SMEM, ANY, VMEM, VMEM, ANY],
-        out_specs=(
-            pl.BlockSpec((parts, rank_rows, features), lambda i: (0, block // rank_rows, 0)),
-            whole(own.shape),
-        ),
+        out_shape=(struct((parts, 2 * rank, block), bf16), struct(own.shape, bf16)),
+        in_specs=[SMEM, SMEM, ANY, VMEM, VMEM],
+        out_specs=(whole((parts, 2 * rank, block)), whole(own.shape)),
         scratch_shapes=[pltpu.SemaphoreType.DMA],
-        input_output_aliases={5: 0},
         compiler_params=params(),
         name="low",
-    )(place, tenants, offered, arrived, upstream, value_parts)
+    )(place, tenants, offered, arrived, upstream)
     back = lax.all_to_all(sent, "tp", 0, 0, tiled=True)
 
-    rank_spec = pl.BlockSpec(
-        (parts, rank_rows, features), lambda i: (0, block // rank_rows, 0)
-    )
     both, mine = pl.pallas_call(
         rank_kernel,
         grid=(1,),
@@ -292,7 +281,7 @@
             struct((2 * rank, block), bf16),
             struct((xlo_n * core_n, rank, features), f32),
         ),
-        in_specs=[SMEM, SMEM, rank_spec, VMEM],
+        in_specs=[SMEM, SMEM, whole((parts, 2 * rank, block)), VMEM],
         out_specs=(
             whole((2 * rank, block)),
             whole((xlo_n * core_n, rank, features)),
@@ -301,17 +290,23 @@
         name="rank",
     )(place, lengths, back, upstream)
     near_parts = lax.all_to_all(mine, ("xlo", "core"), 0, 0, tiled=True)
-    routed = pl.pallas_call(
+    *value_parts, routed = pl.pallas_call(
         functools.partial(route_kernel, sizes),
         grid=(1,),
-        out_shape=struct((far_n * near_n, rank, features), bf16),
-        in_specs=[SMEM, SMEM, whole((xlo_n * core_n, rank, features))],
-        out_specs=whole((far_n * near_n, rank, features)),
+        out_shape=[struct((block, features), bf16)] * parts
+        + [struct((far_n * near_n, rank, features), bf16)],
+        in_specs=[SMEM, SMEM, whole((xlo_n * core_n, rank, features))] + [ANY] * parts,
+        out_specs=[ANY] * parts + [whole((far_n * near_n, rank, features))],
         scratch_shapes=[pltpu.VMEM((far_n * near_n, rank, features), f32)],
+        input_output_aliases={3 + k: k for k in range(parts)},
         compiler_params=params(),
         name="route",
-    )(place, tenants, near_parts)
+    )(place, tenants, near_parts, *value_parts)
     far_parts = lax.all_to_all(routed, ("far", "near"), 0, 0, tiled=True)
+    value_sums = [value_parts[0]] + [
+        lax.ppermute(value_parts[k], "tp", [(d, (d + k) % parts) for d in range(parts)])
+        for k in range(1, parts)
+    ]
     up_grad = pl.pallas_call(
         sum_kernel,
         grid=(1,),
@@ -335,7 +330,7 @@
             pl.BlockSpec(own.shape, lambda i: (0, 0)),
         ],
         out_specs=pl.BlockSpec((row_step, width), lambda i: (i, 0)),
-        compiler_params=params(),
+        compiler_params=params(12),
         cost_estimate=cost(2 * block * width * values, 4 << 20),
         name="gradient",
     )(arrived, base_weight, both, item)
@@ -343,15 +338,12 @@
         functools.partial(projected_kernel, width),
         grid=(1,),
         out_shape=struct((block, features), bf16),
-        in_specs=[
-            pl.BlockSpec((parts, block, features), lambda i: (0, 0, 0)),
-            whole((2 * rank, block)),
-            whole(own.shape),
-        ],
+        in_specs=[whole((2 * rank, block)), whole(own.shape)]
+        + [whole((block, features))] * parts,
         out_specs=whole((block, features)),
         compiler_params=params(),
         name="projected",
-    )(back, both, item)
+    )(both, item, *value_sums)
     return projected, gradient, up_grad
 
 

time: 168 us -> 188 us (1.12)
  Pallas kernels: 15 us -> 46.2 us
  waiting for transfers between devices: 28.9 us -> 2.17 us
  starting transfers between devices: 26.3 us -> 52.9 us
  local copies, waits for them, and re-layouts: 11.4 us -> 3.21 us
  blocking collectives: 82.7 us -> 80.1 us
    pallas_call x1, Pallas kernels: 1.8 us -> 33.1 us  [on_device(): pl.pallas_call(functools.partial(slab_kernel, parts), out_shape=struct((p...]
    ppermute x0 -> x7, starting transfers between devices: none -> 26.4 us  [on_device(): lax.ppermute(value_parts[k], 'tp', [(d, (d + k) % parts) for d in range(p...]
    all_to_all x1, waiting for transfers between devices: 21.3 us -> 0.01 us  [on_device(): far_parts = lax.all_to_all(routed, ('far', 'near'), 0, 0, tiled=True)]
    all_to_all x1, blocking collectives: 23 us -> 12.8 us  [on_device(): back = lax.all_to_all(sent, 'tp', 0, 0, tiled=True)]
    unnamed x34 -> x14, local copies, waits for them, and re-layouts: 11.4 us -> 3.21 us
    all_to_all x1, blocking collectives: 5.78 us -> 13.4 us  [on_device(): offered = lax.all_to_all(table, ('xlo', 'near'), 0, 0, tiled=True)]
    all_to_all x1, waiting for transfers between devices: 6.1 us -> 0.01 us  [on_device(): near_parts = lax.all_to_all(mine, ('xlo', 'core'), 0, 0, tiled=True)]
  transfers between devices with their start and end apart: 4 -> 11, of which waited for: 3 -> 2; matrix products, arithmetic and copies ran while one was open for 0% -> 0% of each run, Pallas kernels for 5% -> 5%
where the time goes in v2:
time: 188 us; the launch traced here: 185 us
  blocking collectives  80.1 us (43%)
  starting transfers between devices  52.9 us (28%)
  Pallas kernels  46.2 us (25%)
  local copies, waits for them, and re-layouts  3.21 us (2%)
  waiting for transfers between devices  2.17 us (1%)
    all_gather x1, blocking collectives, on_device(): held = lax.all_gather(own, 'far', axis=0, tiled=False)  53.9 us
    pallas_call x1, Pallas kernels, on_device(): pl.pallas_call(functools.partial(slab_kernel, parts), out_shape=struct((p...  33.1 us
    ppermute x7, starting transfers between devices, on_device(): lax.ppermute(value_parts[k], 'tp', [(d, (d + k) % parts) for d in range(p...  26.4 us
    all_to_all x1, blocking collectives, on_device(): offered = lax.all_to_all(table, ('xlo', 'near'), 0, 0, tiled=True)  13.4 us
    all_to_all x1, blocking collectives, on_device(): back = lax.all_to_all(sent, 'tp', 0, 0, tiled=True)  12.8 us
    all_to_all x1, starting transfers between devices, on_device(): far_parts = lax.all_to_all(routed, ('far', 'near'), 0, 0, tiled=True)  12.3 us
    all_to_all x1, starting transfers between devices, on_device(): arrived = lax.all_to_all(slabs, 'tp', 0, 0, tiled=True)  7.58 us
    all_to_all x1, starting transfers between devices, on_device(): near_parts = lax.all_to_all(mine, ('xlo', 'core'), 0, 0, tiled=True)  4.7 us
  transfers between devices with their start and end apart: 11, of which 2 were waited for; matrix products, arithmetic and copies ran while one was open for 0% of the time, Pallas kernels for 5%

profile of v2, /device:TPU:6, one launch (start us, length us, event | category | flops | bytes accessed | tf_op | source)
XLA Modules:
  0.0 185.4 jit_solution(4378134643919483610)
XLA Ops:
  0.6 33.1 %slab.1 = bf16[8,128,1024]{2,1,0:T(8,128)(2,1)} custom-call(bf16[64,8192]{1,0:T(8,128)(2,1)} %tokens_ref.1, bf16[512,128]{1,0:T(8,128)(2,1)} %upstream_ref.5), custom_call_target="tpu_custom_call" | custom-call | tf_op jit(solution)/shard_map/slab/pallas_call | solution.py:221
  33.7 0.0 copy-start.5
  33.8 0.0 copy-start.6
  33.8 0.0 copy-start.3
  33.8 0.0 copy-start.2
  33.8 7.6 %all-to-all-start.1 = ((bf16[8,128,1024]{2,1,0:T(8,128)(2,1)}), bf16[8,128,1024]{2,1,0:T(8,128)(2,1)S(1)}, u32[]{:S(2)}, u32[]{:S(2)}) async-start(bf16[8,128,1024]{2,1,0:T(8,128)(2,1)} %slab.1), calls=%async_computation.1 | async-start | bytes 4194304 | tf_op jit(solution)/shard_map/all_to_all | solution.py:233
  41.4 53.9 %all-gather = bf16[128,1152]{1,0:T(8,128)(2,1)S(1)} all-gather(bf16[16,1152]{1,0:T(8,128)(2,1)S(1)} %pad_maximum_fusion), channel_id=2, replica_groups=mesh['xlo'=2,'far'=8,'near'=4,'core'=2,'tp'=8] {'far'}, dimensions={0}, use_global_device_ids=true | all-gather | bytes 331776 | tf_op jit(solution)/shard_map/all_gather | solution.py:236
  95.3 1.9 %collective-permute-start = (bf16[8,16,1152]{2,1,0:T(8,128)(2,1)S(1)}, bf16[8,16,1152]{2,1,0:T(8,128)(2,1)S(1)}, u32[]{:S(2)}, u32[]{:S(2)}) collective-permute-start(bf16[8,16,1152]{2,1,0:T(8,128)(2,1)S(1)} %bitcast.6), channel_id=1, source_target_pairs={{0,8},{8,0},{1,9},{9,1},{2,10},{10,2},{3,11},{11,3},{4,12},{12,4},... | collective-permute-start | bytes 884744 | tf_op jit(solution)/shard_map/ppermute | solution.py:237
  97.2 1.5 collective-permute-done.other_ref
  98.8 1.1 table.1
  99.9 13.4 %all_to_all.25.offered_ref = bf16[8,16,1152]{2,1,0:T(8,128)(2,1)S(1)} all-to-all(bf16[8,16,1152]{2,1,0:T(8,128)(2,1)S(1)} %table.1), channel_id=1, replica_groups=mesh['xlo'=2,'far'=8,'near'=4,'core'=2,'tp'=8] {'xlo','near'}, dimensions={0} | all-to-all | bytes 589824 | tf_op jit(solution)/shard_map/all_to_all | solution.py:263
  113.3 1.0 low.1
  114.4 12.8 %all_to_all.26.parts_ref = bf16[8,32,512]{2,1,0:T(8,128)(2,1)S(1)} all-to-all(bf16[8,32,512]{2,1,0:T(8,128)(2,1)S(1)} %get-tuple-element.24), channel_id=1, replica_groups=mesh['xlo'=2,'far'=8,'near'=4,'core'=2,'tp'=8] {'tp'}, dimensions={0} | all-to-all | bytes 524288 | tf_op jit(solution)/shard_map/all_to_all | solution.py:275
  127.2 1.3 rank.1
  128.5 4.7 %all-to-all-start.3 = ((f32[4,16,128]{2,1,0:T(8,128)}), f32[4,16,128]{2,1,0:T(8,128)S(1)}, u32[]{:S(2)}, u32[]{:S(2)}) async-start(f32[4,16,128]{2,1,0:T(8,128)} %get-tuple-element.27), calls=%async_computation.3 | async-start | bytes 65536 | tf_op jit(solution)/shard_map/all_to_all | solution.py:292
  133.2 1.6 copy-done
  134.8 2.2 %value.1 = (bf16[512,128]{1,0:T(8,128)(2,1)S(1)}, bf16[512,128]{1,0:T(8,128)(2,1)S(1)}, bf16[512,128]{1,0:T(8,128)(2,1)S(1)}, bf16[512,128]{1,0:T(8,128)(2,1)S(1...) custom-call(bf16[8,128,1024]{2,1,0:T(8,128)(2,1)S(1)} %all-to-all-do, ...), custom_call_target="tpu_custom_call" | custom-call | flops 1073741824 | bytes 4194304 | tf_op jit(solution)/shard_map/value/pallas_call | solution.py:239
  137.0 1.3 route.1
  138.3 12.3 %all-to-all-start.4 = ((bf16[32,16,128]{2,1,0:T(8,128)(2,1)}), bf16[32,16,128]{2,1,0:T(8,128)(2,1)S(1)}, u32[]{:S(2)}, u32[]{:S(2)}) async-start(bf16[32,16,128]{2,1,0:T(8,128)(2,1)} %get-tuple-element.44), calls=%async_computation.4 | async-start | bytes 262144 | tf_op jit(solution)/shard_map/all_to_all | solution.py:305
  150.6 4.9 %collective-permute-start.1 = (bf16[512,128]{1,0:T(8,128)(2,1)S(1)}, bf16[512,128]{1,0:T(8,128)(2,1)S(1)}, u32[]{:S(2)}, u32[]{:S(2)}) collective-permute-start(bf16[512,128]{1,0:T(8,128)(2,1)S(1)} %get-tuple-element.37), channel_id=1, source_target_pairs={{0,1},{1,2},{2,3},{3,4},{4,5},{5,6},{6,7},{7,0},{8,9},{9,10},{10,1... | collective-permute-start | bytes 393224 | tf_op jit(solution)/shard_map/ppermute | solution.py:307
  155.5 2.7 %collective-permute-start.2 = (bf16[512,128]{1,0:T(8,128)(2,1)S(1)}, bf16[512,128]{1,0:T(8,128)(2,1)S(1)}, u32[]{:S(2)}, u32[]{:S(2)}) collective-permute-start(bf16[512,128]{1,0:T(8,128)(2,1)S(1)} %get-tuple-element.38), channel_id=1, source_target_pairs={{0,2},{1,3},{2,4},{3,5},{4,6},{5,7},{6,0},{7,1},{8,10},{9,11},{10,... | collective-permute-start | bytes 393224 | tf_op jit(solution)/shard_map/ppermute | solution.py:307
  158.3 3.7 %collective-permute-start.3 = (bf16[512,128]{1,0:T(8,128)(2,1)S(1)}, bf16[512,128]{1,0:T(8,128)(2,1)S(1)}, u32[]{:S(2)}, u32[]{:S(2)}) collective-permute-start(bf16[512,128]{1,0:T(8,128)(2,1)S(1)} %get-tuple-element.39), channel_id=1, source_target_pairs={{0,3},{1,4},{2,5},{3,6},{4,7},{5,0},{6,1},{7,2},{8,11},{9,12},{10,... | collective-permute-start | bytes 393224 | tf_op jit(solution)/shard_map/ppermute | solution.py:307
  162.0 3.7 %collective-permute-start.4 = (bf16[512,128]{1,0:T(8,128)(2,1)S(1)}, bf16[512,128]{1,0:T(8,128)(2,1)S(1)}, u32[]{:S(2)}, u32[]{:S(2)}) collective-permute-start(bf16[512,128]{1,0:T(8,128)(2,1)S(1)} %get-tuple-element.40), channel_id=1, source_target_pairs={{0,4},{1,5},{2,6},{3,7},{4,0},{5,1},{6,2},{7,3},{8,12},{9,13},{10,... | collective-permute-start | bytes 393224 | tf_op jit(solution)/shard_map/ppermute | solution.py:307
  165.7 6.9 %collective-permute-start.5 = (bf16[512,128]{1,0:T(8,128)(2,1)S(1)}, bf16[512,128]{1,0:T(8,128)(2,1)S(1)}, u32[]{:S(2)}, u32[]{:S(2)}) collective-permute-start(bf16[512,128]{1,0:T(8,128)(2,1)S(1)} %get-tuple-element.41), channel_id=1, source_target_pairs={{0,5},{1,6},{2,7},{3,0},{4,1},{5,2},{6,3},{7,4},{8,13},{9,14},{10,... | collective-permute-start | bytes 393224 | tf_op jit(solution)/shard_map/ppermute | solution.py:307
  172.7 1.9 %collective-permute-start.6 = (bf16[512,128]{1,0:T(8,128)(2,1)S(1)}, bf16[512,128]{1,0:T(8,128)(2,1)S(1)}, u32[]{:S(2)}, u32[]{:S(2)}) collective-permute-start(bf16[512,128]{1,0:T(8,128)(2,1)S(1)} %get-tuple-element.42), channel_id=1, source_target_pairs={{0,6},{1,7},{2,0},{3,1},{4,2},{5,3},{6,4},{7,5},{8,14},{9,15},{10,... | collective-permute-start | bytes 393224 | tf_op jit(solution)/shard_map/ppermute | solution.py:307
  174.6 2.5 %collective-permute-start.7 = (bf16[512,128]{1,0:T(8,128)(2,1)S(1)}, bf16[512,128]{1,0:T(8,128)(2,1)S(1)}, u32[]{:S(2)}, u32[]{:S(2)}) collective-permute-start(bf16[512,128]{1,0:T(8,128)(2,1)S(1)} %get-tuple-element.43), channel_id=1, source_target_pairs={{0,7},{1,0},{2,1},{3,2},{4,3},{5,4},{6,5},{7,6},{8,15},{9,8},{10,9... | collective-permute-start | bytes 393224 | tf_op jit(solution)/shard_map/ppermute | solution.py:307
  177.1 0.0 copy-start.1
  177.1 1.6 copy-done.1
  178.7 4.6 %gradient.1 = bf16[512,1024]{1,0:T(8,128)(2,1)} custom-call(bf16[8,128,1024]{2,1,0:T(8,128)(2,1)S(1)} %all-to-all-done.1.arrived_ref.columns_ref.upstream_ref, bf16[1024,1024]{1,0:T(8,128)(2,1)S(1)} %copy-done.1, bf16[32,512]{1,0:T(8,128)(2,1)S(1)} %get-tuple-element.25.both_ref, bf16[16,1152]{1,0:T(8,128)(2,1)S(1)} %get-tuple-element.26.item_ref), custom_call_target="tpu_custom_call" | custom-call | flops 1073741824 | bytes 4194304 | tf_op jit(solution)/shard_map/gradient/pallas_call | solution.py:320
  183.3 0.6 collective-permute-done.7.refs_7_
  183.9 0.9 projected.1
  184.8 0.6 total.1
  (17 shorter events, 0.0 us)
Async XLA Ops:
  33.7 7.6 %copy-start.5 = (bf16[1,1024,16]{1,2,0:T(8,128)(2,1)S(1)}, bf16[1,1024,16]{1,2,0:T(8,128)(2,1)}, u32[]{:S(2)}) copy-start(bf16[1,1024,16]{1,2,0:T(8,128)(2,1)} %param.9) | copy-start | bytes 98308
  33.8 7.6 %copy-start.6 = (bf16[1,16,128]{2,1,0:T(8,128)(2,1)S(1)}, bf16[1,16,128]{2,1,0:T(8,128)(2,1)}, u32[]{:S(2)}) copy-start(bf16[1,16,128]{2,1,0:T(8,128)(2,1)} %param.10) | copy-start | bytes 12292
  33.8 65.0 %copy-start.3 = (s32[128]{0:T(128)S(1)}, s32[128]{0:T(128)}, u32[]{:S(2)}) copy-start(s32[128]{0:T(128)} %tenants_ref.5) | copy-start | bytes 1540
  33.8 79.5 %copy-start.2 = (bf16[512,128]{1,0:T(8,128)(2,1)S(1)}, bf16[512,128]{1,0:T(8,128)(2,1)}, u32[]{:S(2)}) copy-start(bf16[512,128]{1,0:T(8,128)(2,1)} %upstream_ref.5) | copy-start | bytes 393220
  33.8 66.2 %all-to-all-start.1 = ((bf16[8,128,1024]{2,1,0:T(8,128)(2,1)}), bf16[8,128,1024]{2,1,0:T(8,128)(2,1)S(1)}, u32[]{:S(2)}, u32[]{:S(2)}) async-start(bf16[8,128,1024]{2,1,0:T(8,128)(2,1)} %slab.1), calls=%async_computation.1 | async-start | bytes 4194304 | tf_op jit(solution)/shard_map/all_to_all | solution.py:233
  95.3 3.5 %collective-permute-start = (bf16[8,16,1152]{2,1,0:T(8,128)(2,1)S(1)}, bf16[8,16,1152]{2,1,0:T(8,128)(2,1)S(1)}, u32[]{:S(2)}, u32[]{:S(2)}) collective-permute-start(bf16[8,16,1152]{2,1,0:T(8,128)(2,1)S(1)} %bitcast.6), channel_id=1, source_target_pairs={{0,8},{8,0},{1,9},{9,1},{2,10},{10,2},{3,11},{11,3},{4,12},{12,4},... | collective-permute-start | bytes 884744 | tf_op jit(solution)/shard_map/ppermute | solution.py:237
  98.8 28.4 %copy-start.4 = (s32[128]{0:T(128)S(1)}, s32[128]{0:T(128)}, u32[]{:S(2)}) copy-start(s32[128]{0:T(128)} %lengths_ref.1) | copy-start | bytes 1540
  128.5 8.5 %all-to-all-start.3 = ((f32[4,16,128]{2,1,0:T(8,128)}), f32[4,16,128]{2,1,0:T(8,128)S(1)}, u32[]{:S(2)}, u32[]{:S(2)}) async-start(f32[4,16,128]{2,1,0:T(8,128)} %get-tuple-element.27), calls=%async_computation.3 | async-start | bytes 65536 | tf_op jit(solution)/shard_map/all_to_all | solution.py:292
  133.2 1.6 copy-start
  138.3 46.5 %all-to-all-start.4 = ((bf16[32,16,128]{2,1,0:T(8,128)(2,1)}), bf16[32,16,128]{2,1,0:T(8,128)(2,1)S(1)}, u32[]{:S(2)}, u32[]{:S(2)}) async-start(bf16[32,16,128]{2,1,0:T(8,128)(2,1)} %get-tuple-element.44), calls=%async_computation.4 | async-start | bytes 262144 | tf_op jit(solution)/shard_map/all_to_all | solution.py:305
  150.6 22.0 %collective-permute-start.1 = (bf16[512,128]{1,0:T(8,128)(2,1)S(1)}, bf16[512,128]{1,0:T(8,128)(2,1)S(1)}, u32[]{:S(2)}, u32[]{:S(2)}) collective-permute-start(bf16[512,128]{1,0:T(8,128)(2,1)S(1)} %get-tuple-element.37), channel_id=1, source_target_pairs={{0,1},{1,2},{2,3},{3,4},{4,5},{5,6},{6,7},{7,0},{8,9},{9,10},{10,1... | collective-permute-start | bytes 393224 | tf_op jit(solution)/shard_map/ppermute | solution.py:307
  155.5 19.1 %collective-permute-start.2 = (bf16[512,128]{1,0:T(8,128)(2,1)S(1)}, bf16[512,128]{1,0:T(8,128)(2,1)S(1)}, u32[]{:S(2)}, u32[]{:S(2)}) collective-permute-start(bf16[512,128]{1,0:T(8,128)(2,1)S(1)} %get-tuple-element.38), channel_id=1, source_target_pairs={{0,2},{1,3},{2,4},{3,5},{4,6},{5,7},{6,0},{7,1},{8,10},{9,11},{10,... | collective-permute-start | bytes 393224 | tf_op jit(solution)/shard_map/ppermute | solution.py:307
  158.3 25.0 %collective-permute-start.3 = (bf16[512,128]{1,0:T(8,128)(2,1)S(1)}, bf16[512,128]{1,0:T(8,128)(2,1)S(1)}, u32[]{:S(2)}, u32[]{:S(2)}) collective-permute-start(bf16[512,128]{1,0:T(8,128)(2,1)S(1)} %get-tuple-element.39), channel_id=1, source_target_pairs={{0,3},{1,4},{2,5},{3,6},{4,7},{5,0},{6,1},{7,2},{8,11},{9,12},{10,... | collective-permute-start | bytes 393224 | tf_op jit(solution)/shard_map/ppermute | solution.py:307
  162.0 21.3 %collective-permute-start.4 = (bf16[512,128]{1,0:T(8,128)(2,1)S(1)}, bf16[512,128]{1,0:T(8,128)(2,1)S(1)}, u32[]{:S(2)}, u32[]{:S(2)}) collective-permute-start(bf16[512,128]{1,0:T(8,128)(2,1)S(1)} %get-tuple-element.40), channel_id=1, source_target_pairs={{0,4},{1,5},{2,6},{3,7},{4,0},{5,1},{6,2},{7,3},{8,12},{9,13},{10,... | collective-permute-start | bytes 393224 | tf_op jit(solution)/shard_map/ppermute | solution.py:307
  165.7 17.5 %collective-permute-start.5 = (bf16[512,128]{1,0:T(8,128)(2,1)S(1)}, bf16[512,128]{1,0:T(8,128)(2,1)S(1)}, u32[]{:S(2)}, u32[]{:S(2)}) collective-permute-start(bf16[512,128]{1,0:T(8,128)(2,1)S(1)} %get-tuple-element.41), channel_id=1, source_target_pairs={{0,5},{1,6},{2,7},{3,0},{4,1},{5,2},{6,3},{7,4},{8,13},{9,14},{10,... | collective-permute-start | bytes 393224 | tf_op jit(solution)/shard_map/ppermute | solution.py:307
  172.7 10.6 %collective-permute-start.6 = (bf16[512,128]{1,0:T(8,128)(2,1)S(1)}, bf16[512,128]{1,0:T(8,128)(2,1)S(1)}, u32[]{:S(2)}, u32[]{:S(2)}) collective-permute-start(bf16[512,128]{1,0:T(8,128)(2,1)S(1)} %get-tuple-element.42), channel_id=1, source_target_pairs={{0,6},{1,7},{2,0},{3,1},{4,2},{5,3},{6,4},{7,5},{8,14},{9,15},{10,... | collective-permute-start | bytes 393224 | tf_op jit(solution)/shard_map/ppermute | solution.py:307
  174.6 9.3 %collective-permute-start.7 = (bf16[512,128]{1,0:T(8,128)(2,1)S(1)}, bf16[512,128]{1,0:T(8,128)(2,1)S(1)}, u32[]{:S(2)}, u32[]{:S(2)}) collective-permute-start(bf16[512,128]{1,0:T(8,128)(2,1)S(1)} %get-tuple-element.43), channel_id=1, source_target_pairs={{0,7},{1,0},{2,1},{3,2},{4,3},{5,4},{6,5},{7,6},{8,15},{9,8},{10,9... | collective-permute-start | bytes 393224 | tf_op jit(solution)/shard_map/ppermute | solution.py:307
  177.1 1.6 copy-start.1

commit v3 on v2

--- a/solution.py
+++ b/solution.py
@@ -47,36 +47,42 @@
     return lax.div(index, far_n), lax.rem(index, far_n), near, core
 
 
-def slab_kernel(parts, tokens_ref, upstream_ref, out_ref, held_ref, sems):
+def slab_kernel(parts, tokens_ref, upstream_ref, out_ref, slices_ref, fold_ref, sems):
     rows, features = tokens_ref.shape[0], upstream_ref.shape[1]
     width = tokens_ref.shape[1] // parts
-    slices = [
-        pltpu.make_async_copy(
-            tokens_ref.at[:, pl.ds(s * width, width)],
-            out_ref.at[s, pl.ds(0, rows), :],
-            sems.at[0, s],
-        )
-        for s in range(parts)
-    ]
     folds = [
         pltpu.make_async_copy(
             upstream_ref.at[pl.ds(g * rows, rows), :],
-            held_ref.at[:, pl.ds(g * features, features)],
+            fold_ref.at[:, pl.ds(g * features, features)],
             sems.at[1, g],
         )
         for g in range(parts)
     ]
+    slices = [
+        pltpu.make_async_copy(
+            tokens_ref.at[:, pl.ds(s * width, width)], slices_ref.at[s], sems.at[0, s]
+        )
+        for s in range(parts)
+    ]
     for copy in folds + slices:
         copy.start()
+    sends = []
     for copy in folds:
         copy.wait()
-    sends = [
-        pltpu.make_async_copy(held_ref, out_ref.at[s, pl.ds(rows, rows), :], sems.at[2, s])
-        for s in range(parts)
-    ]
+    for s in range(parts):
+        sends.append(
+            pltpu.make_async_copy(fold_ref, out_ref.at[s, pl.ds(rows, rows), :], sems.at[2, s])
+        )
+        sends[-1].start()
+    for s in range(parts):
+        slices[s].wait()
+        sends.append(
+            pltpu.make_async_copy(
+                slices_ref.at[s], out_ref.at[s, pl.ds(0, rows), :], sems.at[3, s]
+            )
+        )
+        sends[-1].start()
     for copy in sends:
-        copy.start()
-    for copy in slices + sends:
         copy.wait()
 
 
@@ -123,10 +129,9 @@
     offered_ref,
     arrived_ref,
     upstream_ref,
-    out_ref,
-    item_ref,
-    sem,
+    *refs,
 ):
+    out_ref, item_ref, sem = refs[-3:]
     xlo, _, near, _ = split_place(tenants_ref[place_ref[0]], sizes)
     copy = pltpu.make_async_copy(offered_ref.at[xlo * sizes[2] + near], item_ref, sem)
     copy.start()
@@ -140,7 +145,8 @@
         out_ref[s] = both
 
 
-def rank_kernel(place_ref, lengths_ref, parts_ref, upstream_ref, both_ref, out_ref):
+def rank_kernel(place_ref, lengths_ref, parts_ref, upstream_ref, *refs):
+    both_ref, out_ref = refs[-2:]
     length = lengths_ref[place_ref[0]]
     total = parts_ref[0].astype(jnp.float32)
     for s in range(1, parts_ref.shape[0]):
@@ -158,16 +164,18 @@
 def route_kernel(sizes, place_ref, tenants_ref, parts_ref, *refs):
     out_ref, total_ref = refs[-2:]
     xlo_n, far_n, near_n, core_n = sizes
-    my_xlo, far, near, my_core = split_place(place_ref[0], sizes)
+    my_xlo, far, my_near, my_core = split_place(place_ref[0], sizes)
     total_ref[...] = jnp.zeros_like(total_ref)
     for xlo in range(xlo_n):
-        for core in range(core_n):
-            block = ((xlo * far_n + far) * near_n + near) * core_n + core
-            to_xlo, to_far, to_near, to_core = split_place(tenants_ref[block], sizes)
-
-            @pl.when((to_xlo == my_xlo) & (to_core == my_core))
-            def _():
-                total_ref[to_far * near_n + to_near] += parts_ref[xlo * core_n + core]
+        for near in range(near_n):
+            for core in range(core_n):
+                block = ((xlo * far_n + far) * near_n + near) * core_n + core
+                to_xlo, to_far, to_near, to_core = split_place(tenants_ref[block], sizes)
+                member = (xlo * near_n + near) * core_n + core
+
+                @pl.when((to_xlo == my_xlo) & (to_near == my_near) & (to_core == my_core))
+                def _():
+                    total_ref[to_far] += parts_ref[member]
 
     out_ref[...] = total_ref[...].astype(out_ref.dtype)
 
@@ -224,8 +232,9 @@
         in_specs=[HBM, HBM],
         out_specs=HBM,
         scratch_shapes=[
+            pltpu.VMEM((parts, rows, width), bf16),
             pltpu.VMEM((rows, width), bf16),
-            pltpu.SemaphoreType.DMA((3, parts)),
+            pltpu.SemaphoreType.DMA((4, parts)),
         ],
         compiler_params=params(60),
         name="slab",
@@ -262,56 +271,78 @@
     )(place, tenants, held, other)
     offered = lax.all_to_all(table, ("xlo", "near"), 0, 0, tiled=True)
 
-    sent, item = pl.pallas_call(
+    early, middle, late, last = (1, 2), (3, 4), (5,), (6, 7)
+    parcels = [struct((block, features), bf16)]
+    sums = [value_parts[0]]
+
+    def leave(buffers, hops):
+        return [
+            lax.ppermute(buffer, "tp", [(d, (d + k) % parts) for d in range(parts)])
+            for buffer, k in zip(buffers, hops)
+        ]
+
+    came = leave([value_parts[k] for k in early], early)
+    ahead = came + [value_parts[k] for k in middle]
+    *ahead, sent, item = pl.pallas_call(
         functools.partial(low_kernel, sizes),
         grid=(1,),
-        out_shape=(struct((parts, 2 * rank, block), bf16), struct(own.shape, bf16)),
-        in_specs=[SMEM, SMEM, ANY, VMEM, VMEM],
-        out_specs=(whole((parts, 2 * rank, block)), whole(own.shape)),
+        out_shape=parcels * len(ahead)
+        + [struct((parts, 2 * rank, block), bf16), struct(own.shape, bf16)],
+        in_specs=[SMEM, SMEM, ANY, VMEM, VMEM] + [ANY] * len(ahead),
+        out_specs=[ANY] * len(ahead) + [whole((parts, 2 * rank, block)), whole(own.shape)],
         scratch_shapes=[pltpu.SemaphoreType.DMA],
+        input_output_aliases={5 + k: k for k in range(len(ahead))},
         compiler_params=params(),
         name="low",
-    )(place, tenants, offered, arrived, upstream)
+    )(place, tenants, offered, arrived, upstream, *ahead)
+    sums += ahead[: len(early)]
     back = lax.all_to_all(sent, "tp", 0, 0, tiled=True)
 
-    both, mine = pl.pallas_call(
+    came = leave(ahead[len(early) :], middle)
+    ahead = came + [value_parts[k] for k in late]
+    *ahead, both, mine = pl.pallas_call(
         rank_kernel,
         grid=(1,),
-        out_shape=(
+        out_shape=parcels * len(ahead)
+        + [
             struct((2 * rank, block), bf16),
-            struct((xlo_n * core_n, rank, features), f32),
-        ),
-        in_specs=[SMEM, SMEM, whole((parts, 2 * rank, block)), VMEM],
-        out_specs=(
+            struct((xlo_n * near_n * core_n, rank, features), f32),
+        ],
+        in_specs=[SMEM, SMEM, whole((parts, 2 * rank, block)), VMEM] + [ANY] * len(ahead),
+        out_specs=[ANY] * len(ahead)
+        + [
             whole((2 * rank, block)),
-            whole((xlo_n * core_n, rank, features)),
-        ),
+            whole((xlo_n * near_n * core_n, rank, features)),
+        ],
+        input_output_aliases={4 + k: k for k in range(len(ahead))},
         compiler_params=params(),
         name="rank",
-    )(place, lengths, back, upstream)
-    near_parts = lax.all_to_all(mine, ("xlo", "core"), 0, 0, tiled=True)
-    *value_parts, routed = pl.pallas_call(
+    )(place, lengths, back, upstream, *ahead)
+    sums += ahead[: len(middle)]
+    near_parts = lax.all_to_all(mine, ("xlo", "near", "core"), 0, 0, tiled=True)
+
+    came = leave(ahead[len(middle) :], late)
+    ahead = came + [value_parts[k] for k in last]
+    *ahead, routed = pl.pallas_call(
         functools.partial(route_kernel, sizes),
         grid=(1,),
-        out_shape=[struct((block, features), bf16)] * parts
-        + [struct((far_n * near_n, rank, features), bf16)],
-        in_specs=[SMEM, SMEM, whole((xlo_n * core_n, rank, features))] + [ANY] * parts,
-        out_specs=[ANY] * parts + [whole((far_n * near_n, rank, features))],
-        scratch_shapes=[pltpu.VMEM((far_n * near_n, rank, features), f32)],
-        input_output_aliases={3 + k: k for k in range(parts)},
+        out_shape=parcels * len(ahead) + [struct((far_n, rank, features), bf16)],
+        in_specs=[SMEM, SMEM, whole((xlo_n * near_n * core_n, rank, features))]
+        + [ANY] * len(ahead),
+        out_specs=[ANY] * len(ahead) + [whole((far_n, rank, features))],
+        scratch_shapes=[pltpu.VMEM((far_n, rank, features), f32)],
+        input_output_aliases={3 + k: k for k in range(len(ahead))},
         compiler_params=params(),
         name="route",
-    )(place, tenants, near_parts, *value_parts)
-    far_parts = lax.all_to_all(routed, ("far", "near"), 0, 0, tiled=True)
-    value_sums = [value_parts[0]] + [
-        lax.ppermute(value_parts[k], "tp", [(d, (d + k) % parts) for d in range(parts)])
-        for k in range(1, parts)
-    ]
+    )(place, tenants, near_parts, *ahead)
+    sums += ahead[: len(late)]
+    far_parts = lax.all_to_all(routed, "far", 0, 0, tiled=True)
+    sums += leave(ahead[len(late) :], last)
     up_grad = pl.pallas_call(
         sum_kernel,
         grid=(1,),
         out_shape=struct((1, rank, features), f32),
-        in_specs=[whole((far_n * near_n, rank, features))],
+        in_specs=[whole((far_n, rank, features))],
         out_specs=whole((1, rank, features)),
         compiler_params=params(),
         name="total",
@@ -343,7 +374,7 @@
         out_specs=whole((block, features)),
         compiler_params=params(),
         name="projected",
-    )(both, item, *value_sums)
+    )(both, item, *sums)
     return projected, gradient, up_grad
 
 

time: 188 us -> 174 us (0.926)
  Pallas kernels: 46.2 us -> 16.7 us
  waiting for transfers between devices: 2.17 us -> 31.2 us
  blocking collectives: 80.1 us -> 53.9 us
  starting transfers between devices: 52.9 us -> 61.4 us
  local copies, waits for them, and re-layouts: 3.21 us -> 9.16 us
    pallas_call x1, Pallas kernels: 33.1 us -> 2.47 us  [on_device(): pl.pallas_call(functools.partial(slab_kernel, parts), out_shape=struct((p...]
    all_to_all x2 -> x0, blocking collectives: 26.2 us -> none  [the longest x1 13.4 us: on_device(): offered = lax.all_to_all(table, ('xlo', 'near'), 0, 0, tiled=True)]
    ppermute x7, waiting for transfers between devices: 0.62 us -> 19.7 us  [leave(): lax.ppermute(buffer, 'tp', [(d, (d + k) % parts) for d in range(parts)])]
    all_to_all x2 -> x4, starting transfers between devices: 17 us -> 27.3 us  [the longest x1 11.4 us: on_device(): far_parts = lax.all_to_all(routed, 'far', 0, 0, tiled=True)]
    all_to_all x2 -> x4, waiting for transfers between devices: 0.01 us -> 9.98 us  [the longest x1 9.97 us: on_device(): far_parts = lax.all_to_all(routed, 'far', 0, 0, tiled=True)]
    unnamed x14 -> x30, local copies, waits for them, and re-layouts: 3.21 us -> 9.16 us
  transfers between devices with their start and end apart: 11 -> 13, of which waited for: 2 -> 7; matrix products, arithmetic and copies ran while one was open for 0% -> 0% of each run, Pallas kernels for 5% -> 5%
where the time goes in v3:
time: 174 us; the launch traced here: 173 us
  starting transfers between devices  61.4 us (35%)
  blocking collectives  53.9 us (31%)
  waiting for transfers between devices  31.2 us (18%)
  Pallas kernels  16.7 us (10%)
  local copies, waits for them, and re-layouts  9.16 us (5%)
    all_gather x1, blocking collectives, on_device(): held = lax.all_gather(own, 'far', axis=0, tiled=False)  53.9 us
    ppermute x7, starting transfers between devices, leave(): lax.ppermute(buffer, 'tp', [(d, (d + k) % parts) for d in range(parts)])  24.7 us
    ppermute x7, waiting for transfers between devices, leave(): lax.ppermute(buffer, 'tp', [(d, (d + k) % parts) for d in range(parts)])  19.7 us
    all_to_all x1, starting transfers between devices, on_device(): far_parts = lax.all_to_all(routed, 'far', 0, 0, tiled=True)  11.4 us
    all_to_all x1, waiting for transfers between devices, on_device(): far_parts = lax.all_to_all(routed, 'far', 0, 0, tiled=True)  9.97 us
    unnamed x30, local copies, waits for them, and re-layouts  9.16 us
    all_to_all x1, starting transfers between devices, on_device(): arrived = lax.all_to_all(slabs, 'tp', 0, 0, tiled=True)  7.58 us
    all_to_all x1, starting transfers between devices, on_device(): near_parts = lax.all_to_all(mine, ('xlo', 'near', 'core'), 0, 0, tiled=True)  6.04 us
  transfers between devices with their start and end apart: 13, of which 7 were waited for; matrix products, arithmetic and copies ran while one was open for 0% of the time, Pallas kernels for 5%

profile of v3, /device:TPU:6, one launch (start us, length us, event | category | flops | bytes accessed | tf_op | source)
XLA Modules:
  0.0 173.3 jit_solution(10285553543317398961)
XLA Ops:
  0.6 2.5 %slab.1 = bf16[8,128,1024]{2,1,0:T(8,128)(2,1)} custom-call(bf16[64,8192]{1,0:T(8,128)(2,1)} %tokens_ref.1, bf16[512,128]{1,0:T(8,128)(2,1)} %upstream_ref.5), custom_call_target="tpu_custom_call" | custom-call | tf_op jit(solution)/shard_map/slab/pallas_call | solution.py:229
  3.1 7.6 %all-to-all-start.1 = ((bf16[8,128,1024]{2,1,0:T(8,128)(2,1)}), bf16[8,128,1024]{2,1,0:T(8,128)(2,1)S(1)}, u32[]{:S(2)}, u32[]{:S(2)}) async-start(bf16[8,128,1024]{2,1,0:T(8,128)(2,1)} %slab.1), calls=%async_computation.1 | async-start | bytes 4194304 | tf_op jit(solution)/shard_map/all_to_all | solution.py:242
  10.7 53.9 %all-gather = bf16[128,1152]{1,0:T(8,128)(2,1)S(1)} all-gather(bf16[16,1152]{1,0:T(8,128)(2,1)S(1)} %pad_maximum_fusion), channel_id=2, replica_groups=mesh['xlo'=2,'far'=8,'near'=4,'core'=2,'tp'=8] {'far'}, dimensions={0}, use_global_device_ids=true | all-gather | bytes 331776 | tf_op jit(solution)/shard_map/all_gather | solution.py:245
  64.7 1.9 %collective-permute-start = (bf16[8,16,1152]{2,1,0:T(8,128)(2,1)S(1)}, bf16[8,16,1152]{2,1,0:T(8,128)(2,1)S(1)}, u32[]{:S(2)}, u32[]{:S(2)}) collective-permute-start(bf16[8,16,1152]{2,1,0:T(8,128)(2,1)S(1)} %bitcast.6), channel_id=1, source_target_pairs={{0,8},{8,0},{1,9},{9,1},{2,10},{10,2},{3,11},{11,3},{4,12},{12,4},... | collective-permute-start | bytes 884744 | tf_op jit(solution)/shard_map/ppermute | solution.py:246
  66.6 1.5 collective-permute-done.other_ref
  68.1 1.3 table.1
  69.5 4.3 %all-to-all-start = ((bf16[8,16,1152]{2,1,0:T(8,128)(2,1)}), bf16[8,16,1152]{2,1,0:T(8,128)(2,1)S(1)}, u32[]{:S(2)}, u32[]{:S(2)}) async-start(bf16[8,16,1152]{2,1,0:T(8,128)(2,1)} %table.1), calls=%async_computation | async-start | bytes 589824 | tf_op jit(solution)/shard_map/all_to_all | solution.py:272
  73.8 1.6 copy-done
  75.4 2.2 %value.1 = (bf16[512,128]{1,0:T(8,128)(2,1)S(1)}, bf16[512,128]{1,0:T(8,128)(2,1)S(1)}, bf16[512,128]{1,0:T(8,128)(2,1)S(1)}, bf16[512,128]{1,0:T(8,128)(2,1)S(1...) custom-call(bf16[8,128,1024]{2,1,0:T(8,128)(2,1)S(1)} %all-to-all-do, ...), custom_call_target="tpu_custom_call" | custom-call | flops 1073741824 | bytes 4194304 | tf_op jit(solution)/shard_map/value/pallas_call | solution.py:248
  79.6 4.4 %collective-permute-start.1 = (bf16[512,128]{1,0:T(8,128)(2,1)S(1)}, bf16[512,128]{1,0:T(8,128)(2,1)S(1)}, u32[]{:S(2)}, u32[]{:S(2)}) collective-permute-start(bf16[512,128]{1,0:T(8,128)(2,1)S(1)} %get-tuple-element.26), channel_id=1, source_target_pairs={{0,1},{1,2},{2,3},{3,4},{4,5},{5,6},{6,7},{7,0},{8,9},{9,10},{10,1... | collective-permute-start | bytes 393224 | tf_op jit(solution)/shard_map/ppermute | solution.py:280
  84.0 3.2 %collective-permute-start.2 = (bf16[512,128]{1,0:T(8,128)(2,1)S(1)}, bf16[512,128]{1,0:T(8,128)(2,1)S(1)}, u32[]{:S(2)}, u32[]{:S(2)}) collective-permute-start(bf16[512,128]{1,0:T(8,128)(2,1)S(1)} %get-tuple-element.27), channel_id=1, source_target_pairs={{0,2},{1,3},{2,4},{3,5},{4,6},{5,7},{6,0},{7,1},{8,10},{9,11},{10,... | collective-permute-start | bytes 393224 | tf_op jit(solution)/shard_map/ppermute | solution.py:280
  87.2 1.2 collective-permute-done.1.refs_0_
  88.3 3.7 %collective-permute-done.2.refs_1_ = bf16[512,128]{1,0:T(8,128)(2,1)S(1)} collective-permute-done((bf16[512,128]{1,0:T(8,128)(2,1)S(1)}, bf16[512,128]{1,0:T(8,128)(2,1)S(1)}, u32[]{:S(2)}, u32[]{:S(2)}) %collective-permute-start.2) | collective-permute-done | bytes 131104 | tf_op jit(solution)/shard_map/ppermute | solution.py:280
  92.1 1.7 %low.1 = (bf16[512,128]{1,0:T(8,128)(2,1)S(1)}, bf16[512,128]{1,0:T(8,128)(2,1)S(1)}, bf16[512,128]{1,0:T(8,128)(2,1)S(1)}, bf16[512,128]{1,0:T(8,128)(2,1)S(1)}...) custom-call(s32[1]{0:T(128)} %bitcast.place_ref, ...), custom_call_target="tpu_custom_call", output_to_operand_aliasing={{0}: (5, {}), {1}: (6, {}), {2}: (7, {}), {3}: (8, {})} | custom-call | tf_op jit(solution)/shard_map/low/pallas_call | solution.py:286
  93.8 5.5 %all-to-all-start.2 = ((bf16[8,32,512]{2,1,0:T(8,128)(2,1)}), bf16[8,32,512]{2,1,0:T(8,128)(2,1)S(1)}, u32[]{:S(2)}, u32[]{:S(2)}) async-start(bf16[8,32,512]{2,1,0:T(8,128)(2,1)} %get-tuple-element.30), calls=%async_computation.2 | async-start | bytes 524288 | tf_op jit(solution)/shard_map/all_to_all | solution.py:299
  99.4 4.9 %collective-permute-start.3 = (bf16[512,128]{1,0:T(8,128)(2,1)S(1)}, bf16[512,128]{1,0:T(8,128)(2,1)S(1)}, u32[]{:S(2)}, u32[]{:S(2)}) collective-permute-start(bf16[512,128]{1,0:T(8,128)(2,1)S(1)} %get-tuple-element.31), channel_id=1, source_target_pairs={{0,3},{1,4},{2,5},{3,6},{4,7},{5,0},{6,1},{7,2},{8,11},{9,12},{10,... | collective-permute-start | bytes 393224 | tf_op jit(solution)/shard_map/ppermute | solution.py:280
  104.2 1.9 %collective-permute-start.4 = (bf16[512,128]{1,0:T(8,128)(2,1)S(1)}, bf16[512,128]{1,0:T(8,128)(2,1)S(1)}, u32[]{:S(2)}, u32[]{:S(2)}) collective-permute-start(bf16[512,128]{1,0:T(8,128)(2,1)S(1)} %get-tuple-element.32), channel_id=1, source_target_pairs={{0,4},{1,5},{2,6},{3,7},{4,0},{5,1},{6,2},{7,3},{8,12},{9,13},{10,... | collective-permute-start | bytes 393224 | tf_op jit(solution)/shard_map/ppermute | solution.py:280
  106.2 3.7 %collective-permute-done.3.refs_0_ = bf16[512,128]{1,0:T(8,128)(2,1)S(1)} collective-permute-done((bf16[512,128]{1,0:T(8,128)(2,1)S(1)}, bf16[512,128]{1,0:T(8,128)(2,1)S(1)}, u32[]{:S(2)}, u32[]{:S(2)}) %collective-permute-start.3) | collective-permute-done | bytes 131104 | tf_op jit(solution)/shard_map/ppermute | solution.py:280
  109.9 3.7 %collective-permute-done.4.refs_1_ = bf16[512,128]{1,0:T(8,128)(2,1)S(1)} collective-permute-done((bf16[512,128]{1,0:T(8,128)(2,1)S(1)}, bf16[512,128]{1,0:T(8,128)(2,1)S(1)}, u32[]{:S(2)}, u32[]{:S(2)}) %collective-permute-start.4) | collective-permute-done | bytes 131104 | tf_op jit(solution)/shard_map/ppermute | solution.py:280
  114.5 1.4 rank.1
  115.8 6.0 %all-to-all-start.3 = ((f32[16,16,128]{2,1,0:T(8,128)}), f32[16,16,128]{2,1,0:T(8,128)S(1)}, u32[]{:S(2)}, u32[]{:S(2)}) async-start(f32[16,16,128]{2,1,0:T(8,128)} %get-tuple-element.41), calls=%async_computation.3 | async-start | bytes 262144 | tf_op jit(solution)/shard_map/all_to_all | solution.py:322
  121.9 4.0 %collective-permute-start.5 = (bf16[512,128]{1,0:T(8,128)(2,1)S(1)}, bf16[512,128]{1,0:T(8,128)(2,1)S(1)}, u32[]{:S(2)}, u32[]{:S(2)}) collective-permute-start(bf16[512,128]{1,0:T(8,128)(2,1)S(1)} %get-tuple-element.42), channel_id=1, source_target_pairs={{0,5},{1,6},{2,7},{3,0},{4,1},{5,2},{6,3},{7,4},{8,13},{9,14},{10,... | collective-permute-start | bytes 393224 | tf_op jit(solution)/shard_map/ppermute | solution.py:280
  125.8 7.5 %collective-permute-done.5.refs_0_ = bf16[512,128]{1,0:T(8,128)(2,1)S(1)} collective-permute-done((bf16[512,128]{1,0:T(8,128)(2,1)S(1)}, bf16[512,128]{1,0:T(8,128)(2,1)S(1)}, u32[]{:S(2)}, u32[]{:S(2)}) %collective-permute-start.5) | collective-permute-done | bytes 131104 | tf_op jit(solution)/shard_map/ppermute | solution.py:280
  133.3 0.9 copy-done.4
  135.1 1.5 route.1
  137.9 11.4 %all-to-all-start.4 = ((bf16[8,16,128]{2,1,0:T(8,128)(2,1)}), bf16[8,16,128]{2,1,0:T(8,128)(2,1)S(1)}, u32[]{:S(2)}, u32[]{:S(2)}) async-start(bf16[8,16,128]{2,1,0:T(8,128)(2,1)} %get-tuple-element.48), calls=%async_computation.4 | async-start | bytes 65536 | tf_op jit(solution)/shard_map/all_to_all | solution.py:339
  149.3 2.3 %collective-permute-start.6 = (bf16[512,128]{1,0:T(8,128)(2,1)}, bf16[512,128]{1,0:T(8,128)(2,1)S(1)}, u32[]{:S(2)}, u32[]{:S(2)}) collective-permute-start(bf16[512,128]{1,0:T(8,128)(2,1)} %copy-done.5), channel_id=1, source_target_pairs={{0,6},{1,7},{2,0},{3,1},{4,2},{5,3},{6,4},{7,5},{8,14},{9,15},{10,... | collective-permute-start | bytes 393224 | tf_op jit(solution)/shard_map/ppermute | solution.py:280
  151.6 4.0 %collective-permute-start.7 = (bf16[512,128]{1,0:T(8,128)(2,1)}, bf16[512,128]{1,0:T(8,128)(2,1)S(1)}, u32[]{:S(2)}, u32[]{:S(2)}) collective-permute-start(bf16[512,128]{1,0:T(8,128)(2,1)} %copy-done.8), channel_id=1, source_target_pairs={{0,7},{1,0},{2,1},{3,2},{4,3},{5,4},{6,5},{7,6},{8,15},{9,8},{10,9... | collective-permute-start | bytes 393224 | tf_op jit(solution)/shard_map/ppermute | solution.py:280
  155.6 1.6 copy-done.1
  157.2 4.6 %gradient.1 = bf16[512,1024]{1,0:T(8,128)(2,1)} custom-call(bf16[8,128,1024]{2,1,0:T(8,128)(2,1)S(1)} %all-to-all-done.1.columns_ref.arrived_ref.upstream_ref, bf16[1024,1024]{1,0:T(8,128)(2,1)S(1)} %copy-done.1, bf16[32,512]{1,0:T(8,128)(2,1)S(1)} %get-tuple-element.34.both_ref, bf16[16,1152]{1,0:T(8,128)(2,1)S(1)} %get-tuple-element.35.item_ref), custom_call_target="tpu_custom_call" | custom-call | flops 1073741824 | bytes 4194304 | tf_op jit(solution)/shard_map/gradient/pallas_call | solution.py:351
  161.8 0.9 projected.1
  162.7 10.0 %all-to-all-done.4.parts_ref = bf16[8,16,128]{2,1,0:T(8,128)(2,1)S(1)} async-done(((bf16[8,16,128]{2,1,0:T(8,128)(2,1)}), bf16[8,16,128]{2,1,0:T(8,128)(2,1)S(1)}, u32[]{:S(2)}, u32[]{:S(2)}) %all-to-all-start.4) | async-done | bytes 32800 | tf_op jit(solution)/shard_map/all_to_all | solution.py:339
  (35 shorter events, 5.7 us)
Async XLA Ops:
  3.1 7.6 %copy-start.13 = (bf16[1,1024,16]{1,2,0:T(8,128)(2,1)S(1)}, bf16[1,1024,16]{1,2,0:T(8,128)(2,1)}, u32[]{:S(2)}) copy-start(bf16[1,1024,16]{1,2,0:T(8,128)(2,1)} %param.9) | copy-start | bytes 98308
  3.1 7.6 %copy-start.14 = (bf16[1,16,128]{2,1,0:T(8,128)(2,1)S(1)}, bf16[1,16,128]{2,1,0:T(8,128)(2,1)}, u32[]{:S(2)}) copy-start(bf16[1,16,128]{2,1,0:T(8,128)(2,1)} %param.10) | copy-start | bytes 12292
  3.1 65.0 %copy-start.11 = (s32[128]{0:T(128)S(1)}, s32[128]{0:T(128)}, u32[]{:S(2)}) copy-start(s32[128]{0:T(128)} %tenants_ref.5) | copy-start | bytes 1540
  3.1 66.3 %all-to-all-start.1 = ((bf16[8,128,1024]{2,1,0:T(8,128)(2,1)}), bf16[8,128,1024]{2,1,0:T(8,128)(2,1)S(1)}, u32[]{:S(2)}, u32[]{:S(2)}) async-start(bf16[8,128,1024]{2,1,0:T(8,128)(2,1)} %slab.1), calls=%async_computation.1 | async-start | bytes 4194304 | tf_op jit(solution)/shard_map/all_to_all | solution.py:242
  64.7 3.5 %collective-permute-start = (bf16[8,16,1152]{2,1,0:T(8,128)(2,1)S(1)}, bf16[8,16,1152]{2,1,0:T(8,128)(2,1)S(1)}, u32[]{:S(2)}, u32[]{:S(2)}) collective-permute-start(bf16[8,16,1152]{2,1,0:T(8,128)(2,1)S(1)} %bitcast.6), channel_id=1, source_target_pairs={{0,8},{8,0},{1,9},{9,1},{2,10},{10,2},{3,11},{11,3},{4,12},{12,4},... | collective-permute-start | bytes 884744 | tf_op jit(solution)/shard_map/ppermute | solution.py:246
  69.5 22.6 %all-to-all-start = ((bf16[8,16,1152]{2,1,0:T(8,128)(2,1)}), bf16[8,16,1152]{2,1,0:T(8,128)(2,1)S(1)}, u32[]{:S(2)}, u32[]{:S(2)}) async-start(bf16[8,16,1152]{2,1,0:T(8,128)(2,1)} %table.1), calls=%async_computation | async-start | bytes 589824 | tf_op jit(solution)/shard_map/all_to_all | solution.py:272
  73.8 1.6 copy-start
  75.4 16.7 %copy-start.2 = (bf16[512,128]{1,0:T(8,128)(2,1)S(1)}, bf16[512,128]{1,0:T(8,128)(2,1)}, u32[]{:S(2)}) copy-start(bf16[512,128]{1,0:T(8,128)(2,1)} %upstream_ref.5) | copy-start | bytes 393220
  77.6 0.6 copy-start.3
  78.3 0.7 copy-start.6
  78.9 0.7 copy-start.9
  79.6 34.0 %copy-start.12 = (s32[128]{0:T(128)S(1)}, s32[128]{0:T(128)}, u32[]{:S(2)}) copy-start(s32[128]{0:T(128)} %lengths_ref.1) | copy-start | bytes 1540
  79.6 8.8 %collective-permute-start.1 = (bf16[512,128]{1,0:T(8,128)(2,1)S(1)}, bf16[512,128]{1,0:T(8,128)(2,1)S(1)}, u32[]{:S(2)}, u32[]{:S(2)}) collective-permute-start(bf16[512,128]{1,0:T(8,128)(2,1)S(1)} %get-tuple-element.26), channel_id=1, source_target_pairs={{0,1},{1,2},{2,3},{3,4},{4,5},{5,6},{6,7},{7,0},{8,9},{9,10},{10,1... | collective-permute-start | bytes 393224 | tf_op jit(solution)/shard_map/ppermute | solution.py:280
  84.0 8.1 %collective-permute-start.2 = (bf16[512,128]{1,0:T(8,128)(2,1)S(1)}, bf16[512,128]{1,0:T(8,128)(2,1)S(1)}, u32[]{:S(2)}, u32[]{:S(2)}) collective-permute-start(bf16[512,128]{1,0:T(8,128)(2,1)S(1)} %get-tuple-element.27), channel_id=1, source_target_pairs={{0,2},{1,3},{2,4},{3,5},{4,6},{5,7},{6,0},{7,1},{8,10},{9,11},{10,... | collective-permute-start | bytes 393224 | tf_op jit(solution)/shard_map/ppermute | solution.py:280
  93.8 19.7 %all-to-all-start.2 = ((bf16[8,32,512]{2,1,0:T(8,128)(2,1)}), bf16[8,32,512]{2,1,0:T(8,128)(2,1)S(1)}, u32[]{:S(2)}, u32[]{:S(2)}) async-start(bf16[8,32,512]{2,1,0:T(8,128)(2,1)} %get-tuple-element.30), calls=%async_computation.2 | async-start | bytes 524288 | tf_op jit(solution)/shard_map/all_to_all | solution.py:299
  99.4 10.5 %collective-permute-start.3 = (bf16[512,128]{1,0:T(8,128)(2,1)S(1)}, bf16[512,128]{1,0:T(8,128)(2,1)S(1)}, u32[]{:S(2)}, u32[]{:S(2)}) collective-permute-start(bf16[512,128]{1,0:T(8,128)(2,1)S(1)} %get-tuple-element.31), channel_id=1, source_target_pairs={{0,3},{1,4},{2,5},{3,6},{4,7},{5,0},{6,1},{7,2},{8,11},{9,12},{10,... | collective-permute-start | bytes 393224 | tf_op jit(solution)/shard_map/ppermute | solution.py:280
  104.2 9.3 %collective-permute-start.4 = (bf16[512,128]{1,0:T(8,128)(2,1)S(1)}, bf16[512,128]{1,0:T(8,128)(2,1)S(1)}, u32[]{:S(2)}, u32[]{:S(2)}) collective-permute-start(bf16[512,128]{1,0:T(8,128)(2,1)S(1)} %get-tuple-element.32), channel_id=1, source_target_pairs={{0,4},{1,5},{2,6},{3,7},{4,0},{5,1},{6,2},{7,3},{8,12},{9,13},{10,... | collective-permute-start | bytes 393224 | tf_op jit(solution)/shard_map/ppermute | solution.py:280
  113.5 0.9 copy-start.10
  115.8 17.5 %all-to-all-start.3 = ((f32[16,16,128]{2,1,0:T(8,128)}), f32[16,16,128]{2,1,0:T(8,128)S(1)}, u32[]{:S(2)}, u32[]{:S(2)}) async-start(f32[16,16,128]{2,1,0:T(8,128)} %get-tuple-element.41), calls=%async_computation.3 | async-start | bytes 262144 | tf_op jit(solution)/shard_map/all_to_all | solution.py:322
  121.9 11.4 %collective-permute-start.5 = (bf16[512,128]{1,0:T(8,128)(2,1)S(1)}, bf16[512,128]{1,0:T(8,128)(2,1)S(1)}, u32[]{:S(2)}, u32[]{:S(2)}) collective-permute-start(bf16[512,128]{1,0:T(8,128)(2,1)S(1)} %get-tuple-element.42), channel_id=1, source_target_pairs={{0,5},{1,6},{2,7},{3,0},{4,1},{5,2},{6,3},{7,4},{8,13},{9,14},{10,... | collective-permute-start | bytes 393224 | tf_op jit(solution)/shard_map/ppermute | solution.py:280
  133.3 0.9 copy-start.4
  134.2 0.9 copy-start.7
  136.6 0.7 copy-start.5
  137.2 0.6 copy-start.8
  137.9 34.8 %all-to-all-start.4 = ((bf16[8,16,128]{2,1,0:T(8,128)(2,1)}), bf16[8,16,128]{2,1,0:T(8,128)(2,1)S(1)}, u32[]{:S(2)}, u32[]{:S(2)}) async-start(bf16[8,16,128]{2,1,0:T(8,128)(2,1)} %get-tuple-element.48), calls=%async_computation.4 | async-start | bytes 65536 | tf_op jit(solution)/shard_map/all_to_all | solution.py:339
  149.3 12.5 %collective-permute-start.6 = (bf16[512,128]{1,0:T(8,128)(2,1)}, bf16[512,128]{1,0:T(8,128)(2,1)S(1)}, u32[]{:S(2)}, u32[]{:S(2)}) collective-permute-start(bf16[512,128]{1,0:T(8,128)(2,1)} %copy-done.5), channel_id=1, source_target_pairs={{0,6},{1,7},{2,0},{3,1},{4,2},{5,3},{6,4},{7,5},{8,14},{9,15},{10,... | collective-permute-start | bytes 393224 | tf_op jit(solution)/shard_map/ppermute | solution.py:280
  151.6 10.2 %collective-permute-start.7 = (bf16[512,128]{1,0:T(8,128)(2,1)}, bf16[512,128]{1,0:T(8,128)(2,1)S(1)}, u32[]{:S(2)}, u32[]{:S(2)}) collective-permute-start(bf16[512,128]{1,0:T(8,128)(2,1)} %copy-done.8), channel_id=1, source_target_pairs={{0,7},{1,0},{2,1},{3,2},{4,3},{5,4},{6,5},{7,6},{8,15},{9,8},{10,9... | collective-permute-start | bytes 393224 | tf_op jit(solution)/shard_map/ppermute | solution.py:280
  155.6 1.6 copy-start.1

commit v4 on v2

--- a/solution.py
+++ b/solution.py
@@ -47,36 +47,42 @@
     return lax.div(index, far_n), lax.rem(index, far_n), near, core
 
 
-def slab_kernel(parts, tokens_ref, upstream_ref, out_ref, held_ref, sems):
+def slab_kernel(parts, tokens_ref, upstream_ref, out_ref, slices_ref, fold_ref, sems):
     rows, features = tokens_ref.shape[0], upstream_ref.shape[1]
     width = tokens_ref.shape[1] // parts
-    slices = [
-        pltpu.make_async_copy(
-            tokens_ref.at[:, pl.ds(s * width, width)],
-            out_ref.at[s, pl.ds(0, rows), :],
-            sems.at[0, s],
-        )
-        for s in range(parts)
-    ]
     folds = [
         pltpu.make_async_copy(
             upstream_ref.at[pl.ds(g * rows, rows), :],
-            held_ref.at[:, pl.ds(g * features, features)],
+            fold_ref.at[:, pl.ds(g * features, features)],
             sems.at[1, g],
         )
         for g in range(parts)
     ]
+    slices = [
+        pltpu.make_async_copy(
+            tokens_ref.at[:, pl.ds(s * width, width)], slices_ref.at[s], sems.at[0, s]
+        )
+        for s in range(parts)
+    ]
     for copy in folds + slices:
         copy.start()
+    sends = []
     for copy in folds:
         copy.wait()
-    sends = [
-        pltpu.make_async_copy(held_ref, out_ref.at[s, pl.ds(rows, rows), :], sems.at[2, s])
-        for s in range(parts)
-    ]
+    for s in range(parts):
+        sends.append(
+            pltpu.make_async_copy(fold_ref, out_ref.at[s, pl.ds(rows, rows), :], sems.at[2, s])
+        )
+        sends[-1].start()
+    for s in range(parts):
+        slices[s].wait()
+        sends.append(
+            pltpu.make_async_copy(
+                slices_ref.at[s], out_ref.at[s, pl.ds(0, rows), :], sems.at[3, s]
+            )
+        )
+        sends[-1].start()
     for copy in sends:
-        copy.start()
-    for copy in slices + sends:
         copy.wait()
 
 
@@ -106,7 +112,8 @@
 
 
 def value_kernel(columns_ref, weight_ref, *refs):
-    outs, held_ref = refs[:-1], refs[-1]
+    outs, mark_ref, held_ref = refs[:-2], refs[-2], refs[-1]
+    mark_ref[...] = jnp.zeros_like(mark_ref)
     sources, rows, width = columns_ref.shape
     columns = columns_ref[...].reshape(sources * rows, width)
     held_ref[...] = dot(columns, weight_ref[...], 1, 0).astype(jnp.bfloat16)
@@ -123,10 +130,9 @@
     offered_ref,
     arrived_ref,
     upstream_ref,
-    out_ref,
-    item_ref,
-    sem,
+    *refs,
 ):
+    out_ref, item_ref, sem = refs[-3:]
     xlo, _, near, _ = split_place(tenants_ref[place_ref[0]], sizes)
     copy = pltpu.make_async_copy(offered_ref.at[xlo * sizes[2] + near], item_ref, sem)
     copy.start()
@@ -140,7 +146,8 @@
         out_ref[s] = both
 
 
-def rank_kernel(place_ref, lengths_ref, parts_ref, upstream_ref, both_ref, out_ref):
+def rank_kernel(place_ref, lengths_ref, parts_ref, upstream_ref, *refs):
+    both_ref, out_ref = refs[-2:]
     length = lengths_ref[place_ref[0]]
     total = parts_ref[0].astype(jnp.float32)
     for s in range(1, parts_ref.shape[0]):
@@ -188,8 +195,8 @@
     out_ref[...] = (total + term).astype(jnp.bfloat16)
 
 
-def gradient_kernel(upstream_ref, weight_ref, both_ref, item_ref, out_ref):
-    rank, width = item_ref.shape[0], weight_ref.shape[0]
+def base_kernel(upstream_ref, weight_ref, out_ref, mark_ref):
+    mark_ref[...] = jnp.zeros_like(mark_ref)
     sources, _, lanes = upstream_ref.shape
     features = weight_ref.shape[1] // sources
     rows = jnp.concatenate(
@@ -201,9 +208,13 @@
         ],
         axis=0,
     )
-    total = dot(rows, weight_ref[...], 1, 1)
-    total = total + dot(both_ref[rank:], item_ref[:, :width], 0, 0)
-    out_ref[...] = total.astype(jnp.bfloat16)
+    out_ref[...] = dot(rows, weight_ref[...], 1, 1)
+
+
+def gradient_kernel(base_ref, both_ref, item_ref, out_ref):
+    rank, width = item_ref.shape[0], out_ref.shape[1]
+    term = dot(both_ref[rank:], item_ref[:, :width], 0, 0)
+    out_ref[...] = (base_ref[...] + term).astype(jnp.bfloat16)
 
 
 def on_device(
@@ -217,15 +228,17 @@
     block, features = upstream.shape
     rank = adapter_up.shape[1]
     values = base_weight.shape[1]
-    row_step = 128
+    row_step, base_step = 128, 256
+    mark = struct((8, 128), f32)
     slabs = pl.pallas_call(
         functools.partial(slab_kernel, parts),
         out_shape=struct((parts, 2 * rows, width), bf16),
         in_specs=[HBM, HBM],
         out_specs=HBM,
         scratch_shapes=[
+            pltpu.VMEM((parts, rows, width), bf16),
             pltpu.VMEM((rows, width), bf16),
-            pltpu.SemaphoreType.DMA((3, parts)),
+            pltpu.SemaphoreType.DMA((4, parts)),
         ],
         compiler_params=params(60),
         name="slab",
@@ -236,15 +249,16 @@
     held = lax.all_gather(own, "far", axis=0, tiled=False)
     other = lax.ppermute(held, "core", [(c, (c + 1) % core_n) for c in range(core_n)])
 
-    value_parts = pl.pallas_call(
+    *value_parts, value_mark = pl.pallas_call(
         value_kernel,
         grid=(block // row_step,),
-        out_shape=[struct((block, features), bf16)] * parts,
+        out_shape=[struct((block, features), bf16)] * parts + [mark],
         in_specs=[
             pl.BlockSpec((row_step // rows, rows, width), lambda i: (i, 0, 0)),
             pl.BlockSpec((width, values), lambda i: (0, 0)),
         ],
-        out_specs=[pl.BlockSpec((row_step, features), lambda i: (i, 0))] * parts,
+        out_specs=[pl.BlockSpec((row_step, features), lambda i: (i, 0))] * parts
+        + [whole(mark.shape)],
         scratch_shapes=[pltpu.VMEM((row_step, values), bf16)],
         compiler_params=params(12),
         cost_estimate=cost(2 * block * width * values, 4 << 20),
@@ -262,18 +276,34 @@
     )(place, tenants, held, other)
     offered = lax.all_to_all(table, ("xlo", "near"), 0, 0, tiled=True)
 
+    parcel = [struct((block, features), bf16)] * parts
     sent, item = pl.pallas_call(
         functools.partial(low_kernel, sizes),
         grid=(1,),
         out_shape=(struct((parts, 2 * rank, block), bf16), struct(own.shape, bf16)),
-        in_specs=[SMEM, SMEM, ANY, VMEM, VMEM],
+        in_specs=[SMEM, SMEM, ANY, VMEM, VMEM, ANY],
         out_specs=(whole((parts, 2 * rank, block)), whole(own.shape)),
         scratch_shapes=[pltpu.SemaphoreType.DMA],
         compiler_params=params(),
         name="low",
-    )(place, tenants, offered, arrived, upstream)
+    )(place, tenants, offered, arrived, upstream, value_mark)
     back = lax.all_to_all(sent, "tp", 0, 0, tiled=True)
 
+    base, base_mark = pl.pallas_call(
+        base_kernel,
+        grid=(block // base_step,),
+        out_shape=(struct((block, width), f32), mark),
+        in_specs=[
+            pl.BlockSpec(
+                (parts, rows, base_step // rows * features), lambda i: (0, 1, i)
+            ),
+            pl.BlockSpec((width, values), lambda i: (0, 0)),
+        ],
+        out_specs=(pl.BlockSpec((base_step, width), lambda i: (i, 0)), whole(mark.shape)),
+        compiler_params=params(16),
+        cost_estimate=cost(2 * block * width * values, 6 << 20),
+        name="base",
+    )(arrived, base_weight)
     both, mine = pl.pallas_call(
         rank_kernel,
         grid=(1,),
@@ -281,20 +311,19 @@
             struct((2 * rank, block), bf16),
             struct((xlo_n * core_n, rank, features), f32),
         ),
-        in_specs=[SMEM, SMEM, whole((parts, 2 * rank, block)), VMEM],
+        in_specs=[SMEM, SMEM, whole((parts, 2 * rank, block)), VMEM, ANY],
         out_specs=(
             whole((2 * rank, block)),
             whole((xlo_n * core_n, rank, features)),
         ),
         compiler_params=params(),
         name="rank",
-    )(place, lengths, back, upstream)
+    )(place, lengths, back, upstream, base_mark)
     near_parts = lax.all_to_all(mine, ("xlo", "core"), 0, 0, tiled=True)
     *value_parts, routed = pl.pallas_call(
         functools.partial(route_kernel, sizes),
         grid=(1,),
-        out_shape=[struct((block, features), bf16)] * parts
-        + [struct((far_n * near_n, rank, features), bf16)],
+        out_shape=parcel + [struct((far_n * near_n, rank, features), bf16)],
         in_specs=[SMEM, SMEM, whole((xlo_n * core_n, rank, features))] + [ANY] * parts,
         out_specs=[ANY] * parts + [whole((far_n * near_n, rank, features))],
         scratch_shapes=[pltpu.VMEM((far_n * near_n, rank, features), f32)],
@@ -303,7 +332,7 @@
         name="route",
     )(place, tenants, near_parts, *value_parts)
     far_parts = lax.all_to_all(routed, ("far", "near"), 0, 0, tiled=True)
-    value_sums = [value_parts[0]] + [
+    sums = [value_parts[0]] + [
         lax.ppermute(value_parts[k], "tp", [(d, (d + k) % parts) for d in range(parts)])
         for k in range(1, parts)
     ]
@@ -322,18 +351,15 @@
         grid=(block // row_step,),
         out_shape=struct((block, width), bf16),
         in_specs=[
-            pl.BlockSpec(
-                (parts, rows, row_step // rows * features), lambda i: (0, 1, i)
-            ),
-            pl.BlockSpec((width, values), lambda i: (0, 0)),
+            pl.BlockSpec((row_step, width), lambda i: (i, 0)),
             pl.BlockSpec((2 * rank, row_step), lambda i: (0, i)),
             pl.BlockSpec(own.shape, lambda i: (0, 0)),
         ],
         out_specs=pl.BlockSpec((row_step, width), lambda i: (i, 0)),
-        compiler_params=params(12),
-        cost_estimate=cost(2 * block * width * values, 4 << 20),
+        compiler_params=params(),
+        cost_estimate=cost(2 * block * width * rank, 3 << 20),
         name="gradient",
-    )(arrived, base_weight, both, item)
+    )(base, both, item)
     projected = pl.pallas_call(
         functools.partial(projected_kernel, width),
         grid=(1,),
@@ -343,7 +369,7 @@
         out_specs=whole((block, features)),
         compiler_params=params(),
         name="projected",
-    )(both, item, *value_sums)
+    )(both, item, *sums)
     return projected, gradient, up_grad
 
 

time: 188 us -> 156 us (0.83)
  Pallas kernels: 46.2 us -> 15 us
  blocking collectives: 80.1 us -> 59.7 us
  waiting for transfers between devices: 2.17 us -> 10.9 us
  starting transfers between devices: 52.9 us -> 59.6 us
  local copies, waits for them, and re-layouts: 3.21 us -> 7.7 us
    pallas_call x1, Pallas kernels: 33.1 us -> 2.43 us  [on_device(): pl.pallas_call(functools.partial(slab_kernel, parts), out_shape=struct((p...]
    all_to_all x2 -> x1, blocking collectives: 26.2 us -> 5.78 us  [on_device(): near_parts = lax.all_to_all(mine, ('xlo', 'core'), 0, 0, tiled=True)]
    all_to_all x1 -> x2, waiting for transfers between devices: 0.01 us -> 6.64 us  [the longest x1 5.08 us: on_device(): offered = lax.all_to_all(table, ('xlo', 'near'), 0, 0, tiled=True)]
    all_to_all x1 -> x2, starting transfers between devices: 4.7 us -> 11.3 us  [the longest x1 7.04 us: on_device(): back = lax.all_to_all(sent, 'tp', 0, 0, tiled=True)]
    unnamed x14 -> x24, local copies, waits for them, and re-layouts: 3.21 us -> 7.7 us
    pallas_call x1, Pallas kernels: 4.56 us -> 2.17 us  [on_device(): pl.pallas_call(gradient_kernel, grid=(block // row_step,), out_shape=stru...]
    ppermute x7, waiting for transfers between devices: 0.62 us -> 2.74 us  [on_device(): lax.ppermute(value_parts[k], 'tp', [(d, (d + k) % parts) for d in range(p...]
  transfers between devices with their start and end apart: 11 -> 12, of which waited for: 2 -> 4; matrix products, arithmetic and copies ran while one was open for 0% -> 0% of each run, Pallas kernels for 5% -> 5%
where the time goes in v4:
time: 156 us; the launch traced here: 154 us
  blocking collectives  59.7 us (38%)
  starting transfers between devices  59.6 us (38%)
  Pallas kernels  15 us (10%)
  waiting for transfers between devices  10.9 us (7%)
  local copies, waits for them, and re-layouts  7.7 us (5%)
    all_gather x1, blocking collectives, on_device(): held = lax.all_gather(own, 'far', axis=0, tiled=False)  53.9 us
    ppermute x7, starting transfers between devices, on_device(): lax.ppermute(value_parts[k], 'tp', [(d, (d + k) % parts) for d in range(p...  26.9 us
    all_to_all x1, starting transfers between devices, on_device(): far_parts = lax.all_to_all(routed, ('far', 'near'), 0, 0, tiled=True)  11.9 us
    unnamed x24, local copies, waits for them, and re-layouts  7.7 us
    all_to_all x1, starting transfers between devices, on_device(): arrived = lax.all_to_all(slabs, 'tp', 0, 0, tiled=True)  7.58 us
    all_to_all x1, starting transfers between devices, on_device(): back = lax.all_to_all(sent, 'tp', 0, 0, tiled=True)  7.04 us
    all_to_all x1, blocking collectives, on_device(): near_parts = lax.all_to_all(mine, ('xlo', 'core'), 0, 0, tiled=True)  5.78 us
    all_to_all x1, waiting for transfers between devices, on_device(): offered = lax.all_to_all(table, ('xlo', 'near'), 0, 0, tiled=True)  5.08 us
  transfers between devices with their start and end apart: 12, of which 4 were waited for; matrix products, arithmetic and copies ran while one was open for 0% of the time, Pallas kernels for 5%

profile of v4, /device:TPU:6, one launch (start us, length us, event | category | flops | bytes accessed | tf_op | source)
XLA Modules:
  0.0 153.8 jit_solution(15279760943629606723)
XLA Ops:
  0.6 2.4 %slab.1 = bf16[8,128,1024]{2,1,0:T(8,128)(2,1)} custom-call(bf16[64,8192]{1,0:T(8,128)(2,1)} %tokens_ref.1, bf16[512,128]{1,0:T(8,128)(2,1)} %upstream_ref.5), custom_call_target="tpu_custom_call" | custom-call | tf_op jit(solution)/shard_map/slab/pallas_call | solution.py:233
  3.1 7.6 %all-to-all-start.1 = ((bf16[8,128,1024]{2,1,0:T(8,128)(2,1)}), bf16[8,128,1024]{2,1,0:T(8,128)(2,1)S(1)}, u32[]{:S(2)}, u32[]{:S(2)}) async-start(bf16[8,128,1024]{2,1,0:T(8,128)(2,1)} %slab.1), calls=%async_computation.1 | async-start | bytes 4194304 | tf_op jit(solution)/shard_map/all_to_all | solution.py:246
  10.7 53.9 %all-gather = bf16[128,1152]{1,0:T(8,128)(2,1)S(1)} all-gather(bf16[16,1152]{1,0:T(8,128)(2,1)S(1)} %pad_maximum_fusion), channel_id=2, replica_groups=mesh['xlo'=2,'far'=8,'near'=4,'core'=2,'tp'=8] {'far'}, dimensions={0}, use_global_device_ids=true | all-gather | bytes 331776 | tf_op jit(solution)/shard_map/all_gather | solution.py:249
  64.6 1.9 %collective-permute-start = (bf16[8,16,1152]{2,1,0:T(8,128)(2,1)S(1)}, bf16[8,16,1152]{2,1,0:T(8,128)(2,1)S(1)}, u32[]{:S(2)}, u32[]{:S(2)}) collective-permute-start(bf16[8,16,1152]{2,1,0:T(8,128)(2,1)S(1)} %bitcast.6), channel_id=1, source_target_pairs={{0,8},{8,0},{1,9},{9,1},{2,10},{10,2},{3,11},{11,3},{4,12},{12,4},... | collective-permute-start | bytes 884744 | tf_op jit(solution)/shard_map/ppermute | solution.py:250
  66.6 1.5 collective-permute-done.other_ref
  68.1 1.3 table.1
  69.4 4.3 %all-to-all-start = ((bf16[8,16,1152]{2,1,0:T(8,128)(2,1)}), bf16[8,16,1152]{2,1,0:T(8,128)(2,1)S(1)}, u32[]{:S(2)}, u32[]{:S(2)}) async-start(bf16[8,16,1152]{2,1,0:T(8,128)(2,1)} %table.1), calls=%async_computation | async-start | bytes 589824 | tf_op jit(solution)/shard_map/all_to_all | solution.py:277
  73.7 1.6 %copy-done = bf16[1024,1024]{1,0:T(8,128)(2,1)S(1)} copy-done((bf16[1024,1024]{1,0:T(8,128)(2,1)S(1)}, bf16[1024,1024]{1,0:T(8,128)(2,1)}, u32[]{:S(2)}) %copy-start) | copy-done | bytes 2097176
  75.3 2.2 %value.1 = (bf16[512,128]{1,0:T(8,128)(2,1)S(1)}, bf16[512,128]{1,0:T(8,128)(2,1)S(1)}, bf16[512,128]{1,0:T(8,128)(2,1)S(1)}, bf16[512,128]{1,0:T(8,128)(2,1)S(1...) custom-call(bf16[8,128,1024]{2,1,0:T(8,128)(2,1)S(1)} %all-to-all-do, ...), custom_call_target="tpu_custom_call" | custom-call | flops 1073741824 | bytes 4194304 | tf_op jit(solution)/shard_map/value/pallas_call | solution.py:252
  78.2 5.1 %all-to-all-done.offered_ref = bf16[8,16,1152]{2,1,0:T(8,128)(2,1)S(1)} async-done(((bf16[8,16,1152]{2,1,0:T(8,128)(2,1)}), bf16[8,16,1152]{2,1,0:T(8,128)(2,1)S(1)}, u32[]{:S(2)}, u32[]{:S(2)}) %all-to-all-start) | async-done | bytes 294944 | tf_op jit(solution)/shard_map/all_to_all | solution.py:277
  83.3 1.7 %low.1 = (bf16[8,32,512]{2,1,0:T(8,128)(2,1)}, bf16[16,1152]{1,0:T(8,128)(2,1)S(1)}) custom-call(s32[1]{0:T(128)} %bitcast.place_ref, s32[128]{0:T(128)S(1)} %copy-done.8, bf16[8,16,1152]{2,1,0:T(8,128)(2,1)S(1)} %all-to-all-done.offered_ref, bf16[8,128,1024]{2,1,0:T(8,128)(2,1)S(1)} %all-to-all-done.1.columns_ref.arrived_ref.upstream_ref, ...), custom_call_target="tpu_custom_call" | custom-call | tf_op jit(solution)/shard_map/low/pallas_call | solution.py:280
  85.1 7.0 %all-to-all-start.2 = ((bf16[8,32,512]{2,1,0:T(8,128)(2,1)}), bf16[8,32,512]{2,1,0:T(8,128)(2,1)S(1)}, u32[]{:S(2)}, u32[]{:S(2)}) async-start(bf16[8,32,512]{2,1,0:T(8,128)(2,1)} %get-tuple-element.28), calls=%async_computation.2 | async-start | bytes 524288 | tf_op jit(solution)/shard_map/all_to_all | solution.py:290
  92.1 1.6 %copy-done.1 = bf16[1024,1024]{1,0:T(8,128)(2,1)S(1)} copy-done((bf16[1024,1024]{1,0:T(8,128)(2,1)S(1)}, bf16[1024,1024]{1,0:T(8,128)(2,1)}, u32[]{:S(2)}) %copy-start.1) | copy-done | bytes 2097176
  93.7 1.6 %base.1 = (f32[512,1024]{1,0:T(8,128)S(1)}, f32[8,128]{1,0:T(8,128)S(1)}) custom-call(bf16[8,128,1024]{2,1,0:T(8,128)(2,1)S(1)} %all-to-all-done.1.columns_ref.arrived_ref.upstream_ref, bf16[1024,1024]{1,0:T(8,128)(2,1)S(1)} %copy-done.1), custom_call_target="tpu_custom_call" | custom-call | flops 1073741824 | bytes 6291456 | tf_op jit(solution)/shard_map/base/pallas_call | solution.py:292
  95.3 1.4 copy-done.2
  96.7 1.6 %all-to-all-done.2.parts_ref = bf16[8,32,512]{2,1,0:T(8,128)(2,1)S(1)} async-done(((bf16[8,32,512]{2,1,0:T(8,128)(2,1)}), bf16[8,32,512]{2,1,0:T(8,128)(2,1)S(1)}, u32[]{:S(2)}, u32[]{:S(2)}) %all-to-all-start.2) | async-done | bytes 262176 | tf_op jit(solution)/shard_map/all_to_all | solution.py:290
  98.2 0.7 rank.1
  98.9 5.8 %all_to_all.25.parts_ref = f32[4,16,128]{2,1,0:T(8,128)S(1)} all-to-all(f32[4,16,128]{2,1,0:T(8,128)S(1)} %get-tuple-element.32), channel_id=1, replica_groups=mesh['xlo'=2,'far'=8,'near'=4,'core'=2,'tp'=8] {'xlo','core'}, dimensions={0} | all-to-all | bytes 65536 | tf_op jit(solution)/shard_map/all_to_all | solution.py:322
  104.7 0.9 copy-done.6
  105.6 1.3 route.1
  106.9 11.9 %all-to-all-start.4 = ((bf16[32,16,128]{2,1,0:T(8,128)(2,1)}), bf16[32,16,128]{2,1,0:T(8,128)(2,1)S(1)}, u32[]{:S(2)}, u32[]{:S(2)}) async-start(bf16[32,16,128]{2,1,0:T(8,128)(2,1)} %get-tuple-element.50), calls=%async_computation.4 | async-start | bytes 262144 | tf_op jit(solution)/shard_map/all_to_all | solution.py:334
  118.8 4.9 %collective-permute-start.1 = (bf16[512,128]{1,0:T(8,128)(2,1)S(1)}, bf16[512,128]{1,0:T(8,128)(2,1)S(1)}, u32[]{:S(2)}, u32[]{:S(2)}) collective-permute-start(bf16[512,128]{1,0:T(8,128)(2,1)S(1)} %get-tuple-element.42), channel_id=1, source_target_pairs={{0,1},{1,2},{2,3},{3,4},{4,5},{5,6},{6,7},{7,0},{8,9},{9,10},{10,1... | collective-permute-start | bytes 393224 | tf_op jit(solution)/shard_map/ppermute | solution.py:336
  123.7 2.7 %collective-permute-start.2 = (bf16[512,128]{1,0:T(8,128)(2,1)S(1)}, bf16[512,128]{1,0:T(8,128)(2,1)S(1)}, u32[]{:S(2)}, u32[]{:S(2)}) collective-permute-start(bf16[512,128]{1,0:T(8,128)(2,1)S(1)} %get-tuple-element.43), channel_id=1, source_target_pairs={{0,2},{1,3},{2,4},{3,5},{4,6},{5,7},{6,0},{7,1},{8,10},{9,11},{10,... | collective-permute-start | bytes 393224 | tf_op jit(solution)/shard_map/ppermute | solution.py:336
  126.5 3.7 %collective-permute-start.3 = (bf16[512,128]{1,0:T(8,128)(2,1)S(1)}, bf16[512,128]{1,0:T(8,128)(2,1)S(1)}, u32[]{:S(2)}, u32[]{:S(2)}) collective-permute-start(bf16[512,128]{1,0:T(8,128)(2,1)S(1)} %get-tuple-element.44), channel_id=1, source_target_pairs={{0,3},{1,4},{2,5},{3,6},{4,7},{5,0},{6,1},{7,2},{8,11},{9,12},{10,... | collective-permute-start | bytes 393224 | tf_op jit(solution)/shard_map/ppermute | solution.py:336
  130.2 3.7 %collective-permute-start.4 = (bf16[512,128]{1,0:T(8,128)(2,1)S(1)}, bf16[512,128]{1,0:T(8,128)(2,1)S(1)}, u32[]{:S(2)}, u32[]{:S(2)}) collective-permute-start(bf16[512,128]{1,0:T(8,128)(2,1)S(1)} %get-tuple-element.45), channel_id=1, source_target_pairs={{0,4},{1,5},{2,6},{3,7},{4,0},{5,1},{6,2},{7,3},{8,12},{9,13},{10,... | collective-permute-start | bytes 393224 | tf_op jit(solution)/shard_map/ppermute | solution.py:336
  133.9 6.9 %collective-permute-start.5 = (bf16[512,128]{1,0:T(8,128)(2,1)S(1)}, bf16[512,128]{1,0:T(8,128)(2,1)S(1)}, u32[]{:S(2)}, u32[]{:S(2)}) collective-permute-start(bf16[512,128]{1,0:T(8,128)(2,1)S(1)} %get-tuple-element.46), channel_id=1, source_target_pairs={{0,5},{1,6},{2,7},{3,0},{4,1},{5,2},{6,3},{7,4},{8,13},{9,14},{10,... | collective-permute-start | bytes 393224 | tf_op jit(solution)/shard_map/ppermute | solution.py:336
  140.9 1.9 %collective-permute-start.6 = (bf16[512,128]{1,0:T(8,128)(2,1)S(1)}, bf16[512,128]{1,0:T(8,128)(2,1)S(1)}, u32[]{:S(2)}, u32[]{:S(2)}) collective-permute-start(bf16[512,128]{1,0:T(8,128)(2,1)S(1)} %get-tuple-element.47), channel_id=1, source_target_pairs={{0,6},{1,7},{2,0},{3,1},{4,2},{5,3},{6,4},{7,5},{8,14},{9,15},{10,... | collective-permute-start | bytes 393224 | tf_op jit(solution)/shard_map/ppermute | solution.py:336
  142.8 2.9 %collective-permute-start.7 = (bf16[512,128]{1,0:T(8,128)(2,1)}, bf16[512,128]{1,0:T(8,128)(2,1)S(1)}, u32[]{:S(2)}, u32[]{:S(2)}) collective-permute-start(bf16[512,128]{1,0:T(8,128)(2,1)} %copy-done.7), channel_id=1, source_target_pairs={{0,7},{1,0},{2,1},{3,2},{4,3},{5,4},{6,5},{7,6},{8,15},{9,8},{10,9... | collective-permute-start | bytes 393224 | tf_op jit(solution)/shard_map/ppermute | solution.py:336
  145.8 1.6 %copy-done.3 = f32[512,1024]{1,0:T(8,128)S(1)} copy-done((f32[512,1024]{1,0:T(8,128)S(1)}, f32[512,1024]{1,0:T(8,128)}, u32[]{:S(2)}) %copy-start.3) | copy-done | bytes 2097176
  147.4 2.2 %gradient.1 = bf16[512,1024]{1,0:T(8,128)(2,1)} custom-call(f32[512,1024]{1,0:T(8,128)S(1)} %copy-done.3, bf16[32,512]{1,0:T(8,128)(2,1)S(1)} %get-tuple-element.30.both_ref, bf16[16,1152]{1,0:T(8,128)(2,1)S(1)} %get-tuple-element.31.item_ref), custom_call_target="tpu_custom_call" | custom-call | flops 16777216 | bytes 3145728 | tf_op jit(solution)/shard_map/gradient/pallas_call | solution.py:349
  149.6 2.7 %collective-permute-done.7.refs_7_ = bf16[512,128]{1,0:T(8,128)(2,1)S(1)} collective-permute-done((bf16[512,128]{1,0:T(8,128)(2,1)}, bf16[512,128]{1,0:T(8,128)(2,1)S(1)}, u32[]{:S(2)}, u32[]{:S(2)}) %collective-permute-start.7) | collective-permute-done | bytes 131104 | tf_op jit(solution)/shard_map/ppermute | solution.py:336
  152.3 0.9 projected.1
  (29 shorter events, 1.3 us)
Async XLA Ops:
  3.1 7.6 %copy-start.10 = (bf16[1,1024,16]{1,2,0:T(8,128)(2,1)S(1)}, bf16[1,1024,16]{1,2,0:T(8,128)(2,1)}, u32[]{:S(2)}) copy-start(bf16[1,1024,16]{1,2,0:T(8,128)(2,1)} %param.9) | copy-start | bytes 98308
  3.1 7.6 %copy-start.11 = (bf16[1,16,128]{2,1,0:T(8,128)(2,1)S(1)}, bf16[1,16,128]{2,1,0:T(8,128)(2,1)}, u32[]{:S(2)}) copy-start(bf16[1,16,128]{2,1,0:T(8,128)(2,1)} %param.10) | copy-start | bytes 12292
  3.1 65.0 %copy-start.8 = (s32[128]{0:T(128)S(1)}, s32[128]{0:T(128)}, u32[]{:S(2)}) copy-start(s32[128]{0:T(128)} %tenants_ref.5) | copy-start | bytes 1540
  3.1 66.3 %all-to-all-start.1 = ((bf16[8,128,1024]{2,1,0:T(8,128)(2,1)}), bf16[8,128,1024]{2,1,0:T(8,128)(2,1)S(1)}, u32[]{:S(2)}, u32[]{:S(2)}) async-start(bf16[8,128,1024]{2,1,0:T(8,128)(2,1)} %slab.1), calls=%async_computation.1 | async-start | bytes 4194304 | tf_op jit(solution)/shard_map/all_to_all | solution.py:246
  64.6 3.5 %collective-permute-start = (bf16[8,16,1152]{2,1,0:T(8,128)(2,1)S(1)}, bf16[8,16,1152]{2,1,0:T(8,128)(2,1)S(1)}, u32[]{:S(2)}, u32[]{:S(2)}) collective-permute-start(bf16[8,16,1152]{2,1,0:T(8,128)(2,1)S(1)} %bitcast.6), channel_id=1, source_target_pairs={{0,8},{8,0},{1,9},{9,1},{2,10},{10,2},{3,11},{11,3},{4,12},{12,4},... | collective-permute-start | bytes 884744 | tf_op jit(solution)/shard_map/ppermute | solution.py:250
  69.4 13.9 %all-to-all-start = ((bf16[8,16,1152]{2,1,0:T(8,128)(2,1)}), bf16[8,16,1152]{2,1,0:T(8,128)(2,1)S(1)}, u32[]{:S(2)}, u32[]{:S(2)}) async-start(bf16[8,16,1152]{2,1,0:T(8,128)(2,1)} %table.1), calls=%async_computation | async-start | bytes 589824 | tf_op jit(solution)/shard_map/all_to_all | solution.py:277
  73.7 1.6 %copy-start = (bf16[1024,1024]{1,0:T(8,128)(2,1)S(1)}, bf16[1024,1024]{1,0:T(8,128)(2,1)}, u32[]{:S(2)}) copy-start(bf16[1024,1024]{1,0:T(8,128)(2,1)} %weight_ref.3) | copy-start | bytes 6291460
  75.3 8.0 %copy-start.4 = (bf16[512,128]{1,0:T(8,128)(2,1)S(1)}, bf16[512,128]{1,0:T(8,128)(2,1)}, u32[]{:S(2)}) copy-start(bf16[512,128]{1,0:T(8,128)(2,1)} %upstream_ref.5) | copy-start | bytes 393220
  77.6 0.7 copy-start.5
  85.1 13.2 %all-to-all-start.2 = ((bf16[8,32,512]{2,1,0:T(8,128)(2,1)}), bf16[8,32,512]{2,1,0:T(8,128)(2,1)S(1)}, u32[]{:S(2)}, u32[]{:S(2)}) async-start(bf16[8,32,512]{2,1,0:T(8,128)(2,1)} %get-tuple-element.28), calls=%async_computation.2 | async-start | bytes 524288 | tf_op jit(solution)/shard_map/all_to_all | solution.py:290
  92.1 1.6 %copy-start.1 = (bf16[1024,1024]{1,0:T(8,128)(2,1)S(1)}, bf16[1024,1024]{1,0:T(8,128)(2,1)}, u32[]{:S(2)}) copy-start(bf16[1024,1024]{1,0:T(8,128)(2,1)} %weight_ref.3) | copy-start | bytes 6291460
  93.7 4.5 %copy-start.9 = (s32[128]{0:T(128)S(1)}, s32[128]{0:T(128)}, u32[]{:S(2)}) copy-start(s32[128]{0:T(128)} %lengths_ref.1) | copy-start | bytes 1540
  95.3 1.4 copy-start.2
  104.7 0.9 copy-start.6
  106.9 11.9 %copy-start.7 = (bf16[512,128]{1,0:T(8,128)(2,1)}, bf16[512,128]{1,0:T(8,128)(2,1)S(1)}, u32[]{:S(2)}) copy-start(bf16[512,128]{1,0:T(8,128)(2,1)S(1)} %get-tuple-element.48) | copy-start | bytes 393220
  106.9 46.3 %all-to-all-start.4 = ((bf16[32,16,128]{2,1,0:T(8,128)(2,1)}), bf16[32,16,128]{2,1,0:T(8,128)(2,1)S(1)}, u32[]{:S(2)}, u32[]{:S(2)}) async-start(bf16[32,16,128]{2,1,0:T(8,128)(2,1)} %get-tuple-element.50), calls=%async_computation.4 | async-start | bytes 262144 | tf_op jit(solution)/shard_map/all_to_all | solution.py:334
  118.8 22.0 %collective-permute-start.1 = (bf16[512,128]{1,0:T(8,128)(2,1)S(1)}, bf16[512,128]{1,0:T(8,128)(2,1)S(1)}, u32[]{:S(2)}, u32[]{:S(2)}) collective-permute-start(bf16[512,128]{1,0:T(8,128)(2,1)S(1)} %get-tuple-element.42), channel_id=1, source_target_pairs={{0,1},{1,2},{2,3},{3,4},{4,5},{5,6},{6,7},{7,0},{8,9},{9,10},{10,1... | collective-permute-start | bytes 393224 | tf_op jit(solution)/shard_map/ppermute | solution.py:336
  123.7 19.1 %collective-permute-start.2 = (bf16[512,128]{1,0:T(8,128)(2,1)S(1)}, bf16[512,128]{1,0:T(8,128)(2,1)S(1)}, u32[]{:S(2)}, u32[]{:S(2)}) collective-permute-start(bf16[512,128]{1,0:T(8,128)(2,1)S(1)} %get-tuple-element.43), channel_id=1, source_target_pairs={{0,2},{1,3},{2,4},{3,5},{4,6},{5,7},{6,0},{7,1},{8,10},{9,11},{10,... | collective-permute-start | bytes 393224 | tf_op jit(solution)/shard_map/ppermute | solution.py:336
  126.5 23.1 %collective-permute-start.3 = (bf16[512,128]{1,0:T(8,128)(2,1)S(1)}, bf16[512,128]{1,0:T(8,128)(2,1)S(1)}, u32[]{:S(2)}, u32[]{:S(2)}) collective-permute-start(bf16[512,128]{1,0:T(8,128)(2,1)S(1)} %get-tuple-element.44), channel_id=1, source_target_pairs={{0,3},{1,4},{2,5},{3,6},{4,7},{5,0},{6,1},{7,2},{8,11},{9,12},{10,... | collective-permute-start | bytes 393224 | tf_op jit(solution)/shard_map/ppermute | solution.py:336
  130.2 19.4 %collective-permute-start.4 = (bf16[512,128]{1,0:T(8,128)(2,1)S(1)}, bf16[512,128]{1,0:T(8,128)(2,1)S(1)}, u32[]{:S(2)}, u32[]{:S(2)}) collective-permute-start(bf16[512,128]{1,0:T(8,128)(2,1)S(1)} %get-tuple-element.45), channel_id=1, source_target_pairs={{0,4},{1,5},{2,6},{3,7},{4,0},{5,1},{6,2},{7,3},{8,12},{9,13},{10,... | collective-permute-start | bytes 393224 | tf_op jit(solution)/shard_map/ppermute | solution.py:336
  133.9 15.6 %collective-permute-start.5 = (bf16[512,128]{1,0:T(8,128)(2,1)S(1)}, bf16[512,128]{1,0:T(8,128)(2,1)S(1)}, u32[]{:S(2)}, u32[]{:S(2)}) collective-permute-start(bf16[512,128]{1,0:T(8,128)(2,1)S(1)} %get-tuple-element.46), channel_id=1, source_target_pairs={{0,5},{1,6},{2,7},{3,0},{4,1},{5,2},{6,3},{7,4},{8,13},{9,14},{10,... | collective-permute-start | bytes 393224 | tf_op jit(solution)/shard_map/ppermute | solution.py:336
  140.9 8.7 %collective-permute-start.6 = (bf16[512,128]{1,0:T(8,128)(2,1)S(1)}, bf16[512,128]{1,0:T(8,128)(2,1)S(1)}, u32[]{:S(2)}, u32[]{:S(2)}) collective-permute-start(bf16[512,128]{1,0:T(8,128)(2,1)S(1)} %get-tuple-element.47), channel_id=1, source_target_pairs={{0,6},{1,7},{2,0},{3,1},{4,2},{5,3},{6,4},{7,5},{8,14},{9,15},{10,... | collective-permute-start | bytes 393224 | tf_op jit(solution)/shard_map/ppermute | solution.py:336
  142.8 9.5 %collective-permute-start.7 = (bf16[512,128]{1,0:T(8,128)(2,1)}, bf16[512,128]{1,0:T(8,128)(2,1)S(1)}, u32[]{:S(2)}, u32[]{:S(2)}) collective-permute-start(bf16[512,128]{1,0:T(8,128)(2,1)} %copy-done.7), channel_id=1, source_target_pairs={{0,7},{1,0},{2,1},{3,2},{4,3},{5,4},{6,5},{7,6},{8,15},{9,8},{10,9... | collective-permute-start | bytes 393224 | tf_op jit(solution)/shard_map/ppermute | solution.py:336
  145.8 1.6 %copy-start.3 = (f32[512,1024]{1,0:T(8,128)S(1)}, f32[512,1024]{1,0:T(8,128)}, u32[]{:S(2)}) copy-start(f32[512,1024]{1,0:T(8,128)} %copy-done.2) | copy-start | bytes 6291460

commit v5 on v4

--- a/solution.py
+++ b/solution.py
@@ -111,6 +111,19 @@
         pltpu.make_async_copy(held_ref.at[0], out_ref.at[slot], sems.at[slot]).wait()
 
 
+def unfold(slabs_ref, features):
+    sources, _, lanes = slabs_ref.shape
+    return jnp.concatenate(
+        [
+            jnp.concatenate(
+                [slabs_ref[s, :, at : at + features] for s in range(sources)], axis=1
+            )
+            for at in range(0, lanes, features)
+        ],
+        axis=0,
+    )
+
+
 def value_kernel(columns_ref, weight_ref, *refs):
     outs, mark_ref, held_ref = refs[:-2], refs[-2], refs[-1]
     mark_ref[...] = jnp.zeros_like(mark_ref)
@@ -123,17 +136,26 @@
         out_ref[...] = held_ref[:, pl.ds(at, features)]
 
 
+def base_kernel(upstream_ref, weight_ref, out_ref, mark_ref):
+    mark_ref[...] = jnp.zeros_like(mark_ref)
+    features = weight_ref.shape[1] // upstream_ref.shape[0]
+    out_ref[...] = dot(unfold(upstream_ref, features), weight_ref[...], 1, 1)
+
+
 def low_kernel(
     sizes,
+    parts,
     place_ref,
     tenants_ref,
+    lengths_ref,
     offered_ref,
     arrived_ref,
     upstream_ref,
     *refs,
 ):
-    out_ref, item_ref, sem = refs[-3:]
-    xlo, _, near, _ = split_place(tenants_ref[place_ref[0]], sizes)
+    outs, share_ref, item_ref, sem = refs[-3 - parts : -3], *refs[-3:]
+    place = place_ref[0]
+    xlo, _, near, _ = split_place(tenants_ref[place], sizes)
     copy = pltpu.make_async_copy(offered_ref.at[xlo * sizes[2] + near], item_ref, sem)
     copy.start()
     copy.wait()
@@ -142,41 +164,43 @@
     low = dot(item_ref[:, :width], columns, 1, 1)
     back = dot(item_ref[:, width:], upstream_ref[...], 1, 1)
     both = jnp.concatenate([low, back], axis=0).astype(jnp.bfloat16)
-    for s in range(out_ref.shape[0]):
-        out_ref[s] = both
-
-
-def rank_kernel(place_ref, lengths_ref, parts_ref, upstream_ref, *refs):
-    both_ref, out_ref = refs[-2:]
-    length = lengths_ref[place_ref[0]]
-    total = parts_ref[0].astype(jnp.float32)
-    for s in range(1, parts_ref.shape[0]):
-        total = total + parts_ref[s].astype(jnp.float32)
-    ranks = both_ref.shape[0]
-    total = total.astype(jnp.bfloat16).astype(jnp.float32)
-    live = lax.broadcasted_iota(jnp.int32, total.shape, 1) < length
-    both = jnp.where(live, adapter_scale * total, 0.0).astype(jnp.bfloat16)
-    both_ref[...] = both
-    mine = dot(both[: ranks // 2], upstream_ref[...], 1, 0)
-    for member in range(out_ref.shape[0]):
-        out_ref[member] = mine
-
-
-def route_kernel(sizes, place_ref, tenants_ref, parts_ref, *refs):
-    out_ref, total_ref = refs[-2:]
+    ranks, lanes = both.shape[0], upstream_ref.shape[1]
+    for out_ref in outs:
+        for g in range(both.shape[1] // lanes):
+            out_ref[g * ranks : (g + 1) * ranks, :] = both[:, g * lanes : (g + 1) * lanes]
+    live = lax.broadcasted_iota(jnp.int32, low.shape, 1) < lengths_ref[place]
+    low = jnp.where(live, adapter_scale * low, 0.0).astype(jnp.bfloat16)
+    share = dot(low, unfold(arrived_ref.at[:, rows:, :], lanes), 1, 0)
+    for slot in range(share_ref.shape[0]):
+        s = slot % parts
+        share_ref[slot] = share[:, s * lanes : (s + 1) * lanes]
+
+
+def route_kernel(sizes, parts, place_ref, tenants_ref, shares_ref, *refs):
+    out_ref = refs[-1]
     xlo_n, far_n, near_n, core_n = sizes
     my_xlo, far, near, my_core = split_place(place_ref[0], sizes)
-    total_ref[...] = jnp.zeros_like(total_ref)
+    sums, slots, mine = [], [], []
     for xlo in range(xlo_n):
         for core in range(core_n):
             block = ((xlo * far_n + far) * near_n + near) * core_n + core
             to_xlo, to_far, to_near, to_core = split_place(tenants_ref[block], sizes)
-
-            @pl.when((to_xlo == my_xlo) & (to_core == my_core))
-            def _():
-                total_ref[to_far * near_n + to_near] += parts_ref[xlo * core_n + core]
-
-    out_ref[...] = total_ref[...].astype(out_ref.dtype)
+            first = (xlo * core_n + core) * parts
+            total = shares_ref[first]
+            for s in range(1, parts):
+                total = total + shares_ref[first + s]
+            sums.append(total)
+            slots.append(to_far * near_n + to_near)
+            mine.append((to_xlo == my_xlo) & (to_core == my_core))
+    out_ref[...] = jnp.zeros_like(out_ref)
+    for slot, wanted in zip(slots, mine):
+        total = jnp.zeros_like(sums[0])
+        for other, other_slot, other_wanted in zip(sums, slots, mine):
+            total = total + jnp.where(other_wanted & (other_slot == slot), other, 0.0)
+
+        @pl.when(wanted)
+        def _():
+            out_ref[slot] = total.astype(out_ref.dtype)
 
 
 def sum_kernel(parts_ref, out_ref):
@@ -186,35 +210,24 @@
     out_ref[0] = total
 
 
-def projected_kernel(width, both_ref, item_ref, *refs):
-    rank, out_ref = item_ref.shape[0], refs[-1]
-    total = refs[0][...].astype(jnp.float32)
-    for part_ref in refs[1:-1]:
-        total = total + part_ref[...].astype(jnp.float32)
-    term = dot(both_ref[:rank], item_ref[:, width:], 0, 0)
-    out_ref[...] = (total + term).astype(jnp.bfloat16)
-
-
-def base_kernel(upstream_ref, weight_ref, out_ref, mark_ref):
-    mark_ref[...] = jnp.zeros_like(mark_ref)
-    sources, _, lanes = upstream_ref.shape
-    features = weight_ref.shape[1] // sources
-    rows = jnp.concatenate(
-        [
-            jnp.concatenate(
-                [upstream_ref[s, :, at : at + features] for s in range(sources)], axis=1
-            )
-            for at in range(0, lanes, features)
-        ],
-        axis=0,
-    )
-    out_ref[...] = dot(rows, weight_ref[...], 1, 1)
-
-
-def gradient_kernel(base_ref, both_ref, item_ref, out_ref):
-    rank, width = item_ref.shape[0], out_ref.shape[1]
-    term = dot(both_ref[rank:], item_ref[:, :width], 0, 0)
-    out_ref[...] = (base_ref[...] + term).astype(jnp.bfloat16)
+def finish_kernel(parts, place_ref, lengths_ref, base_ref, item_ref, *refs):
+    values, ranks = refs[:parts], refs[parts : 2 * parts]
+    projected_ref, gradient_ref = refs[2 * parts :]
+    total = ranks[0][...].astype(jnp.float32)
+    for ref in ranks[1:]:
+        total = total + ref[...].astype(jnp.float32)
+    total = total.astype(jnp.bfloat16).astype(jnp.float32)
+    token = lax.broadcasted_iota(jnp.int32, total.shape, 1) + pl.program_id(0) * total.shape[1]
+    live = token < lengths_ref[place_ref[0]]
+    both = jnp.where(live, adapter_scale * total, 0.0).astype(jnp.bfloat16)
+    rank, width = item_ref.shape[0], gradient_ref.shape[1]
+    term = dot(both[rank:], item_ref[:, :width], 0, 0)
+    gradient_ref[...] = (base_ref[...] + term).astype(jnp.bfloat16)
+    value = values[0][...].astype(jnp.float32)
+    for ref in values[1:]:
+        value = value + ref[...].astype(jnp.float32)
+    term = dot(both[:rank], item_ref[:, width:], 0, 0)
+    projected_ref[...] = (value + term).astype(jnp.bfloat16)
 
 
 def on_device(
@@ -230,6 +243,9 @@
     values = base_weight.shape[1]
     row_step, base_step = 128, 256
     mark = struct((8, 128), f32)
+    rank_rows = 2 * rank * block // features
+    parcel = struct((block + rank_rows, features), bf16)
+    column = xlo_n * core_n * parts
     slabs = pl.pallas_call(
         functools.partial(slab_kernel, parts),
         out_shape=struct((parts, 2 * rows, width), bf16),
@@ -249,10 +265,10 @@
     held = lax.all_gather(own, "far", axis=0, tiled=False)
     other = lax.ppermute(held, "core", [(c, (c + 1) % core_n) for c in range(core_n)])
 
-    *value_parts, value_mark = pl.pallas_call(
+    *parcels, value_mark = pl.pallas_call(
         value_kernel,
         grid=(block // row_step,),
-        out_shape=[struct((block, features), bf16)] * parts + [mark],
+        out_shape=[parcel] * parts + [mark],
         in_specs=[
             pl.BlockSpec((row_step // rows, rows, width), lambda i: (i, 0, 0)),
             pl.BlockSpec((width, values), lambda i: (0, 0)),
@@ -264,30 +280,6 @@
         cost_estimate=cost(2 * block * width * values, 4 << 20),
         name="value",
     )(arrived, base_weight)
-
-    table = pl.pallas_call(
-        functools.partial(table_kernel, sizes),
-        out_shape=struct((xlo_n * near_n,) + own.shape, bf16),
-        in_specs=[SMEM, SMEM, ANY, ANY],
-        out_specs=ANY,
-        scratch_shapes=[pltpu.SemaphoreType.DMA((xlo_n * near_n,))],
-        compiler_params=params(),
-        name="table",
-    )(place, tenants, held, other)
-    offered = lax.all_to_all(table, ("xlo", "near"), 0, 0, tiled=True)
-
-    parcel = [struct((block, features), bf16)] * parts
-    sent, item = pl.pallas_call(
-        functools.partial(low_kernel, sizes),
-        grid=(1,),
-        out_shape=(struct((parts, 2 * rank, block), bf16), struct(own.shape, bf16)),
-        in_specs=[SMEM, SMEM, ANY, VMEM, VMEM, ANY],
-        out_specs=(whole((parts, 2 * rank, block)), whole(own.shape)),
-        scratch_shapes=[pltpu.SemaphoreType.DMA],
-        compiler_params=params(),
-        name="low",
-    )(place, tenants, offered, arrived, upstream, value_mark)
-    back = lax.all_to_all(sent, "tp", 0, 0, tiled=True)
 
     base, base_mark = pl.pallas_call(
         base_kernel,
@@ -304,38 +296,53 @@
         cost_estimate=cost(2 * block * width * values, 6 << 20),
         name="base",
     )(arrived, base_weight)
-    both, mine = pl.pallas_call(
-        rank_kernel,
+
+    table = pl.pallas_call(
+        functools.partial(table_kernel, sizes),
+        out_shape=struct((xlo_n * near_n,) + own.shape, bf16),
+        in_specs=[SMEM, SMEM, ANY, ANY],
+        out_specs=ANY,
+        scratch_shapes=[pltpu.SemaphoreType.DMA((xlo_n * near_n,))],
+        compiler_params=params(),
+        name="table",
+    )(place, tenants, held, other)
+    offered = lax.all_to_all(table, ("xlo", "near"), 0, 0, tiled=True)
+
+    *parcels, shares, item = pl.pallas_call(
+        functools.partial(low_kernel, sizes, parts),
         grid=(1,),
-        out_shape=(
-            struct((2 * rank, block), bf16),
-            struct((xlo_n * core_n, rank, features), f32),
-        ),
-        in_specs=[SMEM, SMEM, whole((parts, 2 * rank, block)), VMEM, ANY],
-        out_specs=(
-            whole((2 * rank, block)),
-            whole((xlo_n * core_n, rank, features)),
-        ),
-        compiler_params=params(),
-        name="rank",
-    )(place, lengths, back, upstream, base_mark)
-    near_parts = lax.all_to_all(mine, ("xlo", "core"), 0, 0, tiled=True)
-    *value_parts, routed = pl.pallas_call(
-        functools.partial(route_kernel, sizes),
+        out_shape=[parcel] * parts
+        + [struct((column, rank, features), f32), struct(own.shape, bf16)],
+        in_specs=[SMEM, SMEM, SMEM, ANY, VMEM, VMEM, ANY, ANY] + [ANY] * parts,
+        out_specs=[pl.BlockSpec((rank_rows, features), lambda i: (block // rank_rows, 0))]
+        * parts
+        + [whole((column, rank, features)), whole(own.shape)],
+        scratch_shapes=[pltpu.SemaphoreType.DMA],
+        input_output_aliases={8 + k: k for k in range(parts)},
+        compiler_params=params(12),
+        name="low",
+    )(place, tenants, lengths, offered, arrived, upstream, value_mark, base_mark, *parcels)
+    arrived_shares = lax.all_to_all(shares, ("xlo", "core", "tp"), 0, 0, tiled=True)
+
+    def leave(k):
+        return lax.ppermute(parcels[k], "tp", [(d, (d + k) % parts) for d in range(parts)])
+
+    early = 1
+    for k in range(1, 1 + early):
+        parcels[k] = leave(k)
+    *parcels, routed = pl.pallas_call(
+        functools.partial(route_kernel, sizes, parts),
         grid=(1,),
-        out_shape=parcel + [struct((far_n * near_n, rank, features), bf16)],
-        in_specs=[SMEM, SMEM, whole((xlo_n * core_n, rank, features))] + [ANY] * parts,
+        out_shape=[parcel] * parts + [struct((far_n * near_n, rank, features), bf16)],
+        in_specs=[SMEM, SMEM, whole((column, rank, features))] + [ANY] * parts,
         out_specs=[ANY] * parts + [whole((far_n * near_n, rank, features))],
-        scratch_shapes=[pltpu.VMEM((far_n * near_n, rank, features), f32)],
         input_output_aliases={3 + k: k for k in range(parts)},
         compiler_params=params(),
         name="route",
-    )(place, tenants, near_parts, *value_parts)
+    )(place, tenants, arrived_shares, *parcels)
     far_parts = lax.all_to_all(routed, ("far", "near"), 0, 0, tiled=True)
-    sums = [value_parts[0]] + [
-        lax.ppermute(value_parts[k], "tp", [(d, (d + k) % parts) for d in range(parts)])
-        for k in range(1, parts)
-    ]
+    for k in range(1 + early, parts):
+        parcels[k] = leave(k)
     up_grad = pl.pallas_call(
         sum_kernel,
         grid=(1,),
@@ -346,30 +353,27 @@
         name="total",
     )(far_parts)
 
-    gradient = pl.pallas_call(
-        gradient_kernel,
-        grid=(block // row_step,),
-        out_shape=struct((block, width), bf16),
+    group = 2 * rank
+    projected, gradient = pl.pallas_call(
+        functools.partial(finish_kernel, parts),
+        grid=(block // features,),
+        out_shape=(struct((block, features), bf16), struct((block, width), bf16)),
         in_specs=[
-            pl.BlockSpec((row_step, width), lambda i: (i, 0)),
-            pl.BlockSpec((2 * rank, row_step), lambda i: (0, i)),
+            SMEM,
+            SMEM,
+            pl.BlockSpec((features, width), lambda i: (i, 0)),
             pl.BlockSpec(own.shape, lambda i: (0, 0)),
-        ],
-        out_specs=pl.BlockSpec((row_step, width), lambda i: (i, 0)),
+        ]
+        + [pl.BlockSpec((features, features), lambda i: (i, 0))] * parts
+        + [pl.BlockSpec((group, features), lambda i: (block // group + i, 0))] * parts,
+        out_specs=(
+            pl.BlockSpec((features, features), lambda i: (i, 0)),
+            pl.BlockSpec((features, width), lambda i: (i, 0)),
+        ),
         compiler_params=params(),
-        cost_estimate=cost(2 * block * width * rank, 3 << 20),
-        name="gradient",
-    )(base, both, item)
-    projected = pl.pallas_call(
-        functools.partial(projected_kernel, width),
-        grid=(1,),
-        out_shape=struct((block, features), bf16),
-        in_specs=[whole((2 * rank, block)), whole(own.shape)]
-        + [whole((block, features))] * parts,
-        out_specs=whole((block, features)),
-        compiler_params=params(),
-        name="projected",
-    )(both, item, *sums)
+        cost_estimate=cost(2 * block * width * rank, 5 << 20),
+        name="finish",
+    )(place, lengths, base, item, *parcels, *parcels)
     return projected, gradient, up_grad
 
 

time: 156 us -> 158 us (1.013)
  blocking collectives: 59.7 us -> 53.9 us
  starting transfers between devices: 59.6 us -> 63.3 us
  local copies, waits for them, and re-layouts: 7.7 us -> 11.1 us
  waiting for transfers between devices: 10.9 us -> 13.6 us
  Pallas kernels: 15 us -> 13 us
    ppermute x7, waiting for transfers between devices: 2.74 us -> 10 us  [leave(): lax.ppermute(parcels[k], 'tp', [(d, (d + k) % parts) for d in range(parts)])]
    all_to_all x1 -> x0, blocking collectives: 5.78 us -> none  [on_device(): near_parts = lax.all_to_all(mine, ('xlo', 'core'), 0, 0, tiled=True)]
    unnamed x24 -> x38, local copies, waits for them, and re-layouts: 7.7 us -> 11.1 us
    all_to_all x1, waiting for transfers between devices: 5.08 us -> 2.1 us  [on_device(): offered = lax.all_to_all(table, ('xlo', 'near'), 0, 0, tiled=True)]
    ppermute x7, starting transfers between devices: 26.9 us -> 29.6 us  [leave(): lax.ppermute(parcels[k], 'tp', [(d, (d + k) % parts) for d in range(parts)])]
    pallas_call x6 -> x4, Pallas kernels: 9.05 us -> 6.93 us  [the longest x1 2.83 us: on_device(): pl.pallas_call(functools.partial(finish_kernel, parts), grid=(block // fe...]
where the time goes in v5:
time: 158 us; the launch traced here: 156 us
  starting transfers between devices  63.3 us (40%)
  blocking collectives  53.9 us (34%)
  waiting for transfers between devices  13.6 us (9%)
  Pallas kernels  13 us (8%)
  local copies, waits for them, and re-layouts  11.1 us (7%)
    all_gather x1, blocking collectives, on_device(): held = lax.all_gather(own, 'far', axis=0, tiled=False)  53.9 us
    ppermute x7, starting transfers between devices, leave(): lax.ppermute(parcels[k], 'tp', [(d, (d + k) % parts) for d in range(parts)])  29.6 us
    all_to_all x1, starting transfers between devices, on_device(): far_parts = lax.all_to_all(routed, ('far', 'near'), 0, 0, tiled=True)  11.9 us
    unnamed x38, local copies, waits for them, and re-layouts  11.1 us
    ppermute x7, waiting for transfers between devices, leave(): lax.ppermute(parcels[k], 'tp', [(d, (d + k) % parts) for d in range(parts)])  10 us
    all_to_all x1, starting transfers between devices, on_device(): lax.all_to_all(shares, ('xlo', 'core', 'tp'), 0, 0, tiled=True)  7.96 us
    all_to_all x1, starting transfers between devices, on_device(): arrived = lax.all_to_all(slabs, 'tp', 0, 0, tiled=True)  7.58 us
    all_to_all x1, starting transfers between devices, on_device(): offered = lax.all_to_all(table, ('xlo', 'near'), 0, 0, tiled=True)  4.28 us
  transfers between devices with their start and end apart: 12, of which 4 were waited for; matrix products, arithmetic and copies ran while one was open for 0% of the time, Pallas kernels for 5%

profile of v5, /device:TPU:6, one launch (start us, length us, event | category | flops | bytes accessed | tf_op | source)
XLA Modules:
  0.0 155.9 jit_solution(8760857857316135683)
XLA Ops:
  0.6 2.5 %slab.1 = bf16[8,128,1024]{2,1,0:T(8,128)(2,1)} custom-call(bf16[64,8192]{1,0:T(8,128)(2,1)} %tokens_ref.1, bf16[512,128]{1,0:T(8,128)(2,1)} %upstream_ref.3), custom_call_target="tpu_custom_call" | custom-call | tf_op jit(solution)/shard_map/slab/pallas_call | solution.py:249
  3.2 7.6 %all-to-all-start = ((bf16[8,128,1024]{2,1,0:T(8,128)(2,1)}), bf16[8,128,1024]{2,1,0:T(8,128)(2,1)S(1)}, u32[]{:S(2)}, u32[]{:S(2)}) async-start(bf16[8,128,1024]{2,1,0:T(8,128)(2,1)} %slab.1), calls=%async_computation | async-start | bytes 4194304 | tf_op jit(solution)/shard_map/all_to_all | solution.py:262
  10.8 53.9 %all-gather = bf16[128,1152]{1,0:T(8,128)(2,1)S(1)} all-gather(bf16[16,1152]{1,0:T(8,128)(2,1)S(1)} %pad_maximum_fusion), channel_id=2, replica_groups=mesh['xlo'=2,'far'=8,'near'=4,'core'=2,'tp'=8] {'far'}, dimensions={0}, use_global_device_ids=true | all-gather | bytes 331776 | tf_op jit(solution)/shard_map/all_gather | solution.py:265
  64.7 1.9 %collective-permute-start = (bf16[8,16,1152]{2,1,0:T(8,128)(2,1)S(1)}, bf16[8,16,1152]{2,1,0:T(8,128)(2,1)S(1)}, u32[]{:S(2)}, u32[]{:S(2)}) collective-permute-start(bf16[8,16,1152]{2,1,0:T(8,128)(2,1)S(1)} %bitcast.6), channel_id=1, source_target_pairs={{0,8},{8,0},{1,9},{9,1},{2,10},{10,2},{3,11},{11,3},{4,12},{12,4},... | collective-permute-start | bytes 884744 | tf_op jit(solution)/shard_map/ppermute | solution.py:266
  66.6 1.5 collective-permute-done.other_ref
  68.2 1.3 table.1
  69.5 4.3 %all-to-all-start.1 = ((bf16[8,16,1152]{2,1,0:T(8,128)(2,1)}), bf16[8,16,1152]{2,1,0:T(8,128)(2,1)S(1)}, u32[]{:S(2)}, u32[]{:S(2)}) async-start(bf16[8,16,1152]{2,1,0:T(8,128)(2,1)} %table.1), calls=%async_computation.1 | async-start | bytes 589824 | tf_op jit(solution)/shard_map/all_to_all | solution.py:309
  73.8 1.6 %copy-done = bf16[1024,1024]{1,0:T(8,128)(2,1)S(1)} copy-done((bf16[1024,1024]{1,0:T(8,128)(2,1)S(1)}, bf16[1024,1024]{1,0:T(8,128)(2,1)}, u32[]{:S(2)}) %copy-start) | copy-done | bytes 2097176
  75.4 1.6 %base.1 = (f32[512,1024]{1,0:T(8,128)S(1)}, f32[8,128]{1,0:T(8,128)S(1)}) custom-call(bf16[8,128,1024]{2,1,0:T(8,128)(2,1)S(1)} %all-to-all-done.upstream_ref.columns_ref.arrived_ref, bf16[1024,1024]{1,0:T(8,128)(2,1)S(1)} %copy-done), custom_call_target="tpu_custom_call" | custom-call | flops 1073741824 | bytes 6291456 | tf_op jit(solution)/shard_map/base/pallas_call | solution.py:284
  77.0 1.4 copy-done.2
  78.4 2.2 %value.1 = (bf16[640,128]{1,0:T(8,128)(2,1)S(1)}, bf16[640,128]{1,0:T(8,128)(2,1)S(1)}, bf16[640,128]{1,0:T(8,128)(2,1)S(1)}, bf16[640,128]{1,0:T(8,128)(2,1)S(1...) custom-call(bf16[8,128,1024]{2,1,0:T(8,128)(2,1)S(1)} %all-to-all-do, ...), custom_call_target="tpu_custom_call" | custom-call | flops 1073741824 | bytes 4194304 | tf_op jit(solution)/shard_map/value/pallas_call | solution.py:268
  81.3 2.1 %all-to-all-done.1.offered_ref = bf16[8,16,1152]{2,1,0:T(8,128)(2,1)S(1)} async-done(((bf16[8,16,1152]{2,1,0:T(8,128)(2,1)}), bf16[8,16,1152]{2,1,0:T(8,128)(2,1)S(1)}, u32[]{:S(2)}, u32[]{:S(2)}) %all-to-all-start.1) | async-done | bytes 294944 | tf_op jit(solution)/shard_map/all_to_all | solution.py:309
  83.4 0.9 copy-done.7
  84.3 0.9 copy-done.10
  85.2 1.2 low.1
  86.5 0.7 copy-done.4
  87.1 0.7 copy-done.8
  87.8 0.7 copy-done.11
  89.1 8.0 %all-to-all-start.2 = ((f32[32,16,128]{2,1,0:T(8,128)}), f32[32,16,128]{2,1,0:T(8,128)S(1)}, u32[]{:S(2)}, u32[]{:S(2)}) async-start(f32[32,16,128]{2,1,0:T(8,128)} %copy-done.8), calls=%async_computation.2 | async-start | bytes 524288 | tf_op jit(solution)/shard_map/all_to_all | solution.py:325
  97.1 4.3 %collective-permute-start.1 = (bf16[640,128]{1,0:T(8,128)(2,1)}, bf16[640,128]{1,0:T(8,128)(2,1)S(1)}, u32[]{:S(2)}, u32[]{:S(2)}) collective-permute-start(bf16[640,128]{1,0:T(8,128)(2,1)} %copy-done.11), channel_id=1, source_target_pairs={{0,1},{1,2},{2,3},{3,4},{4,5},{5,6},{6,7},{7,0},{8,9},{9,10},{10,1... | collective-permute-start | bytes 491528 | tf_op jit(solution)/shard_map/ppermute | solution.py:328
  101.4 5.6 %collective-permute-done.1.refs_1_ = bf16[640,128]{1,0:T(8,128)(2,1)S(1)} collective-permute-done((bf16[640,128]{1,0:T(8,128)(2,1)}, bf16[640,128]{1,0:T(8,128)(2,1)S(1)}, u32[]{:S(2)}, u32[]{:S(2)}) %collective-permute-start.1) | collective-permute-done | bytes 163872 | tf_op jit(solution)/shard_map/ppermute | solution.py:328
  107.0 0.9 copy-done.5
  109.9 11.9 %all-to-all-start.3 = ((bf16[32,16,128]{2,1,0:T(8,128)(2,1)}), bf16[32,16,128]{2,1,0:T(8,128)(2,1)S(1)}, u32[]{:S(2)}, u32[]{:S(2)}) async-start(bf16[32,16,128]{2,1,0:T(8,128)(2,1)} %copy-done.12), calls=%async_computation.3 | async-start | bytes 262144 | tf_op jit(solution)/shard_map/all_to_all | solution.py:343
  121.8 3.4 %collective-permute-start.2 = (bf16[640,128]{1,0:T(8,128)(2,1)S(1)}, bf16[640,128]{1,0:T(8,128)(2,1)S(1)}, u32[]{:S(2)}, u32[]{:S(2)}) collective-permute-start(bf16[640,128]{1,0:T(8,128)(2,1)S(1)} %get-tuple-element.58), channel_id=1, source_target_pairs={{0,2},{1,3},{2,4},{3,5},{4,6},{5,7},{6,0},{7,1},{8,10},{9,11},{10,... | collective-permute-start | bytes 491528 | tf_op jit(solution)/shard_map/ppermute | solution.py:328
  125.2 6.4 %collective-permute-start.3 = (bf16[640,128]{1,0:T(8,128)(2,1)S(1)}, bf16[640,128]{1,0:T(8,128)(2,1)S(1)}, u32[]{:S(2)}, u32[]{:S(2)}) collective-permute-start(bf16[640,128]{1,0:T(8,128)(2,1)S(1)} %get-tuple-element.59), channel_id=1, source_target_pairs={{0,3},{1,4},{2,5},{3,6},{4,7},{5,0},{6,1},{7,2},{8,11},{9,12},{10,... | collective-permute-start | bytes 491528 | tf_op jit(solution)/shard_map/ppermute | solution.py:328
  131.6 2.7 %collective-permute-start.4 = (bf16[640,128]{1,0:T(8,128)(2,1)S(1)}, bf16[640,128]{1,0:T(8,128)(2,1)S(1)}, u32[]{:S(2)}, u32[]{:S(2)}) collective-permute-start(bf16[640,128]{1,0:T(8,128)(2,1)S(1)} %get-tuple-element.60), channel_id=1, source_target_pairs={{0,4},{1,5},{2,6},{3,7},{4,0},{5,1},{6,2},{7,3},{8,12},{9,13},{10,... | collective-permute-start | bytes 491528 | tf_op jit(solution)/shard_map/ppermute | solution.py:328
  134.3 4.3 %collective-permute-start.5 = (bf16[640,128]{1,0:T(8,128)(2,1)S(1)}, bf16[640,128]{1,0:T(8,128)(2,1)S(1)}, u32[]{:S(2)}, u32[]{:S(2)}) collective-permute-start(bf16[640,128]{1,0:T(8,128)(2,1)S(1)} %get-tuple-element.61), channel_id=1, source_target_pairs={{0,5},{1,6},{2,7},{3,0},{4,1},{5,2},{6,3},{7,4},{8,13},{9,14},{10,... | collective-permute-start | bytes 491528 | tf_op jit(solution)/shard_map/ppermute | solution.py:328
  138.7 2.5 %collective-permute-start.6 = (bf16[640,128]{1,0:T(8,128)(2,1)S(1)}, bf16[640,128]{1,0:T(8,128)(2,1)S(1)}, u32[]{:S(2)}, u32[]{:S(2)}) collective-permute-start(bf16[640,128]{1,0:T(8,128)(2,1)S(1)} %get-tuple-element.62), channel_id=1, source_target_pairs={{0,6},{1,7},{2,0},{3,1},{4,2},{5,3},{6,4},{7,5},{8,14},{9,15},{10,... | collective-permute-start | bytes 491528 | tf_op jit(solution)/shard_map/ppermute | solution.py:328
  141.2 6.0 %collective-permute-start.7 = (bf16[640,128]{1,0:T(8,128)(2,1)}, bf16[640,128]{1,0:T(8,128)(2,1)S(1)}, u32[]{:S(2)}, u32[]{:S(2)}) collective-permute-start(bf16[640,128]{1,0:T(8,128)(2,1)} %copy-done.6), channel_id=1, source_target_pairs={{0,7},{1,0},{2,1},{3,2},{4,3},{5,4},{6,5},{7,6},{8,15},{9,8},{10,9... | collective-permute-start | bytes 491528 | tf_op jit(solution)/shard_map/ppermute | solution.py:328
  147.2 4.4 %collective-permute-done.6.refs_6_.refs_14_ = bf16[640,128]{1,0:T(8,128)(2,1)S(1)} collective-permute-done((bf16[640,128]{1,0:T(8,128)(2,1)S(1)}, bf16[640,128]{1,0:T(8,128)(2,1)S(1)}, u32[]{:S(2)}, u32[]{:S(2)}) %collective-permute-start.6) | collective-permute-done | bytes 163872 | tf_op jit(solution)/shard_map/ppermute | solution.py:328
  151.6 0.8 copy-done.14
  152.4 2.8 %finish.1 = (bf16[512,128]{1,0:T(8,128)(2,1)}, bf16[512,1024]{1,0:T(8,128)(2,1)}) custom-call(s32[1]{0:T(128)} %bitcast.place_ref, s32[128]{0:T(128)S(1)} %copy-done.16, f32[512,1024]{1,0:T(8,128)S(1)} %copy-done.3, bf16[16,1152]{1,0:T(8,128)(2,1)S(1)} %copy-done.14, bf16[640,128]{1,0:T(8,128)(2,1)S(1)} %get-tuple-element.56.refs_0_.refs_8_, ...), custom_call_target="tpu_custom_call" | custom-call | flops 16777216 | bytes 5242880 | tf_op jit(solution)/shard_map/finish/pallas_call | solution.py:357
  (40 shorter events, 3.9 us)
Async XLA Ops:
  3.2 7.6 %copy-start.17 = (bf16[1,1024,16]{1,2,0:T(8,128)(2,1)S(1)}, bf16[1,1024,16]{1,2,0:T(8,128)(2,1)}, u32[]{:S(2)}) copy-start(bf16[1,1024,16]{1,2,0:T(8,128)(2,1)} %param.9) | copy-start | bytes 98308
  3.2 7.6 %copy-start.18 = (bf16[1,16,128]{2,1,0:T(8,128)(2,1)S(1)}, bf16[1,16,128]{2,1,0:T(8,128)(2,1)}, u32[]{:S(2)}) copy-start(bf16[1,16,128]{2,1,0:T(8,128)(2,1)} %param.10) | copy-start | bytes 12292
  3.2 65.0 %copy-start.15 = (s32[128]{0:T(128)S(1)}, s32[128]{0:T(128)}, u32[]{:S(2)}) copy-start(s32[128]{0:T(128)} %tenants_ref.5) | copy-start | bytes 1540
  3.2 66.3 %all-to-all-start = ((bf16[8,128,1024]{2,1,0:T(8,128)(2,1)}), bf16[8,128,1024]{2,1,0:T(8,128)(2,1)S(1)}, u32[]{:S(2)}, u32[]{:S(2)}) async-start(bf16[8,128,1024]{2,1,0:T(8,128)(2,1)} %slab.1), calls=%async_computation | async-start | bytes 4194304 | tf_op jit(solution)/shard_map/all_to_all | solution.py:262
  64.7 3.5 %collective-permute-start = (bf16[8,16,1152]{2,1,0:T(8,128)(2,1)S(1)}, bf16[8,16,1152]{2,1,0:T(8,128)(2,1)S(1)}, u32[]{:S(2)}, u32[]{:S(2)}) collective-permute-start(bf16[8,16,1152]{2,1,0:T(8,128)(2,1)S(1)} %bitcast.6), channel_id=1, source_target_pairs={{0,8},{8,0},{1,9},{9,1},{2,10},{10,2},{3,11},{11,3},{4,12},{12,4},... | collective-permute-start | bytes 884744 | tf_op jit(solution)/shard_map/ppermute | solution.py:266
  69.5 13.9 %all-to-all-start.1 = ((bf16[8,16,1152]{2,1,0:T(8,128)(2,1)}), bf16[8,16,1152]{2,1,0:T(8,128)(2,1)S(1)}, u32[]{:S(2)}, u32[]{:S(2)}) async-start(bf16[8,16,1152]{2,1,0:T(8,128)(2,1)} %table.1), calls=%async_computation.1 | async-start | bytes 589824 | tf_op jit(solution)/shard_map/all_to_all | solution.py:309
  73.8 1.6 %copy-start = (bf16[1024,1024]{1,0:T(8,128)(2,1)S(1)}, bf16[1024,1024]{1,0:T(8,128)(2,1)}, u32[]{:S(2)}) copy-start(bf16[1024,1024]{1,0:T(8,128)(2,1)} %weight_ref.3) | copy-start | bytes 6291460
  75.4 3.0 %copy-start.1 = (bf16[1024,1024]{1,0:T(8,128)(2,1)S(1)}, bf16[1024,1024]{1,0:T(8,128)(2,1)}, u32[]{:S(2)}) copy-start(bf16[1024,1024]{1,0:T(8,128)(2,1)} %weight_ref.3) | copy-start | bytes 6291460
  77.0 1.4 copy-start.2
  78.4 5.0 %copy-start.16 = (s32[128]{0:T(128)S(1)}, s32[128]{0:T(128)}, u32[]{:S(2)}) copy-start(s32[128]{0:T(128)} %lengths_ref.3) | copy-start | bytes 1540
  80.6 0.7 copy-start.9
  83.4 0.9 copy-start.7
  84.3 0.9 copy-start.10
  86.5 0.7 copy-start.4
  87.1 0.7 copy-start.8
  87.8 0.7 copy-start.11
  88.5 0.6 copy-start.13
  89.1 62.5 %copy-start.3 = (f32[512,1024]{1,0:T(8,128)S(1)}, f32[512,1024]{1,0:T(8,128)}, u32[]{:S(2)}) copy-start(f32[512,1024]{1,0:T(8,128)} %copy-done.2) | copy-start | bytes 6291460
  89.1 17.8 %all-to-all-start.2 = ((f32[32,16,128]{2,1,0:T(8,128)}), f32[32,16,128]{2,1,0:T(8,128)S(1)}, u32[]{:S(2)}, u32[]{:S(2)}) async-start(f32[32,16,128]{2,1,0:T(8,128)} %copy-done.8), calls=%async_computation.2 | async-start | bytes 524288 | tf_op jit(solution)/shard_map/all_to_all | solution.py:325
  97.1 9.9 %collective-permute-start.1 = (bf16[640,128]{1,0:T(8,128)(2,1)}, bf16[640,128]{1,0:T(8,128)(2,1)S(1)}, u32[]{:S(2)}, u32[]{:S(2)}) collective-permute-start(bf16[640,128]{1,0:T(8,128)(2,1)} %copy-done.11), channel_id=1, source_target_pairs={{0,1},{1,2},{2,3},{3,4},{4,5},{5,6},{6,7},{7,0},{8,9},{9,10},{10,1... | collective-permute-start | bytes 491528 | tf_op jit(solution)/shard_map/ppermute | solution.py:328
  107.0 0.9 copy-start.5
  108.5 0.7 copy-start.6
  109.2 0.7 copy-start.12
  109.9 45.4 %all-to-all-start.3 = ((bf16[32,16,128]{2,1,0:T(8,128)(2,1)}), bf16[32,16,128]{2,1,0:T(8,128)(2,1)S(1)}, u32[]{:S(2)}, u32[]{:S(2)}) async-start(bf16[32,16,128]{2,1,0:T(8,128)(2,1)} %copy-done.12), calls=%async_computation.3 | async-start | bytes 262144 | tf_op jit(solution)/shard_map/all_to_all | solution.py:343
  121.8 19.4 %collective-permute-start.2 = (bf16[640,128]{1,0:T(8,128)(2,1)S(1)}, bf16[640,128]{1,0:T(8,128)(2,1)S(1)}, u32[]{:S(2)}, u32[]{:S(2)}) collective-permute-start(bf16[640,128]{1,0:T(8,128)(2,1)S(1)} %get-tuple-element.58), channel_id=1, source_target_pairs={{0,2},{1,3},{2,4},{3,5},{4,6},{5,7},{6,0},{7,1},{8,10},{9,11},{10,... | collective-permute-start | bytes 491528 | tf_op jit(solution)/shard_map/ppermute | solution.py:328
  125.2 22.0 %collective-permute-start.3 = (bf16[640,128]{1,0:T(8,128)(2,1)S(1)}, bf16[640,128]{1,0:T(8,128)(2,1)S(1)}, u32[]{:S(2)}, u32[]{:S(2)}) collective-permute-start(bf16[640,128]{1,0:T(8,128)(2,1)S(1)} %get-tuple-element.59), channel_id=1, source_target_pairs={{0,3},{1,4},{2,5},{3,6},{4,7},{5,0},{6,1},{7,2},{8,11},{9,12},{10,... | collective-permute-start | bytes 491528 | tf_op jit(solution)/shard_map/ppermute | solution.py:328
  131.6 15.6 %collective-permute-start.4 = (bf16[640,128]{1,0:T(8,128)(2,1)S(1)}, bf16[640,128]{1,0:T(8,128)(2,1)S(1)}, u32[]{:S(2)}, u32[]{:S(2)}) collective-permute-start(bf16[640,128]{1,0:T(8,128)(2,1)S(1)} %get-tuple-element.60), channel_id=1, source_target_pairs={{0,4},{1,5},{2,6},{3,7},{4,0},{5,1},{6,2},{7,3},{8,12},{9,13},{10,... | collective-permute-start | bytes 491528 | tf_op jit(solution)/shard_map/ppermute | solution.py:328
  134.3 12.9 %collective-permute-start.5 = (bf16[640,128]{1,0:T(8,128)(2,1)S(1)}, bf16[640,128]{1,0:T(8,128)(2,1)S(1)}, u32[]{:S(2)}, u32[]{:S(2)}) collective-permute-start(bf16[640,128]{1,0:T(8,128)(2,1)S(1)} %get-tuple-element.61), channel_id=1, source_target_pairs={{0,5},{1,6},{2,7},{3,0},{4,1},{5,2},{6,3},{7,4},{8,13},{9,14},{10,... | collective-permute-start | bytes 491528 | tf_op jit(solution)/shard_map/ppermute | solution.py:328
  138.7 13.0 %collective-permute-start.6 = (bf16[640,128]{1,0:T(8,128)(2,1)S(1)}, bf16[640,128]{1,0:T(8,128)(2,1)S(1)}, u32[]{:S(2)}, u32[]{:S(2)}) collective-permute-start(bf16[640,128]{1,0:T(8,128)(2,1)S(1)} %get-tuple-element.62), channel_id=1, source_target_pairs={{0,6},{1,7},{2,0},{3,1},{4,2},{5,3},{6,4},{7,5},{8,14},{9,15},{10,... | collective-permute-start | bytes 491528 | tf_op jit(solution)/shard_map/ppermute | solution.py:328
  141.2 10.5 %collective-permute-start.7 = (bf16[640,128]{1,0:T(8,128)(2,1)}, bf16[640,128]{1,0:T(8,128)(2,1)S(1)}, u32[]{:S(2)}, u32[]{:S(2)}) collective-permute-start(bf16[640,128]{1,0:T(8,128)(2,1)} %copy-done.6), channel_id=1, source_target_pairs={{0,7},{1,0},{2,1},{3,2},{4,3},{5,4},{6,5},{7,6},{8,15},{9,8},{10,9... | collective-permute-start | bytes 491528 | tf_op jit(solution)/shard_map/ppermute | solution.py:328
  151.6 0.8 copy-start.14

commit v6 on v5

--- a/solution.py
+++ b/solution.py
@@ -124,15 +124,15 @@
     )
 
 
-def value_kernel(columns_ref, weight_ref, *refs):
+def value_kernel(partners, columns_ref, weight_ref, *refs):
     outs, mark_ref, held_ref = refs[:-2], refs[-2], refs[-1]
     mark_ref[...] = jnp.zeros_like(mark_ref)
     sources, rows, width = columns_ref.shape
     columns = columns_ref[...].reshape(sources * rows, width)
     held_ref[...] = dot(columns, weight_ref[...], 1, 0).astype(jnp.bfloat16)
-    me, parts, features = lax.axis_index("tp"), len(outs), outs[0].shape[1]
-    for k, out_ref in enumerate(outs):
-        at = pl.multiple_of(lax.rem(me + k, parts) * features, features)
+    me, features = lax.axis_index("tp"), outs[0].shape[1]
+    for k, out_ref in zip(partners, outs):
+        at = pl.multiple_of(jnp.bitwise_xor(me, k) * features, features)
         out_ref[...] = held_ref[:, pl.ds(at, features)]
 
 
@@ -173,7 +173,7 @@
     share = dot(low, unfold(arrived_ref.at[:, rows:, :], lanes), 1, 0)
     for slot in range(share_ref.shape[0]):
         s = slot % parts
-        share_ref[slot] = share[:, s * lanes : (s + 1) * lanes]
+        share_ref[slot] = share[:, s * lanes : (s + 1) * lanes].astype(share_ref.dtype)
 
 
 def route_kernel(sizes, parts, place_ref, tenants_ref, shares_ref, *refs):
@@ -186,9 +186,9 @@
             block = ((xlo * far_n + far) * near_n + near) * core_n + core
             to_xlo, to_far, to_near, to_core = split_place(tenants_ref[block], sizes)
             first = (xlo * core_n + core) * parts
-            total = shares_ref[first]
+            total = shares_ref[first].astype(jnp.float32)
             for s in range(1, parts):
-                total = total + shares_ref[first + s]
+                total = total + shares_ref[first + s].astype(jnp.float32)
             sums.append(total)
             slots.append(to_far * near_n + to_near)
             mine.append((to_xlo == my_xlo) & (to_core == my_core))
@@ -246,6 +246,9 @@
     rank_rows = 2 * rank * block // features
     parcel = struct((block + rank_rows, features), bf16)
     column = xlo_n * core_n * parts
+    partners = [0] + sorted(
+        range(1, parts), key=lambda k: -(2 * (k % 2) + (0, 1, 2, 1)[k // 2 % 4])
+    )
     slabs = pl.pallas_call(
         functools.partial(slab_kernel, parts),
         out_shape=struct((parts, 2 * rows, width), bf16),
@@ -266,7 +269,7 @@
     other = lax.ppermute(held, "core", [(c, (c + 1) % core_n) for c in range(core_n)])
 
     *parcels, value_mark = pl.pallas_call(
-        value_kernel,
+        functools.partial(value_kernel, partners),
         grid=(block // row_step,),
         out_shape=[parcel] * parts + [mark],
         in_specs=[
@@ -312,7 +315,7 @@
         functools.partial(low_kernel, sizes, parts),
         grid=(1,),
         out_shape=[parcel] * parts
-        + [struct((column, rank, features), f32), struct(own.shape, bf16)],
+        + [struct((column, rank, features), bf16), struct(own.shape, bf16)],
         in_specs=[SMEM, SMEM, SMEM, ANY, VMEM, VMEM, ANY, ANY] + [ANY] * parts,
         out_specs=[pl.BlockSpec((rank_rows, features), lambda i: (block // rank_rows, 0))]
         * parts
@@ -324,12 +327,6 @@
     )(place, tenants, lengths, offered, arrived, upstream, value_mark, base_mark, *parcels)
     arrived_shares = lax.all_to_all(shares, ("xlo", "core", "tp"), 0, 0, tiled=True)
 
-    def leave(k):
-        return lax.ppermute(parcels[k], "tp", [(d, (d + k) % parts) for d in range(parts)])
-
-    early = 1
-    for k in range(1, 1 + early):
-        parcels[k] = leave(k)
     *parcels, routed = pl.pallas_call(
         functools.partial(route_kernel, sizes, parts),
         grid=(1,),
@@ -341,8 +338,10 @@
         name="route",
     )(place, tenants, arrived_shares, *parcels)
     far_parts = lax.all_to_all(routed, ("far", "near"), 0, 0, tiled=True)
-    for k in range(1 + early, parts):
-        parcels[k] = leave(k)
+    parcels = parcels[:1] + [
+        lax.ppermute(parcel, "tp", [(d, d ^ k) for d in range(parts)])
+        for k, parcel in zip(partners[1:], parcels[1:])
+    ]
     up_grad = pl.pallas_call(
         sum_kernel,
         grid=(1,),

time: 158 us -> 154 us (0.975)
  blocking collectives: 53.9 us -> 67.3 us
  starting transfers between devices: 63.3 us -> 52.6 us
  waiting for transfers between devices: 13.6 us -> 8.63 us
  local copies, waits for them, and re-layouts: 11.1 us -> 8.48 us
    all_to_all x0 -> x1, blocking collectives: none -> 13.4 us  [on_device(): lax.all_to_all(shares, ('xlo', 'core', 'tp'), 0, 0, tiled=True)]
    all_to_all x1 -> x0, starting transfers between devices: 7.96 us -> none  [on_device(): lax.all_to_all(shares, ('xlo', 'core', 'tp'), 0, 0, tiled=True)]
    ppermute x7, waiting for transfers between devices: 10 us -> 4.98 us  [on_device(): lax.ppermute(parcel, 'tp', [(d, d ^ k) for d in range(parts)])]
    ppermute x7, starting transfers between devices: 29.6 us -> 26.9 us  [on_device(): lax.ppermute(parcel, 'tp', [(d, d ^ k) for d in range(parts)])]
    unnamed x38 -> x28, local copies, waits for them, and re-layouts: 11.1 us -> 8.48 us
  transfers between devices with their start and end apart: 12 -> 11, of which waited for: 4 -> 4; matrix products, arithmetic and copies ran while one was open for 0% -> 0% of each run, Pallas kernels for 5% -> 5%
where the time goes in v6:
time: 154 us; the launch traced here: 151 us
  blocking collectives  67.3 us (44%)
  starting transfers between devices  52.6 us (34%)
  Pallas kernels  13.6 us (9%)
  waiting for transfers between devices  8.63 us (6%)
  local copies, waits for them, and re-layouts  8.48 us (6%)
    all_gather x1, blocking collectives, on_device(): held = lax.all_gather(own, 'far', axis=0, tiled=False)  53.9 us
    ppermute x7, starting transfers between devices, on_device(): lax.ppermute(parcel, 'tp', [(d, d ^ k) for d in range(parts)])  26.9 us
    all_to_all x1, blocking collectives, on_device(): lax.all_to_all(shares, ('xlo', 'core', 'tp'), 0, 0, tiled=True)  13.4 us
    all_to_all x1, starting transfers between devices, on_device(): far_parts = lax.all_to_all(routed, ('far', 'near'), 0, 0, tiled=True)  11.9 us
    unnamed x28, local copies, waits for them, and re-layouts  8.48 us
    all_to_all x1, starting transfers between devices, on_device(): arrived = lax.all_to_all(slabs, 'tp', 0, 0, tiled=True)  7.58 us
    ppermute x7, waiting for transfers between devices, on_device(): lax.ppermute(parcel, 'tp', [(d, d ^ k) for d in range(parts)])  4.98 us
    all_to_all x1, starting transfers between devices, on_device(): offered = lax.all_to_all(table, ('xlo', 'near'), 0, 0, tiled=True)  4.28 us
  transfers between devices with their start and end apart: 11, of which 4 were waited for; matrix products, arithmetic and copies ran while one was open for 0% of the time, Pallas kernels for 5%

profile of v6, /device:TPU:6, one launch (start us, length us, event | category | flops | bytes accessed | tf_op | source)
XLA Modules:
  0.0 151.5 jit_solution(4486498824924443541)
XLA Ops:
  0.6 2.4 %slab.1 = bf16[8,128,1024]{2,1,0:T(8,128)(2,1)} custom-call(bf16[64,8192]{1,0:T(8,128)(2,1)} %tokens_ref.1, bf16[512,128]{1,0:T(8,128)(2,1)} %upstream_ref.3), custom_call_target="tpu_custom_call" | custom-call | tf_op jit(solution)/shard_map/slab/pallas_call | solution.py:252
  3.1 7.6 %all-to-all-start = ((bf16[8,128,1024]{2,1,0:T(8,128)(2,1)}), bf16[8,128,1024]{2,1,0:T(8,128)(2,1)S(1)}, u32[]{:S(2)}, u32[]{:S(2)}) async-start(bf16[8,128,1024]{2,1,0:T(8,128)(2,1)} %slab.1), calls=%async_computation | async-start | bytes 4194304 | tf_op jit(solution)/shard_map/all_to_all | solution.py:265
  10.7 53.9 %all-gather = bf16[128,1152]{1,0:T(8,128)(2,1)S(1)} all-gather(bf16[16,1152]{1,0:T(8,128)(2,1)S(1)} %pad_maximum_fusion), channel_id=2, replica_groups=mesh['xlo'=2,'far'=8,'near'=4,'core'=2,'tp'=8] {'far'}, dimensions={0}, use_global_device_ids=true | all-gather | bytes 331776 | tf_op jit(solution)/shard_map/all_gather | solution.py:268
  64.6 1.9 %collective-permute-start = (bf16[8,16,1152]{2,1,0:T(8,128)(2,1)S(1)}, bf16[8,16,1152]{2,1,0:T(8,128)(2,1)S(1)}, u32[]{:S(2)}, u32[]{:S(2)}) collective-permute-start(bf16[8,16,1152]{2,1,0:T(8,128)(2,1)S(1)} %bitcast.6), channel_id=1, source_target_pairs={{0,8},{8,0},{1,9},{9,1},{2,10},{10,2},{3,11},{11,3},{4,12},{12,4},... | collective-permute-start | bytes 884744 | tf_op jit(solution)/shard_map/ppermute | solution.py:269
  66.6 1.5 %collective-permute-done.other_ref = bf16[8,16,1152]{2,1,0:T(8,128)(2,1)S(1)} collective-permute-done((bf16[8,16,1152]{2,1,0:T(8,128)(2,1)S(1)}, bf16[8,16,1152]{2,1,0:T(8,128)(2,1)S(1)}, u32[]{:S(2)}, u32[]{:S(2)}) %collective-permute-start) | collective-permute-done | bytes 294944 | tf_op jit(solution)/shard_map/ppermute | solution.py:269
  68.1 1.3 table.1
  69.4 4.3 %all-to-all-start.1 = ((bf16[8,16,1152]{2,1,0:T(8,128)(2,1)}), bf16[8,16,1152]{2,1,0:T(8,128)(2,1)S(1)}, u32[]{:S(2)}, u32[]{:S(2)}) async-start(bf16[8,16,1152]{2,1,0:T(8,128)(2,1)} %table.1), calls=%async_computation.1 | async-start | bytes 589824 | tf_op jit(solution)/shard_map/all_to_all | solution.py:312
  73.7 1.6 %copy-done = bf16[1024,1024]{1,0:T(8,128)(2,1)S(1)} copy-done((bf16[1024,1024]{1,0:T(8,128)(2,1)S(1)}, bf16[1024,1024]{1,0:T(8,128)(2,1)}, u32[]{:S(2)}) %copy-start) | copy-done | bytes 2097176
  75.3 1.6 %base.1 = (f32[512,1024]{1,0:T(8,128)S(1)}, f32[8,128]{1,0:T(8,128)S(1)}) custom-call(bf16[8,128,1024]{2,1,0:T(8,128)(2,1)S(1)} %all-to-all-done.upstream_ref.columns_ref.arrived_ref, bf16[1024,1024]{1,0:T(8,128)(2,1)S(1)} %copy-done), custom_call_target="tpu_custom_call" | custom-call | flops 1073741824 | bytes 6291456 | tf_op jit(solution)/shard_map/base/pallas_call | solution.py:287
  76.9 1.4 copy-done.2
  78.3 2.2 %value.1 = (bf16[640,128]{1,0:T(8,128)(2,1)S(1)}, bf16[640,128]{1,0:T(8,128)(2,1)S(1)}, bf16[640,128]{1,0:T(8,128)(2,1)S(1)}, bf16[640,128]{1,0:T(8,128)(2,1)S(1...) custom-call(bf16[8,128,1024]{2,1,0:T(8,128)(2,1)S(1)} %all-to-all-do, ...), custom_call_target="tpu_custom_call" | custom-call | flops 1073741824 | bytes 4194304 | tf_op jit(solution)/shard_map/value/pallas_call | solution.py:271
  80.5 0.7 copy-done.4
  81.2 2.1 %all-to-all-done.1.offered_ref = bf16[8,16,1152]{2,1,0:T(8,128)(2,1)S(1)} async-done(((bf16[8,16,1152]{2,1,0:T(8,128)(2,1)}), bf16[8,16,1152]{2,1,0:T(8,128)(2,1)S(1)}, u32[]{:S(2)}, u32[]{:S(2)}) %all-to-all-start.1) | async-done | bytes 294944 | tf_op jit(solution)/shard_map/all_to_all | solution.py:312
  83.3 0.9 copy-done.5
  84.2 0.9 copy-done.7
  85.1 1.2 low.1
  86.4 13.4 %all_to_all.20.shares_ref = bf16[32,16,128]{2,1,0:T(8,128)(2,1)S(1)} all-to-all(bf16[32,16,128]{2,1,0:T(8,128)(2,1)S(1)} %get-tuple-element.47), channel_id=1, replica_groups=mesh['xlo'=2,'far'=8,'near'=4,'core'=2,'tp'=8] {'xlo','core','tp'}, dimensions={0} | all-to-all | bytes 262144 | tf_op jit(solution)/shard_map/all_to_all | solution.py:328
  99.8 1.3 route.1
  101.1 0.7 copy-done.6
  101.7 11.9 %all-to-all-start.3 = ((bf16[32,16,128]{2,1,0:T(8,128)(2,1)}), bf16[32,16,128]{2,1,0:T(8,128)(2,1)S(1)}, u32[]{:S(2)}, u32[]{:S(2)}) async-start(bf16[32,16,128]{2,1,0:T(8,128)(2,1)} %get-tuple-element.66), calls=%async_computation.3 | async-start | bytes 262144 | tf_op jit(solution)/shard_map/all_to_all | solution.py:340
  113.7 4.7 %collective-permute-start.1 = (bf16[640,128]{1,0:T(8,128)(2,1)S(1)}, bf16[640,128]{1,0:T(8,128)(2,1)S(1)}, u32[]{:S(2)}, u32[]{:S(2)}) collective-permute-start(bf16[640,128]{1,0:T(8,128)(2,1)S(1)} %get-tuple-element.57), channel_id=1, source_target_pairs={{0,5},{1,4},{2,7},{3,6},{4,1},{5,0},{6,3},{7,2},{8,13},{9,12},{10,... | collective-permute-start | bytes 491528 | tf_op jit(solution)/shard_map/ppermute | solution.py:342
  118.3 3.9 %collective-permute-start.2 = (bf16[640,128]{1,0:T(8,128)(2,1)S(1)}, bf16[640,128]{1,0:T(8,128)(2,1)S(1)}, u32[]{:S(2)}, u32[]{:S(2)}) collective-permute-start(bf16[640,128]{1,0:T(8,128)(2,1)S(1)} %get-tuple-element.58), channel_id=1, source_target_pairs={{0,3},{1,2},{2,1},{3,0},{4,7},{5,6},{6,5},{7,4},{8,11},{9,10},{10,... | collective-permute-start | bytes 491528 | tf_op jit(solution)/shard_map/ppermute | solution.py:342
  122.3 5.2 %collective-permute-start.3 = (bf16[640,128]{1,0:T(8,128)(2,1)S(1)}, bf16[640,128]{1,0:T(8,128)(2,1)S(1)}, u32[]{:S(2)}, u32[]{:S(2)}) collective-permute-start(bf16[640,128]{1,0:T(8,128)(2,1)S(1)} %get-tuple-element.59), channel_id=1, source_target_pairs={{0,7},{1,6},{2,5},{3,4},{4,3},{5,2},{6,1},{7,0},{8,15},{9,14},{10,... | collective-permute-start | bytes 491528 | tf_op jit(solution)/shard_map/ppermute | solution.py:342
  127.5 3.3 %collective-permute-start.4 = (bf16[640,128]{1,0:T(8,128)(2,1)S(1)}, bf16[640,128]{1,0:T(8,128)(2,1)S(1)}, u32[]{:S(2)}, u32[]{:S(2)}) collective-permute-start(bf16[640,128]{1,0:T(8,128)(2,1)S(1)} %get-tuple-element.60), channel_id=1, source_target_pairs={{0,1},{1,0},{2,3},{3,2},{4,5},{5,4},{6,7},{7,6},{8,9},{9,8},{10,11... | collective-permute-start | bytes 491528 | tf_op jit(solution)/shard_map/ppermute | solution.py:342
  130.8 3.6 %collective-permute-start.5 = (bf16[640,128]{1,0:T(8,128)(2,1)S(1)}, bf16[640,128]{1,0:T(8,128)(2,1)S(1)}, u32[]{:S(2)}, u32[]{:S(2)}) collective-permute-start(bf16[640,128]{1,0:T(8,128)(2,1)S(1)} %get-tuple-element.61), channel_id=1, source_target_pairs={{0,4},{1,5},{2,6},{3,7},{4,0},{5,1},{6,2},{7,3},{8,12},{9,13},{10,... | collective-permute-start | bytes 491528 | tf_op jit(solution)/shard_map/ppermute | solution.py:342
  134.4 2.6 %collective-permute-start.6 = (bf16[640,128]{1,0:T(8,128)(2,1)S(1)}, bf16[640,128]{1,0:T(8,128)(2,1)S(1)}, u32[]{:S(2)}, u32[]{:S(2)}) collective-permute-start(bf16[640,128]{1,0:T(8,128)(2,1)S(1)} %get-tuple-element.62), channel_id=1, source_target_pairs={{0,2},{1,3},{2,0},{3,1},{4,6},{5,7},{6,4},{7,5},{8,10},{9,11},{10,... | collective-permute-start | bytes 491528 | tf_op jit(solution)/shard_map/ppermute | solution.py:342
  137.0 3.6 %collective-permute-start.7 = (bf16[640,128]{1,0:T(8,128)(2,1)}, bf16[640,128]{1,0:T(8,128)(2,1)S(1)}, u32[]{:S(2)}, u32[]{:S(2)}) collective-permute-start(bf16[640,128]{1,0:T(8,128)(2,1)} %copy-done.6), channel_id=1, source_target_pairs={{0,6},{1,7},{2,4},{3,5},{4,2},{5,3},{6,0},{7,1},{8,14},{9,15},{10,... | collective-permute-start | bytes 491528 | tf_op jit(solution)/shard_map/ppermute | solution.py:342
  140.7 1.2 collective-permute-done.6.refs_6_.refs_14_
  141.9 3.8 %collective-permute-done.7.refs_7_.refs_15_ = bf16[640,128]{1,0:T(8,128)(2,1)S(1)} collective-permute-done((bf16[640,128]{1,0:T(8,128)(2,1)}, bf16[640,128]{1,0:T(8,128)(2,1)S(1)}, u32[]{:S(2)}, u32[]{:S(2)}) %collective-permute-start.7) | collective-permute-done | bytes 163872 | tf_op jit(solution)/shard_map/ppermute | solution.py:342
  145.6 1.6 %copy-done.3 = f32[512,1024]{1,0:T(8,128)S(1)} copy-done((f32[512,1024]{1,0:T(8,128)S(1)}, f32[512,1024]{1,0:T(8,128)}, u32[]{:S(2)}) %copy-start.3) | copy-done | bytes 2097176
  147.2 0.8 copy-done.9
  148.0 2.8 %finish.1 = (bf16[512,128]{1,0:T(8,128)(2,1)}, bf16[512,1024]{1,0:T(8,128)(2,1)}) custom-call(s32[1]{0:T(128)} %bitcast.place_ref, s32[128]{0:T(128)S(1)} %copy-done.11, f32[512,1024]{1,0:T(8,128)S(1)} %copy-done.3, bf16[16,1152]{1,0:T(8,128)(2,1)S(1)} %copy-done.9, bf16[640,128]{1,0:T(8,128)(2,1)S(1)} %get-tuple-element.56.refs_0_.refs_8_, ...), custom_call_target="tpu_custom_call" | custom-call | flops 16777216 | bytes 5242880 | tf_op jit(solution)/shard_map/finish/pallas_call | solution.py:356
  (29 shorter events, 0.7 us)
Async XLA Ops:
  3.1 7.6 %copy-start.12 = (bf16[1,1024,16]{1,2,0:T(8,128)(2,1)S(1)}, bf16[1,1024,16]{1,2,0:T(8,128)(2,1)}, u32[]{:S(2)}) copy-start(bf16[1,1024,16]{1,2,0:T(8,128)(2,1)} %param.9) | copy-start | bytes 98308
  3.1 7.6 %copy-start.13 = (bf16[1,16,128]{2,1,0:T(8,128)(2,1)S(1)}, bf16[1,16,128]{2,1,0:T(8,128)(2,1)}, u32[]{:S(2)}) copy-start(bf16[1,16,128]{2,1,0:T(8,128)(2,1)} %param.10) | copy-start | bytes 12292
  3.1 65.0 %copy-start.10 = (s32[128]{0:T(128)S(1)}, s32[128]{0:T(128)}, u32[]{:S(2)}) copy-start(s32[128]{0:T(128)} %tenants_ref.5) | copy-start | bytes 1540
  3.1 66.3 %all-to-all-start = ((bf16[8,128,1024]{2,1,0:T(8,128)(2,1)}), bf16[8,128,1024]{2,1,0:T(8,128)(2,1)S(1)}, u32[]{:S(2)}, u32[]{:S(2)}) async-start(bf16[8,128,1024]{2,1,0:T(8,128)(2,1)} %slab.1), calls=%async_computation | async-start | bytes 4194304 | tf_op jit(solution)/shard_map/all_to_all | solution.py:265
  64.6 3.5 %collective-permute-start = (bf16[8,16,1152]{2,1,0:T(8,128)(2,1)S(1)}, bf16[8,16,1152]{2,1,0:T(8,128)(2,1)S(1)}, u32[]{:S(2)}, u32[]{:S(2)}) collective-permute-start(bf16[8,16,1152]{2,1,0:T(8,128)(2,1)S(1)} %bitcast.6), channel_id=1, source_target_pairs={{0,8},{8,0},{1,9},{9,1},{2,10},{10,2},{3,11},{11,3},{4,12},{12,4},... | collective-permute-start | bytes 884744 | tf_op jit(solution)/shard_map/ppermute | solution.py:269
  69.4 13.9 %all-to-all-start.1 = ((bf16[8,16,1152]{2,1,0:T(8,128)(2,1)}), bf16[8,16,1152]{2,1,0:T(8,128)(2,1)S(1)}, u32[]{:S(2)}, u32[]{:S(2)}) async-start(bf16[8,16,1152]{2,1,0:T(8,128)(2,1)} %table.1), calls=%async_computation.1 | async-start | bytes 589824 | tf_op jit(solution)/shard_map/all_to_all | solution.py:312
  73.7 1.6 %copy-start = (bf16[1024,1024]{1,0:T(8,128)(2,1)S(1)}, bf16[1024,1024]{1,0:T(8,128)(2,1)}, u32[]{:S(2)}) copy-start(bf16[1024,1024]{1,0:T(8,128)(2,1)} %weight_ref.3) | copy-start | bytes 6291460
  75.3 3.0 %copy-start.1 = (bf16[1024,1024]{1,0:T(8,128)(2,1)S(1)}, bf16[1024,1024]{1,0:T(8,128)(2,1)}, u32[]{:S(2)}) copy-start(bf16[1024,1024]{1,0:T(8,128)(2,1)} %weight_ref.3) | copy-start | bytes 6291460
  76.9 1.4 copy-start.2
  78.3 5.0 %copy-start.11 = (s32[128]{0:T(128)S(1)}, s32[128]{0:T(128)}, u32[]{:S(2)}) copy-start(s32[128]{0:T(128)} %lengths_ref.3) | copy-start | bytes 1540
  80.5 0.7 copy-start.4
  83.3 0.9 copy-start.5
  84.2 0.9 copy-start.7
  86.4 14.7 %copy-start.8 = (bf16[16,1152]{1,0:T(8,128)(2,1)}, bf16[16,1152]{1,0:T(8,128)(2,1)S(1)}, u32[]{:S(2)}) copy-start(bf16[16,1152]{1,0:T(8,128)(2,1)S(1)} %get-tuple-element.46.item_ref) | copy-start | bytes 110596
  101.1 0.7 copy-start.6
  101.7 49.1 %all-to-all-start.3 = ((bf16[32,16,128]{2,1,0:T(8,128)(2,1)}), bf16[32,16,128]{2,1,0:T(8,128)(2,1)S(1)}, u32[]{:S(2)}, u32[]{:S(2)}) async-start(bf16[32,16,128]{2,1,0:T(8,128)(2,1)} %get-tuple-element.66), calls=%async_computation.3 | async-start | bytes 262144 | tf_op jit(solution)/shard_map/all_to_all | solution.py:340
  113.7 20.8 %collective-permute-start.1 = (bf16[640,128]{1,0:T(8,128)(2,1)S(1)}, bf16[640,128]{1,0:T(8,128)(2,1)S(1)}, u32[]{:S(2)}, u32[]{:S(2)}) collective-permute-start(bf16[640,128]{1,0:T(8,128)(2,1)S(1)} %get-tuple-element.57), channel_id=1, source_target_pairs={{0,5},{1,4},{2,7},{3,6},{4,1},{5,0},{6,3},{7,2},{8,13},{9,12},{10,... | collective-permute-start | bytes 491528 | tf_op jit(solution)/shard_map/ppermute | solution.py:342
  118.3 18.7 %collective-permute-start.2 = (bf16[640,128]{1,0:T(8,128)(2,1)S(1)}, bf16[640,128]{1,0:T(8,128)(2,1)S(1)}, u32[]{:S(2)}, u32[]{:S(2)}) collective-permute-start(bf16[640,128]{1,0:T(8,128)(2,1)S(1)} %get-tuple-element.58), channel_id=1, source_target_pairs={{0,3},{1,2},{2,1},{3,0},{4,7},{5,6},{6,5},{7,4},{8,11},{9,10},{10,... | collective-permute-start | bytes 491528 | tf_op jit(solution)/shard_map/ppermute | solution.py:342
  122.3 18.4 %collective-permute-start.3 = (bf16[640,128]{1,0:T(8,128)(2,1)S(1)}, bf16[640,128]{1,0:T(8,128)(2,1)S(1)}, u32[]{:S(2)}, u32[]{:S(2)}) collective-permute-start(bf16[640,128]{1,0:T(8,128)(2,1)S(1)} %get-tuple-element.59), channel_id=1, source_target_pairs={{0,7},{1,6},{2,5},{3,4},{4,3},{5,2},{6,1},{7,0},{8,15},{9,14},{10,... | collective-permute-start | bytes 491528 | tf_op jit(solution)/shard_map/ppermute | solution.py:342
  127.5 13.1 %collective-permute-start.4 = (bf16[640,128]{1,0:T(8,128)(2,1)S(1)}, bf16[640,128]{1,0:T(8,128)(2,1)S(1)}, u32[]{:S(2)}, u32[]{:S(2)}) collective-permute-start(bf16[640,128]{1,0:T(8,128)(2,1)S(1)} %get-tuple-element.60), channel_id=1, source_target_pairs={{0,1},{1,0},{2,3},{3,2},{4,5},{5,4},{6,7},{7,6},{8,9},{9,8},{10,11... | collective-permute-start | bytes 491528 | tf_op jit(solution)/shard_map/ppermute | solution.py:342
  130.8 9.9 %collective-permute-start.5 = (bf16[640,128]{1,0:T(8,128)(2,1)S(1)}, bf16[640,128]{1,0:T(8,128)(2,1)S(1)}, u32[]{:S(2)}, u32[]{:S(2)}) collective-permute-start(bf16[640,128]{1,0:T(8,128)(2,1)S(1)} %get-tuple-element.61), channel_id=1, source_target_pairs={{0,4},{1,5},{2,6},{3,7},{4,0},{5,1},{6,2},{7,3},{8,12},{9,13},{10,... | collective-permute-start | bytes 491528 | tf_op jit(solution)/shard_map/ppermute | solution.py:342
  134.4 7.4 %collective-permute-start.6 = (bf16[640,128]{1,0:T(8,128)(2,1)S(1)}, bf16[640,128]{1,0:T(8,128)(2,1)S(1)}, u32[]{:S(2)}, u32[]{:S(2)}) collective-permute-start(bf16[640,128]{1,0:T(8,128)(2,1)S(1)} %get-tuple-element.62), channel_id=1, source_target_pairs={{0,2},{1,3},{2,0},{3,1},{4,6},{5,7},{6,4},{7,5},{8,10},{9,11},{10,... | collective-permute-start | bytes 491528 | tf_op jit(solution)/shard_map/ppermute | solution.py:342
  137.0 8.6 %collective-permute-start.7 = (bf16[640,128]{1,0:T(8,128)(2,1)}, bf16[640,128]{1,0:T(8,128)(2,1)S(1)}, u32[]{:S(2)}, u32[]{:S(2)}) collective-permute-start(bf16[640,128]{1,0:T(8,128)(2,1)} %copy-done.6), channel_id=1, source_target_pairs={{0,6},{1,7},{2,4},{3,5},{4,2},{5,3},{6,0},{7,1},{8,14},{9,15},{10,... | collective-permute-start | bytes 491528 | tf_op jit(solution)/shard_map/ppermute | solution.py:342
  145.6 1.6 %copy-start.3 = (f32[512,1024]{1,0:T(8,128)S(1)}, f32[512,1024]{1,0:T(8,128)}, u32[]{:S(2)}) copy-start(f32[512,1024]{1,0:T(8,128)} %copy-done.2) | copy-start | bytes 6291460
  147.2 0.8 copy-start.9

commit v7 on v6

--- a/solution.py
+++ b/solution.py
@@ -369,7 +369,7 @@
             pl.BlockSpec((features, features), lambda i: (i, 0)),
             pl.BlockSpec((features, width), lambda i: (i, 0)),
         ),
-        compiler_params=params(),
+        compiler_params=params(52),
         cost_estimate=cost(2 * block * width * rank, 5 << 20),
         name="finish",
     )(place, lengths, base, item, *parcels, *parcels)

time: 154 us -> 154 us (level)
  local copies, waits for them, and re-layouts: 8.48 us -> 6.86 us
    unnamed x28 -> x26, local copies, waits for them, and re-layouts: 8.48 us -> 6.86 us
  transfers between devices with their start and end apart: 11 -> 11, of which waited for: 4 -> 4; matrix products, arithmetic and copies ran while one was open for 0% -> 0% of each run, Pallas kernels for 5% -> 6%
where the time goes in v7:
time: 154 us; the launch traced here: 151 us
  blocking collectives  67.3 us (44%)
  starting transfers between devices  52.6 us (34%)
  Pallas kernels  14.8 us (10%)
  waiting for transfers between devices  8.66 us (6%)
  local copies, waits for them, and re-layouts  6.86 us (4%)
    all_gather x1, blocking collectives, on_device(): held = lax.all_gather(own, 'far', axis=0, tiled=False)  53.9 us
    ppermute x7, starting transfers between devices, on_device(): lax.ppermute(parcel, 'tp', [(d, d ^ k) for d in range(parts)])  26.9 us
    all_to_all x1, blocking collectives, on_device(): lax.all_to_all(shares, ('xlo', 'core', 'tp'), 0, 0, tiled=True)  13.4 us
    all_to_all x1, starting transfers between devices, on_device(): far_parts = lax.all_to_all(routed, ('far', 'near'), 0, 0, tiled=True)  11.9 us
    all_to_all x1, starting transfers between devices, on_device(): arrived = lax.all_to_all(slabs, 'tp', 0, 0, tiled=True)  7.58 us
    unnamed x26, local copies, waits for them, and re-layouts  6.86 us
    ppermute x7, waiting for transfers between devices, on_device(): lax.ppermute(parcel, 'tp', [(d, d ^ k) for d in range(parts)])  4.98 us
    all_to_all x1, starting transfers between devices, on_device(): offered = lax.all_to_all(table, ('xlo', 'near'), 0, 0, tiled=True)  4.28 us
  transfers between devices with their start and end apart: 11, of which 4 were waited for; matrix products, arithmetic and copies ran while one was open for 0% of the time, Pallas kernels for 6%

profile of v7, /device:TPU:6, one launch (start us, length us, event | category | flops | bytes accessed | tf_op | source)
XLA Modules:
  0.0 151.1 jit_solution(3194174432083921106)
XLA Ops:
  0.6 2.4 %slab.1 = bf16[8,128,1024]{2,1,0:T(8,128)(2,1)} custom-call(bf16[64,8192]{1,0:T(8,128)(2,1)} %tokens_ref.1, bf16[512,128]{1,0:T(8,128)(2,1)} %upstream_ref.3), custom_call_target="tpu_custom_call" | custom-call | tf_op jit(solution)/shard_map/slab/pallas_call | solution.py:252
  3.1 7.6 %all-to-all-start = ((bf16[8,128,1024]{2,1,0:T(8,128)(2,1)}), bf16[8,128,1024]{2,1,0:T(8,128)(2,1)S(1)}, u32[]{:S(2)}, u32[]{:S(2)}) async-start(bf16[8,128,1024]{2,1,0:T(8,128)(2,1)} %slab.1), calls=%async_computation | async-start | bytes 4194304 | tf_op jit(solution)/shard_map/all_to_all | solution.py:265
  10.7 53.9 %all-gather = bf16[128,1152]{1,0:T(8,128)(2,1)S(1)} all-gather(bf16[16,1152]{1,0:T(8,128)(2,1)S(1)} %pad_maximum_fusion), channel_id=2, replica_groups=mesh['xlo'=2,'far'=8,'near'=4,'core'=2,'tp'=8] {'far'}, dimensions={0}, use_global_device_ids=true | all-gather | bytes 331776 | tf_op jit(solution)/shard_map/all_gather | solution.py:268
  64.6 1.9 %collective-permute-start = (bf16[8,16,1152]{2,1,0:T(8,128)(2,1)S(1)}, bf16[8,16,1152]{2,1,0:T(8,128)(2,1)S(1)}, u32[]{:S(2)}, u32[]{:S(2)}) collective-permute-start(bf16[8,16,1152]{2,1,0:T(8,128)(2,1)S(1)} %bitcast.6), channel_id=1, source_target_pairs={{0,8},{8,0},{1,9},{9,1},{2,10},{10,2},{3,11},{11,3},{4,12},{12,4},... | collective-permute-start | bytes 884744 | tf_op jit(solution)/shard_map/ppermute | solution.py:269
  66.5 1.5 %collective-permute-done.other_ref = bf16[8,16,1152]{2,1,0:T(8,128)(2,1)S(1)} collective-permute-done((bf16[8,16,1152]{2,1,0:T(8,128)(2,1)S(1)}, bf16[8,16,1152]{2,1,0:T(8,128)(2,1)S(1)}, u32[]{:S(2)}, u32[]{:S(2)}) %collective-permute-start) | collective-permute-done | bytes 294944 | tf_op jit(solution)/shard_map/ppermute | solution.py:269
  68.1 1.3 table.1
  69.4 4.3 %all-to-all-start.1 = ((bf16[8,16,1152]{2,1,0:T(8,128)(2,1)}), bf16[8,16,1152]{2,1,0:T(8,128)(2,1)S(1)}, u32[]{:S(2)}, u32[]{:S(2)}) async-start(bf16[8,16,1152]{2,1,0:T(8,128)(2,1)} %table.1), calls=%async_computation.1 | async-start | bytes 589824 | tf_op jit(solution)/shard_map/all_to_all | solution.py:312
  73.7 1.6 %copy-done = bf16[1024,1024]{1,0:T(8,128)(2,1)S(1)} copy-done((bf16[1024,1024]{1,0:T(8,128)(2,1)S(1)}, bf16[1024,1024]{1,0:T(8,128)(2,1)}, u32[]{:S(2)}) %copy-start) | copy-done | bytes 2097176
  75.3 1.6 %base.1 = (f32[512,1024]{1,0:T(8,128)S(1)}, f32[8,128]{1,0:T(8,128)S(1)}) custom-call(bf16[8,128,1024]{2,1,0:T(8,128)(2,1)S(1)} %all-to-all-done.upstream_ref.columns_ref.arrived_ref, bf16[1024,1024]{1,0:T(8,128)(2,1)S(1)} %copy-done), custom_call_target="tpu_custom_call" | custom-call | flops 1073741824 | bytes 6291456 | tf_op jit(solution)/shard_map/base/pallas_call | solution.py:287
  76.9 1.3 copy-done.2
  78.3 2.2 %value.1 = (bf16[640,128]{1,0:T(8,128)(2,1)S(1)}, bf16[640,128]{1,0:T(8,128)(2,1)S(1)}, bf16[640,128]{1,0:T(8,128)(2,1)S(1)}, bf16[640,128]{1,0:T(8,128)(2,1)S(1...) custom-call(bf16[8,128,1024]{2,1,0:T(8,128)(2,1)S(1)} %all-to-all-do, ...), custom_call_target="tpu_custom_call" | custom-call | flops 1073741824 | bytes 4194304 | tf_op jit(solution)/shard_map/value/pallas_call | solution.py:271
  80.5 0.6 copy-done.3
  81.2 2.1 %all-to-all-done.1.offered_ref = bf16[8,16,1152]{2,1,0:T(8,128)(2,1)S(1)} async-done(((bf16[8,16,1152]{2,1,0:T(8,128)(2,1)}), bf16[8,16,1152]{2,1,0:T(8,128)(2,1)S(1)}, u32[]{:S(2)}, u32[]{:S(2)}) %all-to-all-start.1) | async-done | bytes 294944 | tf_op jit(solution)/shard_map/all_to_all | solution.py:312
  83.3 0.9 copy-done.4
  84.2 0.9 copy-done.6
  85.1 1.2 low.1
  86.4 13.4 %all_to_all.20.shares_ref = bf16[32,16,128]{2,1,0:T(8,128)(2,1)S(1)} all-to-all(bf16[32,16,128]{2,1,0:T(8,128)(2,1)S(1)} %get-tuple-element.47), channel_id=1, replica_groups=mesh['xlo'=2,'far'=8,'near'=4,'core'=2,'tp'=8] {'xlo','core','tp'}, dimensions={0} | all-to-all | bytes 262144 | tf_op jit(solution)/shard_map/all_to_all | solution.py:328
  99.8 1.3 route.1
  101.0 0.7 copy-done.5
  101.7 11.9 %all-to-all-start.3 = ((bf16[32,16,128]{2,1,0:T(8,128)(2,1)}), bf16[32,16,128]{2,1,0:T(8,128)(2,1)S(1)}, u32[]{:S(2)}, u32[]{:S(2)}) async-start(bf16[32,16,128]{2,1,0:T(8,128)(2,1)} %get-tuple-element.66), calls=%async_computation.3 | async-start | bytes 262144 | tf_op jit(solution)/shard_map/all_to_all | solution.py:340
  113.6 4.7 %collective-permute-start.1 = (bf16[640,128]{1,0:T(8,128)(2,1)S(1)}, bf16[640,128]{1,0:T(8,128)(2,1)S(1)}, u32[]{:S(2)}, u32[]{:S(2)}) collective-permute-start(bf16[640,128]{1,0:T(8,128)(2,1)S(1)} %get-tuple-element.57), channel_id=1, source_target_pairs={{0,5},{1,4},{2,7},{3,6},{4,1},{5,0},{6,3},{7,2},{8,13},{9,12},{10,... | collective-permute-start | bytes 491528 | tf_op jit(solution)/shard_map/ppermute | solution.py:342
  118.3 3.9 %collective-permute-start.2 = (bf16[640,128]{1,0:T(8,128)(2,1)S(1)}, bf16[640,128]{1,0:T(8,128)(2,1)S(1)}, u32[]{:S(2)}, u32[]{:S(2)}) collective-permute-start(bf16[640,128]{1,0:T(8,128)(2,1)S(1)} %get-tuple-element.58), channel_id=1, source_target_pairs={{0,3},{1,2},{2,1},{3,0},{4,7},{5,6},{6,5},{7,4},{8,11},{9,10},{10,... | collective-permute-start | bytes 491528 | tf_op jit(solution)/shard_map/ppermute | solution.py:342
  122.2 5.2 %collective-permute-start.3 = (bf16[640,128]{1,0:T(8,128)(2,1)S(1)}, bf16[640,128]{1,0:T(8,128)(2,1)S(1)}, u32[]{:S(2)}, u32[]{:S(2)}) collective-permute-start(bf16[640,128]{1,0:T(8,128)(2,1)S(1)} %get-tuple-element.59), channel_id=1, source_target_pairs={{0,7},{1,6},{2,5},{3,4},{4,3},{5,2},{6,1},{7,0},{8,15},{9,14},{10,... | collective-permute-start | bytes 491528 | tf_op jit(solution)/shard_map/ppermute | solution.py:342
  127.5 3.3 %collective-permute-start.4 = (bf16[640,128]{1,0:T(8,128)(2,1)S(1)}, bf16[640,128]{1,0:T(8,128)(2,1)S(1)}, u32[]{:S(2)}, u32[]{:S(2)}) collective-permute-start(bf16[640,128]{1,0:T(8,128)(2,1)S(1)} %get-tuple-element.60), channel_id=1, source_target_pairs={{0,1},{1,0},{2,3},{3,2},{4,5},{5,4},{6,7},{7,6},{8,9},{9,8},{10,11... | collective-permute-start | bytes 491528 | tf_op jit(solution)/shard_map/ppermute | solution.py:342
  130.8 3.6 %collective-permute-start.5 = (bf16[640,128]{1,0:T(8,128)(2,1)S(1)}, bf16[640,128]{1,0:T(8,128)(2,1)S(1)}, u32[]{:S(2)}, u32[]{:S(2)}) collective-permute-start(bf16[640,128]{1,0:T(8,128)(2,1)S(1)} %get-tuple-element.61), channel_id=1, source_target_pairs={{0,4},{1,5},{2,6},{3,7},{4,0},{5,1},{6,2},{7,3},{8,12},{9,13},{10,... | collective-permute-start | bytes 491528 | tf_op jit(solution)/shard_map/ppermute | solution.py:342
  134.4 2.6 %collective-permute-start.6 = (bf16[640,128]{1,0:T(8,128)(2,1)S(1)}, bf16[640,128]{1,0:T(8,128)(2,1)S(1)}, u32[]{:S(2)}, u32[]{:S(2)}) collective-permute-start(bf16[640,128]{1,0:T(8,128)(2,1)S(1)} %get-tuple-element.62), channel_id=1, source_target_pairs={{0,2},{1,3},{2,0},{3,1},{4,6},{5,7},{6,4},{7,5},{8,10},{9,11},{10,... | collective-permute-start | bytes 491528 | tf_op jit(solution)/shard_map/ppermute | solution.py:342
  137.0 3.6 %collective-permute-start.7 = (bf16[640,128]{1,0:T(8,128)(2,1)}, bf16[640,128]{1,0:T(8,128)(2,1)S(1)}, u32[]{:S(2)}, u32[]{:S(2)}) collective-permute-start(bf16[640,128]{1,0:T(8,128)(2,1)} %copy-done.5), channel_id=1, source_target_pairs={{0,6},{1,7},{2,4},{3,5},{4,2},{5,3},{6,0},{7,1},{8,14},{9,15},{10,... | collective-permute-start | bytes 491528 | tf_op jit(solution)/shard_map/ppermute | solution.py:342
  140.7 1.2 collective-permute-done.6.refs_6_.refs_14_
  141.8 3.8 %collective-permute-done.7.refs_7_.refs_15_ = bf16[640,128]{1,0:T(8,128)(2,1)S(1)} collective-permute-done((bf16[640,128]{1,0:T(8,128)(2,1)}, bf16[640,128]{1,0:T(8,128)(2,1)S(1)}, u32[]{:S(2)}, u32[]{:S(2)}) %collective-permute-start.7) | collective-permute-done | bytes 163872 | tf_op jit(solution)/shard_map/ppermute | solution.py:342
  145.6 0.8 copy-done.8
  146.4 4.1 %finish.1 = (bf16[512,128]{1,0:T(8,128)(2,1)}, bf16[512,1024]{1,0:T(8,128)(2,1)}) custom-call(s32[1]{0:T(128)} %bitcast.place_ref, s32[128]{0:T(128)S(1)} %copy-done.10, f32[512,1024]{1,0:T(8,128)} %copy-done.2, bf16[16,1152]{1,0:T(8,128)(2,1)S(1)} %copy-done.8, bf16[640,128]{1,0:T(8,128)(2,1)S(1)} %get-tuple-element.56.refs_0_.refs_8_, ...), custom_call_target="tpu_custom_call" | custom-call | flops 16777216 | bytes 5242880 | tf_op jit(solution)/shard_map/finish/pallas_call | solution.py:356
  150.5 0.6 total.1
  (27 shorter events, 0.1 us)
Async XLA Ops:
  3.1 7.6 %copy-start.11 = (bf16[1,1024,16]{1,2,0:T(8,128)(2,1)S(1)}, bf16[1,1024,16]{1,2,0:T(8,128)(2,1)}, u32[]{:S(2)}) copy-start(bf16[1,1024,16]{1,2,0:T(8,128)(2,1)} %param.9) | copy-start | bytes 98308
  3.1 7.6 %copy-start.12 = (bf16[1,16,128]{2,1,0:T(8,128)(2,1)S(1)}, bf16[1,16,128]{2,1,0:T(8,128)(2,1)}, u32[]{:S(2)}) copy-start(bf16[1,16,128]{2,1,0:T(8,128)(2,1)} %param.10) | copy-start | bytes 12292
  3.1 65.0 %copy-start.9 = (s32[128]{0:T(128)S(1)}, s32[128]{0:T(128)}, u32[]{:S(2)}) copy-start(s32[128]{0:T(128)} %tenants_ref.5) | copy-start | bytes 1540
  3.1 66.3 %all-to-all-start = ((bf16[8,128,1024]{2,1,0:T(8,128)(2,1)}), bf16[8,128,1024]{2,1,0:T(8,128)(2,1)S(1)}, u32[]{:S(2)}, u32[]{:S(2)}) async-start(bf16[8,128,1024]{2,1,0:T(8,128)(2,1)} %slab.1), calls=%async_computation | async-start | bytes 4194304 | tf_op jit(solution)/shard_map/all_to_all | solution.py:265
  64.6 3.5 %collective-permute-start = (bf16[8,16,1152]{2,1,0:T(8,128)(2,1)S(1)}, bf16[8,16,1152]{2,1,0:T(8,128)(2,1)S(1)}, u32[]{:S(2)}, u32[]{:S(2)}) collective-permute-start(bf16[8,16,1152]{2,1,0:T(8,128)(2,1)S(1)} %bitcast.6), channel_id=1, source_target_pairs={{0,8},{8,0},{1,9},{9,1},{2,10},{10,2},{3,11},{11,3},{4,12},{12,4},... | collective-permute-start | bytes 884744 | tf_op jit(solution)/shard_map/ppermute | solution.py:269
  69.4 13.9 %all-to-all-start.1 = ((bf16[8,16,1152]{2,1,0:T(8,128)(2,1)}), bf16[8,16,1152]{2,1,0:T(8,128)(2,1)S(1)}, u32[]{:S(2)}, u32[]{:S(2)}) async-start(bf16[8,16,1152]{2,1,0:T(8,128)(2,1)} %table.1), calls=%async_computation.1 | async-start | bytes 589824 | tf_op jit(solution)/shard_map/all_to_all | solution.py:312
  73.7 1.6 %copy-start = (bf16[1024,1024]{1,0:T(8,128)(2,1)S(1)}, bf16[1024,1024]{1,0:T(8,128)(2,1)}, u32[]{:S(2)}) copy-start(bf16[1024,1024]{1,0:T(8,128)(2,1)} %weight_ref.3) | copy-start | bytes 6291460
  75.3 3.0 %copy-start.1 = (bf16[1024,1024]{1,0:T(8,128)(2,1)S(1)}, bf16[1024,1024]{1,0:T(8,128)(2,1)}, u32[]{:S(2)}) copy-start(bf16[1024,1024]{1,0:T(8,128)(2,1)} %weight_ref.3) | copy-start | bytes 6291460
  76.9 1.3 copy-start.2
  78.3 5.0 %copy-start.10 = (s32[128]{0:T(128)S(1)}, s32[128]{0:T(128)}, u32[]{:S(2)}) copy-start(s32[128]{0:T(128)} %lengths_ref.3) | copy-start | bytes 1540
  80.5 0.7 copy-start.3
  83.3 0.9 copy-start.4
  84.2 0.9 copy-start.6
  86.4 14.7 %copy-start.7 = (bf16[16,1152]{1,0:T(8,128)(2,1)}, bf16[16,1152]{1,0:T(8,128)(2,1)S(1)}, u32[]{:S(2)}) copy-start(bf16[16,1152]{1,0:T(8,128)(2,1)S(1)} %get-tuple-element.46.item_ref) | copy-start | bytes 110596
  101.0 0.7 copy-start.5
  101.7 48.8 %all-to-all-start.3 = ((bf16[32,16,128]{2,1,0:T(8,128)(2,1)}), bf16[32,16,128]{2,1,0:T(8,128)(2,1)S(1)}, u32[]{:S(2)}, u32[]{:S(2)}) async-start(bf16[32,16,128]{2,1,0:T(8,128)(2,1)} %get-tuple-element.66), calls=%async_computation.3 | async-start | bytes 262144 | tf_op jit(solution)/shard_map/all_to_all | solution.py:340
  113.6 20.8 %collective-permute-start.1 = (bf16[640,128]{1,0:T(8,128)(2,1)S(1)}, bf16[640,128]{1,0:T(8,128)(2,1)S(1)}, u32[]{:S(2)}, u32[]{:S(2)}) collective-permute-start(bf16[640,128]{1,0:T(8,128)(2,1)S(1)} %get-tuple-element.57), channel_id=1, source_target_pairs={{0,5},{1,4},{2,7},{3,6},{4,1},{5,0},{6,3},{7,2},{8,13},{9,12},{10,... | collective-permute-start | bytes 491528 | tf_op jit(solution)/shard_map/ppermute | solution.py:342
  118.3 18.7 %collective-permute-start.2 = (bf16[640,128]{1,0:T(8,128)(2,1)S(1)}, bf16[640,128]{1,0:T(8,128)(2,1)S(1)}, u32[]{:S(2)}, u32[]{:S(2)}) collective-permute-start(bf16[640,128]{1,0:T(8,128)(2,1)S(1)} %get-tuple-element.58), channel_id=1, source_target_pairs={{0,3},{1,2},{2,1},{3,0},{4,7},{5,6},{6,5},{7,4},{8,11},{9,10},{10,... | collective-permute-start | bytes 491528 | tf_op jit(solution)/shard_map/ppermute | solution.py:342
  122.2 18.4 %collective-permute-start.3 = (bf16[640,128]{1,0:T(8,128)(2,1)S(1)}, bf16[640,128]{1,0:T(8,128)(2,1)S(1)}, u32[]{:S(2)}, u32[]{:S(2)}) collective-permute-start(bf16[640,128]{1,0:T(8,128)(2,1)S(1)} %get-tuple-element.59), channel_id=1, source_target_pairs={{0,7},{1,6},{2,5},{3,4},{4,3},{5,2},{6,1},{7,0},{8,15},{9,14},{10,... | collective-permute-start | bytes 491528 | tf_op jit(solution)/shard_map/ppermute | solution.py:342
  127.5 13.1 %collective-permute-start.4 = (bf16[640,128]{1,0:T(8,128)(2,1)S(1)}, bf16[640,128]{1,0:T(8,128)(2,1)S(1)}, u32[]{:S(2)}, u32[]{:S(2)}) collective-permute-start(bf16[640,128]{1,0:T(8,128)(2,1)S(1)} %get-tuple-element.60), channel_id=1, source_target_pairs={{0,1},{1,0},{2,3},{3,2},{4,5},{5,4},{6,7},{7,6},{8,9},{9,8},{10,11... | collective-permute-start | bytes 491528 | tf_op jit(solution)/shard_map/ppermute | solution.py:342
  130.8 9.9 %collective-permute-start.5 = (bf16[640,128]{1,0:T(8,128)(2,1)S(1)}, bf16[640,128]{1,0:T(8,128)(2,1)S(1)}, u32[]{:S(2)}, u32[]{:S(2)}) collective-permute-start(bf16[640,128]{1,0:T(8,128)(2,1)S(1)} %get-tuple-element.61), channel_id=1, source_target_pairs={{0,4},{1,5},{2,6},{3,7},{4,0},{5,1},{6,2},{7,3},{8,12},{9,13},{10,... | collective-permute-start | bytes 491528 | tf_op jit(solution)/shard_map/ppermute | solution.py:342
  134.4 7.4 %collective-permute-start.6 = (bf16[640,128]{1,0:T(8,128)(2,1)S(1)}, bf16[640,128]{1,0:T(8,128)(2,1)S(1)}, u32[]{:S(2)}, u32[]{:S(2)}) collective-permute-start(bf16[640,128]{1,0:T(8,128)(2,1)S(1)} %get-tuple-element.62), channel_id=1, source_target_pairs={{0,2},{1,3},{2,0},{3,1},{4,6},{5,7},{6,4},{7,5},{8,10},{9,11},{10,... | collective-permute-start | bytes 491528 | tf_op jit(solution)/shard_map/ppermute | solution.py:342
  137.0 8.6 %collective-permute-start.7 = (bf16[640,128]{1,0:T(8,128)(2,1)}, bf16[640,128]{1,0:T(8,128)(2,1)S(1)}, u32[]{:S(2)}, u32[]{:S(2)}) collective-permute-start(bf16[640,128]{1,0:T(8,128)(2,1)} %copy-done.5), channel_id=1, source_target_pairs={{0,6},{1,7},{2,4},{3,5},{4,2},{5,3},{6,0},{7,1},{8,14},{9,15},{10,... | collective-permute-start | bytes 491528 | tf_op jit(solution)/shard_map/ppermute | solution.py:342
  145.6 0.8 copy-start.8

commit v8 on v7

--- a/solution.py
+++ b/solution.py
@@ -210,6 +210,13 @@
     out_ref[0] = total
 
 
+def presum_kernel(*refs):
+    total = refs[0][...].astype(jnp.float32)
+    for ref in refs[1:-1]:
+        total = total + ref[...].astype(jnp.float32)
+    refs[-1][...] = total
+
+
 def finish_kernel(parts, place_ref, lengths_ref, base_ref, item_ref, *refs):
     values, ranks = refs[:parts], refs[parts : 2 * parts]
     projected_ref, gradient_ref = refs[2 * parts :]
@@ -353,8 +360,20 @@
     )(far_parts)
 
     group = 2 * rank
+    ready = parcels[:-2]
+    presum = pl.pallas_call(
+        presum_kernel,
+        grid=(1,),
+        out_shape=struct(parcel.shape, f32),
+        in_specs=[whole(parcel.shape)] * len(ready),
+        out_specs=whole(parcel.shape),
+        compiler_params=params(),
+        cost_estimate=cost(len(ready) * parcel.shape[0] * features, 2 << 20),
+        name="presum",
+    )(*ready)
+    parcels = [presum] + parcels[-2:]
     projected, gradient = pl.pallas_call(
-        functools.partial(finish_kernel, parts),
+        functools.partial(finish_kernel, len(parcels)),
         grid=(block // features,),
         out_shape=(struct((block, features), bf16), struct((block, width), bf16)),
         in_specs=[
@@ -363,8 +382,8 @@
             pl.BlockSpec((features, width), lambda i: (i, 0)),
             pl.BlockSpec(own.shape, lambda i: (0, 0)),
         ]
-        + [pl.BlockSpec((features, features), lambda i: (i, 0))] * parts
-        + [pl.BlockSpec((group, features), lambda i: (block // group + i, 0))] * parts,
+        + [pl.BlockSpec((features, features), lambda i: (i, 0))] * len(parcels)
+        + [pl.BlockSpec((group, features), lambda i: (block // group + i, 0))] * len(parcels),
         out_specs=(
             pl.BlockSpec((features, features), lambda i: (i, 0)),
             pl.BlockSpec((features, width), lambda i: (i, 0)),

time: 154 us -> 154 us (level)
    pallas_call x1 -> x2, Pallas kernels: 4.11 us -> 4.22 us  [the longest x1 4.1 us: on_device(): pl.pallas_call(functools.partial(finish_kernel, len(parcels)), grid=(bloc...]
where the time goes in v8:
time: 154 us; the launch traced here: 151 us
  blocking collectives  67.3 us (44%)
  starting transfers between devices  52.6 us (34%)
  Pallas kernels  15 us (10%)
  waiting for transfers between devices  8.51 us (6%)
  local copies, waits for them, and re-layouts  6.86 us (4%)
    all_gather x1, blocking collectives, on_device(): held = lax.all_gather(own, 'far', axis=0, tiled=False)  53.9 us
    ppermute x7, starting transfers between devices, on_device(): lax.ppermute(parcel, 'tp', [(d, d ^ k) for d in range(parts)])  26.9 us
    all_to_all x1, blocking collectives, on_device(): lax.all_to_all(shares, ('xlo', 'core', 'tp'), 0, 0, tiled=True)  13.4 us
    all_to_all x1, starting transfers between devices, on_device(): far_parts = lax.all_to_all(routed, ('far', 'near'), 0, 0, tiled=True)  11.9 us
    all_to_all x1, starting transfers between devices, on_device(): arrived = lax.all_to_all(slabs, 'tp', 0, 0, tiled=True)  7.58 us
    unnamed x26, local copies, waits for them, and re-layouts  6.86 us
    ppermute x7, waiting for transfers between devices, on_device(): lax.ppermute(parcel, 'tp', [(d, d ^ k) for d in range(parts)])  4.85 us
    all_to_all x1, starting transfers between devices, on_device(): offered = lax.all_to_all(table, ('xlo', 'near'), 0, 0, tiled=True)  4.28 us
  transfers between devices with their start and end apart: 11, of which 4 were waited for; matrix products, arithmetic and copies ran while one was open for 0% of the time, Pallas kernels for 6%

profile of v8, /device:TPU:6, one launch (start us, length us, event | category | flops | bytes accessed | tf_op | source)
XLA Modules:
  0.0 151.1 jit_solution(17392669387704353138)
XLA Ops:
  0.6 2.4 %slab.1 = bf16[8,128,1024]{2,1,0:T(8,128)(2,1)} custom-call(bf16[64,8192]{1,0:T(8,128)(2,1)} %tokens_ref.1, bf16[512,128]{1,0:T(8,128)(2,1)} %upstream_ref.3), custom_call_target="tpu_custom_call" | custom-call | tf_op jit(solution)/shard_map/slab/pallas_call | solution.py:259
  3.1 7.6 %all-to-all-start = ((bf16[8,128,1024]{2,1,0:T(8,128)(2,1)}), bf16[8,128,1024]{2,1,0:T(8,128)(2,1)S(1)}, u32[]{:S(2)}, u32[]{:S(2)}) async-start(bf16[8,128,1024]{2,1,0:T(8,128)(2,1)} %slab.1), calls=%async_computation | async-start | bytes 4194304 | tf_op jit(solution)/shard_map/all_to_all | solution.py:272
  10.7 53.9 %all-gather = bf16[128,1152]{1,0:T(8,128)(2,1)S(1)} all-gather(bf16[16,1152]{1,0:T(8,128)(2,1)S(1)} %pad_maximum_fusion), channel_id=2, replica_groups=mesh['xlo'=2,'far'=8,'near'=4,'core'=2,'tp'=8] {'far'}, dimensions={0}, use_global_device_ids=true | all-gather | bytes 331776 | tf_op jit(solution)/shard_map/all_gather | solution.py:275
  64.6 1.9 %collective-permute-start = (bf16[8,16,1152]{2,1,0:T(8,128)(2,1)S(1)}, bf16[8,16,1152]{2,1,0:T(8,128)(2,1)S(1)}, u32[]{:S(2)}, u32[]{:S(2)}) collective-permute-start(bf16[8,16,1152]{2,1,0:T(8,128)(2,1)S(1)} %bitcast.6), channel_id=1, source_target_pairs={{0,8},{8,0},{1,9},{9,1},{2,10},{10,2},{3,11},{11,3},{4,12},{12,4},... | collective-permute-start | bytes 884744 | tf_op jit(solution)/shard_map/ppermute | solution.py:276
  66.5 1.5 %collective-permute-done.other_ref = bf16[8,16,1152]{2,1,0:T(8,128)(2,1)S(1)} collective-permute-done((bf16[8,16,1152]{2,1,0:T(8,128)(2,1)S(1)}, bf16[8,16,1152]{2,1,0:T(8,128)(2,1)S(1)}, u32[]{:S(2)}, u32[]{:S(2)}) %collective-permute-start) | collective-permute-done | bytes 294944 | tf_op jit(solution)/shard_map/ppermute | solution.py:276
  68.1 1.3 table.1
  69.4 4.3 %all-to-all-start.1 = ((bf16[8,16,1152]{2,1,0:T(8,128)(2,1)}), bf16[8,16,1152]{2,1,0:T(8,128)(2,1)S(1)}, u32[]{:S(2)}, u32[]{:S(2)}) async-start(bf16[8,16,1152]{2,1,0:T(8,128)(2,1)} %table.1), calls=%async_computation.1 | async-start | bytes 589824 | tf_op jit(solution)/shard_map/all_to_all | solution.py:319
  73.7 1.6 %copy-done = bf16[1024,1024]{1,0:T(8,128)(2,1)S(1)} copy-done((bf16[1024,1024]{1,0:T(8,128)(2,1)S(1)}, bf16[1024,1024]{1,0:T(8,128)(2,1)}, u32[]{:S(2)}) %copy-start) | copy-done | bytes 2097176
  75.3 1.6 %base.1 = (f32[512,1024]{1,0:T(8,128)S(1)}, f32[8,128]{1,0:T(8,128)S(1)}) custom-call(bf16[8,128,1024]{2,1,0:T(8,128)(2,1)S(1)} %all-to-all-done.upstream_ref.columns_ref.arrived_ref, bf16[1024,1024]{1,0:T(8,128)(2,1)S(1)} %copy-done), custom_call_target="tpu_custom_call" | custom-call | flops 1073741824 | bytes 6291456 | tf_op jit(solution)/shard_map/base/pallas_call | solution.py:294
  76.9 1.3 copy-done.2
  78.3 2.2 %value.1 = (bf16[640,128]{1,0:T(8,128)(2,1)S(1)}, bf16[640,128]{1,0:T(8,128)(2,1)S(1)}, bf16[640,128]{1,0:T(8,128)(2,1)S(1)}, bf16[640,128]{1,0:T(8,128)(2,1)S(1...) custom-call(bf16[8,128,1024]{2,1,0:T(8,128)(2,1)S(1)} %all-to-all-do, ...), custom_call_target="tpu_custom_call" | custom-call | flops 1073741824 | bytes 4194304 | tf_op jit(solution)/shard_map/value/pallas_call | solution.py:278
  80.5 0.6 copy-done.3
  81.2 2.1 %all-to-all-done.1.offered_ref = bf16[8,16,1152]{2,1,0:T(8,128)(2,1)S(1)} async-done(((bf16[8,16,1152]{2,1,0:T(8,128)(2,1)}), bf16[8,16,1152]{2,1,0:T(8,128)(2,1)S(1)}, u32[]{:S(2)}, u32[]{:S(2)}) %all-to-all-start.1) | async-done | bytes 294944 | tf_op jit(solution)/shard_map/all_to_all | solution.py:319
  83.3 0.9 copy-done.4
  84.2 0.9 copy-done.6
  85.1 1.2 low.1
  86.4 13.4 %all_to_all.20.shares_ref = bf16[32,16,128]{2,1,0:T(8,128)(2,1)S(1)} all-to-all(bf16[32,16,128]{2,1,0:T(8,128)(2,1)S(1)} %get-tuple-element.47), channel_id=1, replica_groups=mesh['xlo'=2,'far'=8,'near'=4,'core'=2,'tp'=8] {'xlo','core','tp'}, dimensions={0} | all-to-all | bytes 262144 | tf_op jit(solution)/shard_map/all_to_all | solution.py:335
  99.8 1.3 route.1
  101.0 0.7 copy-done.5
  101.7 11.9 %all-to-all-start.3 = ((bf16[32,16,128]{2,1,0:T(8,128)(2,1)}), bf16[32,16,128]{2,1,0:T(8,128)(2,1)S(1)}, u32[]{:S(2)}, u32[]{:S(2)}) async-start(bf16[32,16,128]{2,1,0:T(8,128)(2,1)} %get-tuple-element.66), calls=%async_computation.3 | async-start | bytes 262144 | tf_op jit(solution)/shard_map/all_to_all | solution.py:347
  113.6 4.7 %collective-permute-start.1 = (bf16[640,128]{1,0:T(8,128)(2,1)S(1)}, bf16[640,128]{1,0:T(8,128)(2,1)S(1)}, u32[]{:S(2)}, u32[]{:S(2)}) collective-permute-start(bf16[640,128]{1,0:T(8,128)(2,1)S(1)} %get-tuple-element.57), channel_id=1, source_target_pairs={{0,5},{1,4},{2,7},{3,6},{4,1},{5,0},{6,3},{7,2},{8,13},{9,12},{10,... | collective-permute-start | bytes 491528 | tf_op jit(solution)/shard_map/ppermute | solution.py:349
  118.3 3.9 %collective-permute-start.2 = (bf16[640,128]{1,0:T(8,128)(2,1)S(1)}, bf16[640,128]{1,0:T(8,128)(2,1)S(1)}, u32[]{:S(2)}, u32[]{:S(2)}) collective-permute-start(bf16[640,128]{1,0:T(8,128)(2,1)S(1)} %get-tuple-element.58), channel_id=1, source_target_pairs={{0,3},{1,2},{2,1},{3,0},{4,7},{5,6},{6,5},{7,4},{8,11},{9,10},{10,... | collective-permute-start | bytes 491528 | tf_op jit(solution)/shard_map/ppermute | solution.py:349
  122.2 5.2 %collective-permute-start.3 = (bf16[640,128]{1,0:T(8,128)(2,1)S(1)}, bf16[640,128]{1,0:T(8,128)(2,1)S(1)}, u32[]{:S(2)}, u32[]{:S(2)}) collective-permute-start(bf16[640,128]{1,0:T(8,128)(2,1)S(1)} %get-tuple-element.59), channel_id=1, source_target_pairs={{0,7},{1,6},{2,5},{3,4},{4,3},{5,2},{6,1},{7,0},{8,15},{9,14},{10,... | collective-permute-start | bytes 491528 | tf_op jit(solution)/shard_map/ppermute | solution.py:349
  127.5 3.3 %collective-permute-start.4 = (bf16[640,128]{1,0:T(8,128)(2,1)S(1)}, bf16[640,128]{1,0:T(8,128)(2,1)S(1)}, u32[]{:S(2)}, u32[]{:S(2)}) collective-permute-start(bf16[640,128]{1,0:T(8,128)(2,1)S(1)} %get-tuple-element.60), channel_id=1, source_target_pairs={{0,1},{1,0},{2,3},{3,2},{4,5},{5,4},{6,7},{7,6},{8,9},{9,8},{10,11... | collective-permute-start | bytes 491528 | tf_op jit(solution)/shard_map/ppermute | solution.py:349
  130.8 3.6 %collective-permute-start.5 = (bf16[640,128]{1,0:T(8,128)(2,1)S(1)}, bf16[640,128]{1,0:T(8,128)(2,1)S(1)}, u32[]{:S(2)}, u32[]{:S(2)}) collective-permute-start(bf16[640,128]{1,0:T(8,128)(2,1)S(1)} %get-tuple-element.61), channel_id=1, source_target_pairs={{0,4},{1,5},{2,6},{3,7},{4,0},{5,1},{6,2},{7,3},{8,12},{9,13},{10,... | collective-permute-start | bytes 491528 | tf_op jit(solution)/shard_map/ppermute | solution.py:349
  134.4 2.6 %collective-permute-start.6 = (bf16[640,128]{1,0:T(8,128)(2,1)S(1)}, bf16[640,128]{1,0:T(8,128)(2,1)S(1)}, u32[]{:S(2)}, u32[]{:S(2)}) collective-permute-start(bf16[640,128]{1,0:T(8,128)(2,1)S(1)} %get-tuple-element.62), channel_id=1, source_target_pairs={{0,2},{1,3},{2,0},{3,1},{4,6},{5,7},{6,4},{7,5},{8,10},{9,11},{10,... | collective-permute-start | bytes 491528 | tf_op jit(solution)/shard_map/ppermute | solution.py:349
  137.0 3.6 %collective-permute-start.7 = (bf16[640,128]{1,0:T(8,128)(2,1)}, bf16[640,128]{1,0:T(8,128)(2,1)S(1)}, u32[]{:S(2)}, u32[]{:S(2)}) collective-permute-start(bf16[640,128]{1,0:T(8,128)(2,1)} %copy-done.5), channel_id=1, source_target_pairs={{0,6},{1,7},{2,4},{3,5},{4,2},{5,3},{6,0},{7,1},{8,14},{9,15},{10,... | collective-permute-start | bytes 491528 | tf_op jit(solution)/shard_map/ppermute | solution.py:349
  140.8 1.0 collective-permute-done.6.refs_1_.refs_4_
  141.8 3.8 %collective-permute-done.7.refs_2_.refs_5_ = bf16[640,128]{1,0:T(8,128)(2,1)S(1)} collective-permute-done((bf16[640,128]{1,0:T(8,128)(2,1)}, bf16[640,128]{1,0:T(8,128)(2,1)S(1)}, u32[]{:S(2)}, u32[]{:S(2)}) %collective-permute-start.7) | collective-permute-done | bytes 163872 | tf_op jit(solution)/shard_map/ppermute | solution.py:349
  145.6 0.8 copy-done.8
  146.4 4.1 %finish.1 = (bf16[512,128]{1,0:T(8,128)(2,1)}, bf16[512,1024]{1,0:T(8,128)(2,1)}) custom-call(s32[1]{0:T(128)} %bitcast.place_ref, s32[128]{0:T(128)S(1)} %copy-done.10, f32[512,1024]{1,0:T(8,128)} %copy-done.2, bf16[16,1152]{1,0:T(8,128)(2,1)S(1)} %copy-done.8, f32[640,128]{1,0:T(8,128)S(1)} %presum.1.refs_0_.refs_3_, ...), custom_call_target="tpu_custom_call" | custom-call | flops 16777216 | bytes 5242880 | tf_op jit(solution)/shard_map/finish/pallas_call | solution.py:375
  150.5 0.6 total.1
  (28 shorter events, 0.2 us)
Async XLA Ops:
  3.1 7.6 %copy-start.11 = (bf16[1,1024,16]{1,2,0:T(8,128)(2,1)S(1)}, bf16[1,1024,16]{1,2,0:T(8,128)(2,1)}, u32[]{:S(2)}) copy-start(bf16[1,1024,16]{1,2,0:T(8,128)(2,1)} %param.9) | copy-start | bytes 98308
  3.1 7.6 %copy-start.12 = (bf16[1,16,128]{2,1,0:T(8,128)(2,1)S(1)}, bf16[1,16,128]{2,1,0:T(8,128)(2,1)}, u32[]{:S(2)}) copy-start(bf16[1,16,128]{2,1,0:T(8,128)(2,1)} %param.10) | copy-start | bytes 12292
  3.1 65.0 %copy-start.9 = (s32[128]{0:T(128)S(1)}, s32[128]{0:T(128)}, u32[]{:S(2)}) copy-start(s32[128]{0:T(128)} %tenants_ref.5) | copy-start | bytes 1540
  3.1 66.3 %all-to-all-start = ((bf16[8,128,1024]{2,1,0:T(8,128)(2,1)}), bf16[8,128,1024]{2,1,0:T(8,128)(2,1)S(1)}, u32[]{:S(2)}, u32[]{:S(2)}) async-start(bf16[8,128,1024]{2,1,0:T(8,128)(2,1)} %slab.1), calls=%async_computation | async-start | bytes 4194304 | tf_op jit(solution)/shard_map/all_to_all | solution.py:272
  64.6 3.5 %collective-permute-start = (bf16[8,16,1152]{2,1,0:T(8,128)(2,1)S(1)}, bf16[8,16,1152]{2,1,0:T(8,128)(2,1)S(1)}, u32[]{:S(2)}, u32[]{:S(2)}) collective-permute-start(bf16[8,16,1152]{2,1,0:T(8,128)(2,1)S(1)} %bitcast.6), channel_id=1, source_target_pairs={{0,8},{8,0},{1,9},{9,1},{2,10},{10,2},{3,11},{11,3},{4,12},{12,4},... | collective-permute-start | bytes 884744 | tf_op jit(solution)/shard_map/ppermute | solution.py:276
  69.4 13.9 %all-to-all-start.1 = ((bf16[8,16,1152]{2,1,0:T(8,128)(2,1)}), bf16[8,16,1152]{2,1,0:T(8,128)(2,1)S(1)}, u32[]{:S(2)}, u32[]{:S(2)}) async-start(bf16[8,16,1152]{2,1,0:T(8,128)(2,1)} %table.1), calls=%async_computation.1 | async-start | bytes 589824 | tf_op jit(solution)/shard_map/all_to_all | solution.py:319
  73.7 1.6 %copy-start = (bf16[1024,1024]{1,0:T(8,128)(2,1)S(1)}, bf16[1024,1024]{1,0:T(8,128)(2,1)}, u32[]{:S(2)}) copy-start(bf16[1024,1024]{1,0:T(8,128)(2,1)} %weight_ref.3) | copy-start | bytes 6291460
  75.3 3.0 %copy-start.1 = (bf16[1024,1024]{1,0:T(8,128)(2,1)S(1)}, bf16[1024,1024]{1,0:T(8,128)(2,1)}, u32[]{:S(2)}) copy-start(bf16[1024,1024]{1,0:T(8,128)(2,1)} %weight_ref.3) | copy-start | bytes 6291460
  76.9 1.3 copy-start.2
  78.3 5.0 %copy-start.10 = (s32[128]{0:T(128)S(1)}, s32[128]{0:T(128)}, u32[]{:S(2)}) copy-start(s32[128]{0:T(128)} %lengths_ref.3) | copy-start | bytes 1540
  80.5 0.7 copy-start.3
  83.3 0.9 copy-start.4
  84.2 0.9 copy-start.6
  86.4 14.7 %copy-start.7 = (bf16[16,1152]{1,0:T(8,128)(2,1)}, bf16[16,1152]{1,0:T(8,128)(2,1)S(1)}, u32[]{:S(2)}) copy-start(bf16[16,1152]{1,0:T(8,128)(2,1)S(1)} %get-tuple-element.46.item_ref) | copy-start | bytes 110596
  101.0 0.7 copy-start.5
  101.7 48.8 %all-to-all-start.3 = ((bf16[32,16,128]{2,1,0:T(8,128)(2,1)}), bf16[32,16,128]{2,1,0:T(8,128)(2,1)S(1)}, u32[]{:S(2)}, u32[]{:S(2)}) async-start(bf16[32,16,128]{2,1,0:T(8,128)(2,1)} %get-tuple-element.66), calls=%async_computation.3 | async-start | bytes 262144 | tf_op jit(solution)/shard_map/all_to_all | solution.py:347
  113.6 20.8 %collective-permute-start.1 = (bf16[640,128]{1,0:T(8,128)(2,1)S(1)}, bf16[640,128]{1,0:T(8,128)(2,1)S(1)}, u32[]{:S(2)}, u32[]{:S(2)}) collective-permute-start(bf16[640,128]{1,0:T(8,128)(2,1)S(1)} %get-tuple-element.57), channel_id=1, source_target_pairs={{0,5},{1,4},{2,7},{3,6},{4,1},{5,0},{6,3},{7,2},{8,13},{9,12},{10,... | collective-permute-start | bytes 491528 | tf_op jit(solution)/shard_map/ppermute | solution.py:349
  118.3 18.7 %collective-permute-start.2 = (bf16[640,128]{1,0:T(8,128)(2,1)S(1)}, bf16[640,128]{1,0:T(8,128)(2,1)S(1)}, u32[]{:S(2)}, u32[]{:S(2)}) collective-permute-start(bf16[640,128]{1,0:T(8,128)(2,1)S(1)} %get-tuple-element.58), channel_id=1, source_target_pairs={{0,3},{1,2},{2,1},{3,0},{4,7},{5,6},{6,5},{7,4},{8,11},{9,10},{10,... | collective-permute-start | bytes 491528 | tf_op jit(solution)/shard_map/ppermute | solution.py:349
  122.2 18.4 %collective-permute-start.3 = (bf16[640,128]{1,0:T(8,128)(2,1)S(1)}, bf16[640,128]{1,0:T(8,128)(2,1)S(1)}, u32[]{:S(2)}, u32[]{:S(2)}) collective-permute-start(bf16[640,128]{1,0:T(8,128)(2,1)S(1)} %get-tuple-element.59), channel_id=1, source_target_pairs={{0,7},{1,6},{2,5},{3,4},{4,3},{5,2},{6,1},{7,0},{8,15},{9,14},{10,... | collective-permute-start | bytes 491528 | tf_op jit(solution)/shard_map/ppermute | solution.py:349
  127.5 13.1 %collective-permute-start.4 = (bf16[640,128]{1,0:T(8,128)(2,1)S(1)}, bf16[640,128]{1,0:T(8,128)(2,1)S(1)}, u32[]{:S(2)}, u32[]{:S(2)}) collective-permute-start(bf16[640,128]{1,0:T(8,128)(2,1)S(1)} %get-tuple-element.60), channel_id=1, source_target_pairs={{0,1},{1,0},{2,3},{3,2},{4,5},{5,4},{6,7},{7,6},{8,9},{9,8},{10,11... | collective-permute-start | bytes 491528 | tf_op jit(solution)/shard_map/ppermute | solution.py:349
  130.8 9.9 %collective-permute-start.5 = (bf16[640,128]{1,0:T(8,128)(2,1)S(1)}, bf16[640,128]{1,0:T(8,128)(2,1)S(1)}, u32[]{:S(2)}, u32[]{:S(2)}) collective-permute-start(bf16[640,128]{1,0:T(8,128)(2,1)S(1)} %get-tuple-element.61), channel_id=1, source_target_pairs={{0,4},{1,5},{2,6},{3,7},{4,0},{5,1},{6,2},{7,3},{8,12},{9,13},{10,... | collective-permute-start | bytes 491528 | tf_op jit(solution)/shard_map/ppermute | solution.py:349
  134.4 7.4 %collective-permute-start.6 = (bf16[640,128]{1,0:T(8,128)(2,1)S(1)}, bf16[640,128]{1,0:T(8,128)(2,1)S(1)}, u32[]{:S(2)}, u32[]{:S(2)}) collective-permute-start(bf16[640,128]{1,0:T(8,128)(2,1)S(1)} %get-tuple-element.62), channel_id=1, source_target_pairs={{0,2},{1,3},{2,0},{3,1},{4,6},{5,7},{6,4},{7,5},{8,10},{9,11},{10,... | collective-permute-start | bytes 491528 | tf_op jit(solution)/shard_map/ppermute | solution.py:349
  137.0 8.6 %collective-permute-start.7 = (bf16[640,128]{1,0:T(8,128)(2,1)}, bf16[640,128]{1,0:T(8,128)(2,1)S(1)}, u32[]{:S(2)}, u32[]{:S(2)}) collective-permute-start(bf16[640,128]{1,0:T(8,128)(2,1)} %copy-done.5), channel_id=1, source_target_pairs={{0,6},{1,7},{2,4},{3,5},{4,2},{5,3},{6,0},{7,1},{8,14},{9,15},{10,... | collective-permute-start | bytes 491528 | tf_op jit(solution)/shard_map/ppermute | solution.py:349
  145.6 0.8 copy-start.8
